TPU v7x, 1024 devices: a whole 4x4x32 slice. The times are simulated.
1024 devices in a mesh: expert: 32 (over z), mp: 32 (over y, x, core).
Axes of the slice: x: 4, y: 4, z: 32, core: 2. Of those that a mesh axis runs over, the one named last changes fastest.
Arguments:
- x_tokens: bfloat16 [4096, 2048], P('expert', 'mp'), may hold values from -6 to 6
- cotangent: bfloat16 [4096, 2048], P('expert', 'mp'), may hold values from -2 to 2
- w_gate: bfloat16 [32, 1024, 8192], P('expert', None, 'mp'), may hold values from -0.125 to 0.125
- w_up: bfloat16 [32, 1024, 8192], P('expert', None, 'mp'), may hold values from -0.125 to 0.125
- w_down: bfloat16 [32, 8192, 1024], P('expert', 'mp'), may hold values from -0.125 to 0.125
- combine: float32 [64, 128], P('expert'), may hold values from 0.1 to 1
- indices: int32 [64, 128], replicated, may hold values from -1 to 4095, as said below
Outputs:
- grad_tokens: bfloat16 [4096, 2048], P('expert', 'mp')
- grad_gate: bfloat16 [32, 1024, 8192], P('expert', None, 'mp')
- grad_up: bfloat16 [32, 1024, 8192], P('expert', None, 'mp')
- grad_down: bfloat16 [32, 8192, 1024], P('expert', 'mp')
- grad_combine: float32 [64, 128], P('expert')
Inputs may be any that keep to these rules, and one draw needn't show every extreme that they name: `indices`: each row lists the tokens one expert chose, in increasing order, then -1 in its remaining slots. Tokens are owned in blocks of 128 along expert; one expert takes at most 8 tokens from one block, and in every row some block gives exactly 8. In every draw some expert fills all 128 slots.
All inputs are finite; a program needn't handle non-finite values.
Results may differ from a plain program's by a relative error of at most 0.022.
Values may be sent and summed in bfloat16 or wider, within the bound.
No kernel may reach another device: no remote copies, remote signals or barrier semaphores. Data moves between devices by JAX's collectives and lax.ppermute only.
A program may use at most 32 MiB of HBM per device.

v0:
```python
import jax
import jax.numpy as jnp
from jax import lax
from jax.sharding import PartitionSpec as P


def from_partner(block, axis, distance):
    count = lax.axis_size(axis)
    route = []
    for low in range(count):
        high = low | 1 << distance
        if high != low and high < count:
            route += [(low, high), (high, low)]
    return lax.ppermute(block, axis, route)


def local(x_tokens, cotangent, w_gate, w_up, w_down, combine, indices):
    groups = lax.axis_size("expert")
    lane_count = lax.axis_size("mp")
    tok_dev, width_part = x_tokens.shape
    experts, capacity = indices.shape
    exp_dev = experts // groups
    peer_slots = 2 * capacity // groups
    half_width = w_gate.shape[1]
    hidden = w_gate.shape[2]
    per_expert = lane_count // exp_dev
    blocks = per_expert // 2
    half_lanes = lane_count // 2
    group_index = lax.axis_index("expert")
    lane_index = lax.axis_index("mp")
    own_expert = lane_index // per_expert
    own_half = lane_index // blocks % 2
    offsets = jnp.arange(peer_slots, dtype=jnp.int32)
    slot_valid = indices >= 0
    keyed = jnp.where(slot_valid, indices, groups * tok_dev)
    bounds = jnp.arange(groups + 1, dtype=jnp.int32) * tok_dev
    edges = jax.vmap(lambda row_keys: jnp.searchsorted(row_keys, bounds, side="left"))(keyed)
    slot_starts = edges[:, :-1]
    per_source = edges[:, 1:] - edges[:, :-1]
    send_start = lax.dynamic_index_in_dim(slot_starts, group_index, 1, keepdims=False)
    send_count = lax.dynamic_index_in_dim(per_source, group_index, 1, keepdims=False)
    send_live = offsets[None, :] < send_count[:, None]
    send_slot = jnp.where(send_live, send_start[:, None] + offsets[None, :], 0)
    chosen = jnp.take_along_axis(indices, send_slot, axis=1)
    local_row = jnp.where(send_live, chosen - group_index * tok_dev, 0)
    send_mask = send_live[:, :, None]
    zero_half = jnp.zeros((), jnp.bfloat16)
    send_in = jnp.where(send_mask, x_tokens[local_row], zero_half).reshape(
        groups, exp_dev, peer_slots, width_part
    )
    send_out = jnp.where(send_mask, cotangent[local_row], zero_half).reshape(
        groups, exp_dev, peer_slots, width_part
    )
    recv_in, recv_out = (
        lax.all_to_all(send_in, "expert", split_axis=0, concat_axis=0, tiled=True),
        lax.all_to_all(send_out, "expert", split_axis=0, concat_axis=0, tiled=True),
    )
    own_rows = lax.dynamic_slice_in_dim(indices, group_index * exp_dev, exp_dev, 0)
    own_valid = own_rows >= 0
    own_source = jnp.where(own_valid, own_rows // tok_dev, 0)
    own_starts = lax.dynamic_slice_in_dim(slot_starts, group_index * exp_dev, exp_dev, 0)
    own_counts = lax.dynamic_slice_in_dim(per_source, group_index * exp_dev, exp_dev, 0)
    base_slot = jnp.take_along_axis(own_starts, own_source, axis=1)
    position = jnp.arange(capacity, dtype=jnp.int32)[None, :] - base_slot
    member_ids = jnp.arange(exp_dev, dtype=jnp.int32)
    half_ids = jnp.arange(2, dtype=jnp.int32)
    flat_index = own_source * (exp_dev * peer_slots) + member_ids[:, None] * peer_slots + position
    flat_index = jnp.where(own_valid, flat_index, 0)
    compact_in = jnp.where(
        own_valid[:, :, None], recv_in.reshape(-1, width_part)[flat_index], zero_half
    )
    compact_out = jnp.where(
        own_valid[:, :, None], recv_out.reshape(-1, width_part)[flat_index], zero_half
    )
    full_in, full_out = (
        lax.all_gather(compact_in, "mp", axis=2, tiled=True),
        lax.all_gather(compact_out, "mp", axis=2, tiled=True),
    )
    whole_in = lax.dynamic_index_in_dim(full_in, own_expert, 0, keepdims=False)
    whole_out = lax.dynamic_index_in_dim(full_out, own_expert, 0, keepdims=False)
    rows_in = lax.dynamic_slice_in_dim(whole_in, own_half * half_width, half_width, 1)
    rows_out = lax.dynamic_slice_in_dim(whole_out, own_half * half_width, half_width, 1)
    wg = w_gate[0]
    wu = w_up[0]
    wd = w_down[0]
    slot_weight = lax.dynamic_index_in_dim(combine, own_expert, 0, keepdims=False)
    gate_mine = jnp.dot(rows_in, wg, preferred_element_type=jnp.float32)
    up_mine = jnp.dot(rows_in, wu, preferred_element_type=jnp.float32)
    back_mine = lax.dot_general(
        rows_out, wd, (((1,), (1,)), ((), ())), preferred_element_type=jnp.float32
    )
    gate_other, up_other, back_other = (
        from_partner(gate_mine.astype(jnp.bfloat16), "mp", blocks.bit_length() - 1).astype(
            gate_mine.dtype
        ),
        from_partner(up_mine.astype(jnp.bfloat16), "mp", blocks.bit_length() - 1).astype(
            up_mine.dtype
        ),
        from_partner(back_mine.astype(jnp.bfloat16), "mp", blocks.bit_length() - 1).astype(
            back_mine.dtype
        ),
    )
    gate_pre = gate_mine + gate_other
    up_pre = up_mine + up_other
    back_grad = back_mine + back_other
    sigmoid_gate = jax.nn.sigmoid(gate_pre)
    activation = (gate_pre * sigmoid_gate * up_pre).astype(jnp.bfloat16)
    slot_term = jnp.sum(activation.astype(jnp.float32) * back_grad, axis=1)
    term_keep = (member_ids[:, None] == own_expert) & (own_half == 0)
    term_table = jnp.where(term_keep, slot_term[None, :], 0.0)
    grad_combine = lax.psum(term_table, "mp")
    scaled_out = (slot_weight[:, None] * rows_out.astype(jnp.float32)).astype(jnp.bfloat16)
    grad_down = lax.dot_general(
        activation, scaled_out, (((0,), (0,)), ((), ())), preferred_element_type=jnp.float32
    )
    d_act = slot_weight[:, None] * back_grad
    d_gate = (d_act * up_pre * sigmoid_gate * (1.0 + gate_pre * (1.0 - sigmoid_gate))).astype(
        jnp.bfloat16
    )
    d_up = (d_act * gate_pre * sigmoid_gate).astype(jnp.bfloat16)
    grad_gate = lax.dot_general(
        rows_in, d_gate, (((0,), (0,)), ((), ())), preferred_element_type=jnp.float32
    )
    grad_up = lax.dot_general(
        rows_in, d_up, (((0,), (0,)), ((), ())), preferred_element_type=jnp.float32
    )
    partial_value = jnp.einsum(
        "ch,ldh->lcd",
        d_gate,
        wg.reshape(half_lanes, width_part, hidden),
        preferred_element_type=jnp.float32,
    )
    partial_value = partial_value + jnp.einsum(
        "ch,ldh->lcd",
        d_up,
        wu.reshape(half_lanes, width_part, hidden),
        preferred_element_type=jnp.float32,
    )
    partial_half = partial_value.astype(jnp.bfloat16)
    keep = (member_ids[:, None] == own_expert) & (half_ids[None, :] == own_half)
    padded = jnp.where(keep[:, :, None, None, None], partial_half[None, None], zero_half)
    padded = padded.reshape(exp_dev, lane_count, capacity, width_part)
    summed = lax.psum_scatter(padded, "mp", scatter_dimension=1, tiled=True).astype(jnp.float32)[
        :, 0
    ]
    back_start = jnp.transpose(own_starts)[:, :, None] + offsets[None, None, :]
    back_live = offsets[None, None, :] < jnp.transpose(own_counts)[:, :, None]
    back_index = member_ids[None, :, None] * capacity + jnp.where(back_live, back_start, 0)
    send_back = jnp.where(
        back_live[:, :, :, None], summed.reshape(exp_dev * capacity, width_part)[back_index], 0.0
    )
    returned = lax.all_to_all(
        send_back.astype(jnp.bfloat16), "expert", split_axis=0, concat_axis=0, tiled=True
    ).astype(send_back.dtype)
    targets = jnp.where(send_live, local_row, tok_dev).reshape(-1)
    gathered = (
        jnp.zeros((tok_dev + 1, width_part), jnp.float32)
        .at[targets]
        .add(returned.reshape(-1, width_part))
    )
    grad_tokens = gathered[:tok_dev].astype(jnp.bfloat16)
    return (
        grad_tokens,
        grad_gate.astype(jnp.bfloat16)[None],
        grad_up.astype(jnp.bfloat16)[None],
        grad_down.astype(jnp.bfloat16)[None],
        grad_combine,
    )


def solution(mesh):
    placed = (
        P("expert", "mp"),
        P("expert", "mp"),
        P("expert", None, "mp"),
        P("expert", None, "mp"),
        P("expert", "mp", None),
        P("expert", None),
        P(),
    )
    return jax.shard_map(
        local,
        mesh=mesh,
        in_specs=placed,
        out_specs=(
            P("expert", "mp"),
            P("expert", None, "mp"),
            P("expert", None, "mp"),
            P("expert", "mp", None),
            P("expert", None),
        ),
        check_vma=False,
    )
```

profile of v0, /device:TPU:1, one launch (start us, length us, event | category | flops | bytes accessed | tf_op | source)
XLA Modules:
  0.0 600.9 jit_solution(14179567291219262071)
XLA Ops:
  7.2 0.8 compare_select_fusion.3
  8.0 105.1 %while.24 = (s32[]{:T(128)}, u32[64,33]{1,0:T(8,128)S(1)}, u32[64,33]{1,0:T(8,128)S(1)}, s32[64,128]{1,0:T(8,128)S(1)}, s32[]{:T(128)}, /*index=5*/s32[]{:T(128)}) while((s32[]{:T(128)}, u32[64,33]{1,0:T(8,128)S(1)}, u32[64,33]{1,0:T(8,128)S(1)}, s32[64,128]{1,0:T(8,128)S(1)}, s32[]{:T(128)}, /*index=5*/s32[]{:T(128)}) %tuple.53), condition=%wide.region_1.2_spmd.clone, body=%wide.region_0.1_spmd.clone.sunk | while | flops 48612 | bytes 173537 | solution.py:37
  8.2 12.7 %gather_fusion = s32[2112]{0:T(1024)S(1)} fusion(s32[64,128]{1,0:T(8,128)S(1)} %get-tuple-element.180, u32[2112]{0:T(1024)S(1)} %reshape.579), kind=kCustom, calls=%fused_computation.clone.clone.1 | custom fusion | bytes 33792 | tf_op jit(solution)/shard_map/vmap(jit(searchsorted))/vmap(jit(_searchsorted_scan_impl))/while/body/eval_jaxpr/gather | solution.py:37
  20.9 0.1 squeeze.28
  21.2 0.1 reshape.579
  21.3 12.7 %gather_fusion = s32[2112]{0:T(1024)S(1)} fusion(s32[64,128]{1,0:T(8,128)S(1)} %get-tuple-element.180, u32[2112]{0:T(1024)S(1)} %reshape.579), kind=kCustom, calls=%fused_computation.clone.clone.1 | custom fusion | bytes 33792 | tf_op jit(solution)/shard_map/vmap(jit(searchsorted))/vmap(jit(_searchsorted_scan_impl))/while/body/eval_jaxpr/gather | solution.py:37
  34.3 0.1 reshape.579
  34.4 12.7 %gather_fusion = s32[2112]{0:T(1024)S(1)} fusion(s32[64,128]{1,0:T(8,128)S(1)} %get-tuple-element.180, u32[2112]{0:T(1024)S(1)} %reshape.579), kind=kCustom, calls=%fused_computation.clone.clone.1 | custom fusion | bytes 33792 | tf_op jit(solution)/shard_map/vmap(jit(searchsorted))/vmap(jit(_searchsorted_scan_impl))/while/body/eval_jaxpr/gather | solution.py:37
  47.6 12.7 %gather_fusion = s32[2112]{0:T(1024)S(1)} fusion(s32[64,128]{1,0:T(8,128)S(1)} %get-tuple-element.180, u32[2112]{0:T(1024)S(1)} %reshape.579), kind=kCustom, calls=%fused_computation.clone.clone.1 | custom fusion | bytes 33792 | tf_op jit(solution)/shard_map/vmap(jit(searchsorted))/vmap(jit(_searchsorted_scan_impl))/while/body/eval_jaxpr/gather | solution.py:37
  60.7 12.7 %gather_fusion = s32[2112]{0:T(1024)S(1)} fusion(s32[64,128]{1,0:T(8,128)S(1)} %get-tuple-element.180, u32[2112]{0:T(1024)S(1)} %reshape.579), kind=kCustom, calls=%fused_computation.clone.clone.1 | custom fusion | bytes 33792 | tf_op jit(solution)/shard_map/vmap(jit(searchsorted))/vmap(jit(_searchsorted_scan_impl))/while/body/eval_jaxpr/gather | solution.py:37
  73.8 12.7 %gather_fusion = s32[2112]{0:T(1024)S(1)} fusion(s32[64,128]{1,0:T(8,128)S(1)} %get-tuple-element.180, u32[2112]{0:T(1024)S(1)} %reshape.579), kind=kCustom, calls=%fused_computation.clone.clone.1 | custom fusion | bytes 33792 | tf_op jit(solution)/shard_map/vmap(jit(searchsorted))/vmap(jit(_searchsorted_scan_impl))/while/body/eval_jaxpr/gather | solution.py:37
  87.0 12.7 %gather_fusion = s32[2112]{0:T(1024)S(1)} fusion(s32[64,128]{1,0:T(8,128)S(1)} %get-tuple-element.180, u32[2112]{0:T(1024)S(1)} %reshape.579), kind=kCustom, calls=%fused_computation.clone.clone.1 | custom fusion | bytes 33792 | tf_op jit(solution)/shard_map/vmap(jit(searchsorted))/vmap(jit(_searchsorted_scan_impl))/while/body/eval_jaxpr/gather | solution.py:37
  100.1 12.7 %gather_fusion = s32[2112]{0:T(1024)S(1)} fusion(s32[64,128]{1,0:T(8,128)S(1)} %get-tuple-element.180, u32[2112]{0:T(1024)S(1)} %reshape.579), kind=kCustom, calls=%fused_computation.clone.clone.1 | custom fusion | bytes 33792 | tf_op jit(solution)/shard_map/vmap(jit(searchsorted))/vmap(jit(_searchsorted_scan_impl))/while/body/eval_jaxpr/gather | solution.py:37
  113.2 0.2 dynamic-slice_reduce_fusion
  113.7 0.2 copy-done.1
  113.8 3.6 gather_fusion.6
  118.1 1.3 gather_fusion.1
  119.5 1.3 gather_fusion.3
  120.8 0.1 broadcast_select_fusion.2
  121.0 0.8 reshape.570
  121.8 29.3 %all-to-all-start = ((bf16[32,2,512]{2,1,0:T(2,128)(2,1)}), bf16[32,2,512]{2,1,0:T(2,128)(2,1)S(1)}, u32[]{:S(2)}, u32[]{:S(2)}) async-start(bf16[32,2,512]{2,1,0:T(2,128)(2,1)} %reshape.570), calls=%async_computation | async-start | bytes 131072 | tf_op jit(solution)/shard_map/all_to_all | solution.py:56
  151.0 0.8 reshape.568
  151.8 23.3 %all-to-all-done = bf16[32,2,512]{2,1,0:T(2,128)(2,1)S(1)} async-done(((bf16[32,2,512]{2,1,0:T(2,128)(2,1)}), bf16[32,2,512]{2,1,0:T(2,128)(2,1)S(1)}, u32[]{:S(2)}, u32[]{:S(2)}) %all-to-all-start) | async-done | bytes 65568 | tf_op jit(solution)/shard_map/all_to_all | solution.py:56
  175.1 3.9 all-to-all-start.1
  179.1 2.4 gather_fusion.7
  181.6 0.1 reshape.571
  181.8 0.9 gather_fusion.2
  182.7 19.6 %all-to-all-done.1 = bf16[32,2,512]{2,1,0:T(2,128)(2,1)S(1)} async-done(((bf16[32,2,512]{2,1,0:T(2,128)(2,1)}), bf16[32,2,512]{2,1,0:T(2,128)(2,1)S(1)}, u32[]{:S(2)}, u32[]{:S(2)}) %all-to-all-start.1) | async-done | bytes 65568 | tf_op jit(solution)/shard_map/all_to_all | solution.py:55
  202.3 0.1 reshape.569
  202.5 0.9 gather_fusion.4
  203.5 0.7 broadcast_select_fusion.4
  204.2 0.7 all-gather.5.cloned.1.call-update
  205.2 62.4 %all-gather.3.cloned.1.call-done = bf16[2,128,2048]{1,0,2:T(2,128)(2,1)} async-done(((bf16[2,128,64]{1,0,2:T(2,128)(2,1)}), bf16[2,128,2048]{1,0,2:T(2,128)(2,1)}) %all-gather.3.cloned.1.call-update) | async-done | bytes 1048592 | tf_op jit(solution)/shard_map/all_gather | solution.py:77
  267.6 1.6 constant_dynamic-slice_fusion.1
  269.2 0.4 copy.51
  269.6 0.3 fusion.40
  269.9 3.0 collective-permute-start
  272.9 77.8 %all-gather.5.cloned.1.call-done = bf16[2,128,2048]{1,0,2:T(2,128)(2,1)} async-done(((bf16[2,128,64]{1,0,2:T(2,128)(2,1)}), bf16[2,128,2048]{1,0,2:T(2,128)(2,1)}) %all-gather.5.cloned.1.call-update) | async-done | bytes 1048592 | tf_op jit(solution)/shard_map/all_gather | solution.py:76
  350.7 1.6 constant_dynamic-slice_fusion
  352.3 0.4 copy.52
  352.7 0.2 fusion.41
  352.9 3.0 collective-permute-start.1
  356.0 0.2 fusion.42
  356.2 2.2 collective-permute-start.2
  358.5 2.7 collective-permute-done.2
  361.2 0.2 multiply_reduce_fusion
  361.4 0.3 fusion.23
  361.7 0.3 fusion.6
  362.0 0.3 copy.46
  362.3 0.2 broadcast_in_dim.201
  362.5 1.6 broadcast_select_fusion
  364.8 0.1 compare_select_fusion
  365.2 130.5 %reduce-scatter.2.cloned.1.call-done = bf16[2,1,128,64]{3,2,0,1:T(8,128)(2,1)} async-done(((bf16[2,32,128,64]{3,2,0,1:T(8,128)(2,1)}), bf16[2,1,128,64]{3,2,0,1:T(8,128)(2,1)}) %reduce-scatter.2.cloned.1.call-update) | async-done | bytes 32784 | tf_op jit(solution)/shard_map/reduce_scatter | solution.py:143
  495.7 1.9 gather_fusion.5
  497.7 0.1 select_convert_fusion
  497.8 0.8 reshape.572
  498.6 22.7 %all-to-all-start.2 = ((bf16[32,2,512]{2,1,0:T(2,128)(2,1)}), bf16[32,2,512]{2,1,0:T(2,128)(2,1)S(1)}, u32[]{:S(2)}, u32[]{:S(2)}) async-start(bf16[32,2,512]{2,1,0:T(2,128)(2,1)} %reshape.572), calls=%async_computation.3 | async-start | bytes 131072 | tf_op jit(solution)/shard_map/all_to_all | solution.py:152
  521.4 65.9 %psum.7 = f32[2,128]{1,0:T(2,128)} all-reduce(f32[2,128]{1,0:T(2,128)S(1)} %broadcast_select_fusion.5), channel_id=1, replica_groups=mesh['expert'=32,'mp'=32] {'mp'}, use_global_device_ids=true, to_apply=%region_5.6 | all-reduce | flops 256 | bytes 2048 | tf_op jit(solution)/shard_map/psum | solution.py:111
  587.3 1.1 fusion.2
  588.4 1.1 fusion.3
  589.5 1.2 fusion.4
  590.7 0.1 reshape.573
  590.8 2.8 scatter_custom_fusion
  593.6 0.7 copy.49
  (119 shorter events, 4.9 us)
Async XLA Ops:
  7.2 348.8 %copy-start = (bf16[1,1024,256]{2,1,0:T(8,128)(2,1)S(1)}, bf16[1,1024,256]{2,1,0:T(8,128)(2,1)}, u32[]{:S(2)}) copy-start(bf16[1,1024,256]{2,1,0:T(8,128)(2,1)} %param.11) | copy-start | bytes 1572868
  113.1 0.8 copy-start.1
  113.8 3.6 copy-start.4
  113.8 4.2 copy-start.5
  121.8 53.4 %all-to-all-start = ((bf16[32,2,512]{2,1,0:T(2,128)(2,1)}), bf16[32,2,512]{2,1,0:T(2,128)(2,1)S(1)}, u32[]{:S(2)}, u32[]{:S(2)}) async-start(bf16[32,2,512]{2,1,0:T(2,128)(2,1)} %reshape.570), calls=%async_computation | async-start | bytes 131072 | tf_op jit(solution)/shard_map/all_to_all | solution.py:56
  175.1 27.2 %all-to-all-start.1 = ((bf16[32,2,512]{2,1,0:T(2,128)(2,1)}), bf16[32,2,512]{2,1,0:T(2,128)(2,1)S(1)}, u32[]{:S(2)}, u32[]{:S(2)}) async-start(bf16[32,2,512]{2,1,0:T(2,128)(2,1)} %reshape.568), calls=%async_computation.1 | async-start | bytes 131072 | tf_op jit(solution)/shard_map/all_to_all | solution.py:55
  179.0 88.6 %all-gather.3.cloned.1.call-start = ((), (), s32[]{:S(2)}) async-start(), calls=%async_computation.4 | async-start | bytes 1081344 | tf_op jit(solution)/shard_map/all_gather | solution.py:77
  202.5 67.1 %copy-start.3 = (bf16[1,256,1024]{2,1,0:T(8,128)(2,1)S(1)}, bf16[1,256,1024]{2,1,0:T(8,128)(2,1)}, u32[]{:S(2)}) copy-start(bf16[1,256,1024]{2,1,0:T(8,128)(2,1)} %param.13) | copy-start | bytes 1572868
  204.2 146.5 %all-gather.5.cloned.1.call-start = ((), (), s32[]{:S(2)}) async-start(), calls=%async_computation.5 | async-start | bytes 1081344 | tf_op jit(solution)/shard_map/all_gather | solution.py:76
  204.9 290.8 %reduce-scatter.2.cloned.1.call-start = ((), (), s32[]{:S(2)}) async-start(), calls=%async_computation.6 | async-start | bytes 2162688 | tf_op jit(solution)/shard_map/reduce_scatter | solution.py:143
  269.5 83.1 %copy-start.2 = (bf16[1,1024,256]{2,1,0:T(8,128)(2,1)S(1)}, bf16[1,1024,256]{2,1,0:T(8,128)(2,1)}, u32[]{:S(2)}) copy-start(bf16[1,1024,256]{2,1,0:T(8,128)(2,1)} %param.12) | copy-start | bytes 1572868
  269.9 88.6 %collective-permute-start = (bf16[128,256]{1,0:T(8,128)(2,1)S(1)}, bf16[128,256]{1,0:T(8,128)(2,1)S(1)}, u32[]{:S(2)}, u32[]{:S(2)}) collective-permute-start(bf16[128,256]{1,0:T(8,128)(2,1)S(1)} %get-tuple-element.126), channel_id=1, source_target_pairs={{0,8},{8,0},{1,9},{9,1},{2,10},{10,2},{3,11},{11,3},{4,12},{12,4},... | collective-permute-start | bytes 196616 | tf_op jit(solution)/shard_map/ppermute | solution.py:14
  352.3 6.2 %copy-start.6 = (f32[2,128]{1,0:T(2,128)S(1)}, f32[2,128]{1,0:T(2,128)}, u32[]{:S(2)}) copy-start(f32[2,128]{1,0:T(2,128)} %param.14) | copy-start | bytes 3076
  352.9 5.6 collective-permute-start.1
  356.2 5.0 collective-permute-start.2
  498.6 92.1 %all-to-all-start.2 = ((bf16[32,2,512]{2,1,0:T(2,128)(2,1)}), bf16[32,2,512]{2,1,0:T(2,128)(2,1)S(1)}, u32[]{:S(2)}, u32[]{:S(2)}) async-start(bf16[32,2,512]{2,1,0:T(2,128)(2,1)} %reshape.572), calls=%async_computation.3 | async-start | bytes 131072 | tf_op jit(solution)/shard_map/all_to_all | solution.py:152
Sparse Core Ops, SparseCore 0:
  204.3 63.2 all-gather.2
  272.5 78.1 all-gather.4
  364.2 131.4 reduce-scatter.1
where the time goes:
time: 601 us
  waiting for transfers between devices  317 us (53%)
  local copies, waits for them, and re-layouts  126 us (21%)
  blocking collectives  65.9 us (11%)
  starting transfers between devices  64.3 us (11%)
  between operations  14.3 us (2%)
  other arithmetic  7.7 us (1%)
    reduce_scatter x1, waiting for transfers between devices, local(): lax.psum_scatter(padded, 'mp', scatter_dimension=1, tiled=True)  130 us
    gather x16, local copies, waits for them, and re-layouts, local(): jnp.searchsorted(row_keys, bounds, side='left')  103 us
    all_gather x1, waiting for transfers between devices, local(): lax.all_gather(compact_in, 'mp', axis=2, tiled=True)  77.8 us
    psum x1, blocking collectives, local(): grad_combine = lax.psum(term_table, 'mp')  65.9 us
    all_gather x1, waiting for transfers between devices, local(): lax.all_gather(compact_out, 'mp', axis=2, tiled=True)  62.4 us
    all_to_all x1, starting transfers between devices, local(): lax.all_to_all(send_out, 'expert', split_axis=0, concat_axis=0, tiled=True)  29.3 us
    all_to_all x1, waiting for transfers between devices, local(): lax.all_to_all(send_out, 'expert', split_axis=0, concat_axis=0, tiled=True)  23.3 us
    all_to_all x1, starting transfers between devices, local(): lax.all_to_all(send_back.astype(jnp.bfloat16), 'expert', split_axis=0, co...  22.7 us
  transfers between devices with their start and end apart: 9, of which 6 were waited for; matrix products, arithmetic and copies ran while one was open for 2% of the time, Pallas kernels for 0%

commit v1 on v0

v1 whole, which is shorter than its diff:
```python
import jax
import jax.numpy as jnp
from jax import lax
from jax.sharding import Mesh
from jax.sharding import PartitionSpec as P


def local(x_tokens, cotangent, w_gate, w_up, w_down, combine, indices):
    bf16 = jnp.bfloat16
    f32 = jnp.float32
    groups = lax.axis_size("z")
    spread = lax.axis_size("x") * lax.axis_size("c")
    tok_dev, part = x_tokens.shape
    experts, capacity = indices.shape
    exp_dev = experts // groups
    peer = 2 * capacity // groups
    z = lax.axis_index("z")
    p = lax.axis_index("p")
    q = lax.axis_index("q")
    wg = w_gate[0]
    wu = w_up[0]
    wd = w_down[0]

    table = jnp.concatenate([x_tokens, cotangent], axis=1)
    table = lax.ppermute(table, ("p", "q"), [(0, 0), (1, 2), (2, 1), (3, 3)])

    slots = jnp.arange(capacity, dtype=jnp.int32)
    places = jnp.arange(peer, dtype=jnp.int32)
    tokens = jnp.arange(tok_dev, dtype=jnp.int32)
    ordered = jnp.transpose(indices.reshape(groups, exp_dev, capacity), (1, 0, 2)).reshape(
        experts, capacity
    )
    base = z * tok_dev
    start = jnp.sum(((ordered >= 0) & (ordered < base)).astype(jnp.int32), axis=1)
    want = start[:, None] + places[None, :]
    shifted = jnp.where(ordered >= 0, ordered - base + 1, 0)
    chosen = (
        jnp.sum(jnp.where(slots[None, None, :] == want[:, :, None], shifted[:, None, :], 0), axis=2)
        - 1
    )
    pick = (chosen[:, :, None] == tokens[None, None, :]).astype(bf16)
    pick = pick.reshape(experts * peer, tok_dev)
    send = jnp.dot(pick, table, preferred_element_type=f32).astype(bf16)
    recv = lax.all_to_all(
        send.reshape(experts, peer, 2 * part), ("p", "z"), split_axis=0, concat_axis=0, tiled=True
    )

    own = lax.dynamic_index_in_dim(indices, z * exp_dev + p, 0, keepdims=False)
    blocks = jnp.arange(groups, dtype=jnp.int32)
    own_start = jnp.sum(
        ((own[None, :] >= 0) & (own[None, :] < blocks[:, None] * tok_dev)).astype(jnp.int32), axis=1
    )
    own_want = own_start[:, None] + places[None, :]
    own_block = jnp.where(own >= 0, own // tok_dev, -1)
    place = (slots[:, None, None] == own_want[None]) & (
        own_block[:, None, None] == blocks[None, :, None]
    )
    place = place.astype(bf16).reshape(capacity, groups * peer)
    recv = recv.reshape(2, groups * peer, 2 * part)
    compact = jnp.concatenate(
        [jnp.dot(place, recv[i], preferred_element_type=f32).astype(bf16) for i in range(2)], axis=1
    )
    gathered = lax.all_gather(compact, ("x", "c"), axis=0)
    gathered = gathered.reshape(spread, capacity, 2, 2, part)
    rows = jnp.transpose(gathered, (3, 1, 2, 0, 4)).reshape(2, capacity, 2 * spread * part)
    rows_in = rows[0]
    rows_out = rows[1]

    hidden = wg.shape[1]
    gate_mine = jnp.dot(rows_in, wg, preferred_element_type=f32)
    up_mine = jnp.dot(rows_in, wu, preferred_element_type=f32)
    back_mine = lax.dot_general(rows_out, wd, (((1,), (1,)), ((), ())), preferred_element_type=f32)
    mine = jnp.concatenate([gate_mine, up_mine, back_mine], axis=1)
    other = lax.ppermute(mine.astype(bf16), "q", [(0, 1), (1, 0)]).astype(f32)
    total = mine + other
    gate_pre = total[:, :hidden]
    up_pre = total[:, hidden : 2 * hidden]
    back_grad = total[:, 2 * hidden :]

    weight = lax.dynamic_index_in_dim(combine, p, 0, keepdims=False)[:, None]
    sig = jax.nn.sigmoid(gate_pre)
    activation = (gate_pre * sig * up_pre).astype(bf16)
    term = jnp.sum(activation.astype(f32) * back_grad, axis=1)
    d_act = weight * back_grad
    d_gate = (d_act * up_pre * sig * (1.0 + gate_pre * (1.0 - sig))).astype(bf16)
    d_up = (d_act * gate_pre * sig).astype(bf16)
    piece = lax.dot_general(d_gate, wg, (((1,), (1,)), ((), ())), preferred_element_type=f32)
    piece = piece + lax.dot_general(d_up, wu, (((1,), (1,)), ((), ())), preferred_element_type=f32)
    piece = piece.astype(bf16).reshape(capacity, 2, spread, part)
    piece = jnp.transpose(piece, (2, 0, 1, 3)).reshape(spread, capacity, 2 * part)
    high = lax.reduce_precision(term, 8, 7)
    extra = jnp.stack([high.astype(bf16), (term - high).astype(bf16)])
    extra = jnp.pad(extra, ((0, 14), (0, 0)))
    piece = jnp.concatenate(
        [piece, jnp.broadcast_to(extra[None], (spread,) + extra.shape)], axis=1
    )
    pieces = lax.all_to_all(piece, ("x", "c"), split_axis=0, concat_axis=0, tiled=True)
    summed = jnp.sum(pieces.astype(f32), axis=0)
    term_sum = summed[capacity] + summed[capacity + 1]
    summed = summed[:capacity].astype(bf16)

    back = lax.dot_general(
        place, summed, (((0,), (0,)), ((), ())), preferred_element_type=f32
    ).astype(bf16)
    back = jnp.transpose(back.reshape(groups, peer, 2, part), (2, 0, 1, 3))
    back = jnp.stack([jnp.where(q == i, back, jnp.zeros((), bf16)) for i in range(2)])
    returned = lax.all_to_all(
        back.reshape(4 * groups, peer * part),
        ("p", "q", "z"),
        split_axis=0,
        concat_axis=0,
        tiled=True,
    )
    returned = returned.reshape(2, 2, groups * peer, part)
    returned = lax.dynamic_index_in_dim(returned, p, 1, keepdims=False)
    grad_tokens = lax.dot_general(
        pick,
        returned.reshape(experts * peer, part),
        (((0,), (0,)), ((), ())),
        preferred_element_type=f32,
    ).astype(bf16)

    from_zero = lax.ppermute(term_sum, "q", [(0, 1)])
    term_sum = jnp.where(q == 0, term_sum, from_zero)
    term_other = lax.ppermute(term_sum, "p", [(0, 1), (1, 0)])
    grad_combine = jnp.stack(
        [jnp.where(p == 0, term_sum, term_other), jnp.where(p == 0, term_other, term_sum)]
    )

    scaled_out = (weight * rows_out.astype(f32)).astype(bf16)
    over_slots = (((0,), (0,)), ((), ()))
    grad_down = lax.dot_general(activation, scaled_out, over_slots, preferred_element_type=f32)
    grad_gate = lax.dot_general(rows_in, d_gate, over_slots, preferred_element_type=f32)
    grad_up = lax.dot_general(rows_in, d_up, over_slots, preferred_element_type=f32)
    return (
        grad_tokens,
        grad_gate.astype(bf16)[None],
        grad_up.astype(bf16)[None],
        grad_down.astype(bf16)[None],
        grad_combine,
    )


def solution(mesh):
    groups, lanes = mesh.devices.shape
    split = Mesh(
        mesh.devices.reshape(groups, 2, 2, lanes // 8, 2), ("z", "p", "q", "x", "c")
    )
    mp = ("p", "q", "x", "c")
    placed = (
        P("z", mp),
        P("z", mp),
        P("z", None, mp),
        P("z", None, mp),
        P("z", mp, None),
        P("z", None),
        P(),
    )
    return jax.shard_map(
        local,
        mesh=split,
        in_specs=placed,
        out_specs=(
            P("z", mp),
            P("z", None, mp),
            P("z", None, mp),
            P("z", mp, None),
            P("z", None),
        ),
        check_vma=False,
    )
```

time: 601 us -> 154 us (0.26)
  waiting for transfers between devices: 317 us -> 58.6 us
  local copies, waits for them, and re-layouts: 126 us -> 6.85 us
  blocking collectives: 65.9 us -> 18.4 us
  between operations: 14.3 us -> 1.08 us
  starting transfers between devices: 64.3 us -> 55 us
    all_gather x2 -> x0, waiting for transfers between devices: 140 us -> none  [the longest x1 77.8 us: local(): lax.all_gather(compact_in, 'mp', axis=2, tiled=True)]
    reduce_scatter x1 -> x0, waiting for transfers between devices: 130 us -> none  [local(): lax.psum_scatter(padded, 'mp', scatter_dimension=1, tiled=True)]
    gather x27 -> x0, local copies, waits for them, and re-layouts: 116 us -> none  [the longest x16 103 us: local(): jnp.searchsorted(row_keys, bounds, side='left')]
    psum x1 -> x0, blocking collectives: 65.9 us -> none  [local(): grad_combine = lax.psum(term_table, 'mp')]
    all_gather x0 -> x1, blocking collectives: none -> 18.4 us  [local(): gathered = lax.all_gather(compact, ('x', 'c'), axis=0)]
    all_to_all x3, starting transfers between devices: 55.9 us -> 45.1 us  [the longest x1 34.7 us: local(): lax.all_to_all(send.reshape(experts, peer, 2 * part), ('p', 'z'), split_a...]
    all_to_all x3, waiting for transfers between devices: 42.9 us -> 53 us  [the longest x1 27.8 us: local(): lax.all_to_all(send.reshape(experts, peer, 2 * part), ('p', 'z'), split_a...]
  transfers between devices with their start and end apart: 9 -> 7, of which waited for: 6 -> 4; matrix products, arithmetic and copies ran while one was open for 2% -> 4% of each run, Pallas kernels for 0% -> 0%
where the time goes in v1:
time: 154 us; the launch traced here: 153 us
  waiting for transfers between devices  58.6 us (38%)
  starting transfers between devices  55 us (36%)
  blocking collectives  18.4 us (12%)
  matrix products  7.29 us (5%)
  local copies, waits for them, and re-layouts  6.85 us (4%)
  other arithmetic  5.82 us (4%)
    all_to_all x1, starting transfers between devices, local(): lax.all_to_all(send.reshape(experts, peer, 2 * part), ('p', 'z'), split_a...  34.7 us
    all_to_all x1, waiting for transfers between devices, local(): lax.all_to_all(send.reshape(experts, peer, 2 * part), ('p', 'z'), split_a...  27.8 us
    all_to_all x1, waiting for transfers between devices, local(): lax.all_to_all(back.reshape(4 * groups, peer * part), ('p', 'q', 'z'), sp...  19.8 us
    all_gather x1, blocking collectives, local(): gathered = lax.all_gather(compact, ('x', 'c'), axis=0)  18.4 us
    all_to_all x1, starting transfers between devices, local(): lax.all_to_all(back.reshape(4 * groups, peer * part), ('p', 'q', 'z'), sp...  6.15 us
    ppermute x1, waiting for transfers between devices, local(): other = lax.ppermute(mine.astype(bf16), 'q', [(0, 1), (1, 0)]).astype(f32)  5.63 us
    all_to_all x1, waiting for transfers between devices, local(): lax.all_to_all(piece, ('x', 'c'), split_axis=0, concat_axis=0, tiled=True)  5.44 us
    ppermute x1, starting transfers between devices, local(): term_other = lax.ppermute(term_sum, 'p', [(0, 1), (1, 0)])  4.73 us
  transfers between devices with their start and end apart: 7, of which 4 were waited for; matrix products, arithmetic and copies ran while one was open for 4% of the time, Pallas kernels for 0%

profile of v1, /device:TPU:1, one launch (start us, length us, event | category | flops | bytes accessed | tf_op | source)
XLA Modules:
  0.0 153.0 jit_solution(14955100372211139716)
XLA Ops:
  0.6 0.0 copy-start
  0.7 0.8 pad_maximum_fusion.4
  1.5 0.7 collective-permute-start
  2.1 0.1 convert_reduce_fusion.1
  2.2 0.1 reshape.238
  2.4 0.1 copy.54
  2.4 0.1 add.106
  2.5 0.1 iota_add_fusion
  2.6 1.2 select_reduce_fusion
  3.9 0.1 sub.38
  4.0 0.9 fusion.4
  4.9 34.7 %all-to-all-start = ((bf16[64,8,128]{2,1,0:T(8,128)(2,1)}), bf16[64,8,128]{2,1,0:T(8,128)(2,1)S(1)}, u32[]{:S(2)}, u32[]{:S(2)}) async-start(bf16[64,8,128]{2,1,0:T(8,128)(2,1)} %fusion.4), calls=%async_computation | async-start | bytes 262144 | tf_op jit(solution)/shard_map/all_to_all | solution.py:44
  39.6 0.2 convert_reduce_fusion.2
  39.8 0.1 iota_add_fusion.1
  39.9 27.8 %all-to-all-done = bf16[64,8,128]{2,1,0:T(8,128)(2,1)S(1)} async-done(((bf16[64,8,128]{2,1,0:T(8,128)(2,1)}), bf16[64,8,128]{2,1,0:T(8,128)(2,1)S(1)}, u32[]{:S(2)}, u32[]{:S(2)}) %all-to-all-start) | async-done | bytes 131104 | tf_op jit(solution)/shard_map/all_to_all | solution.py:44
  67.6 0.3 fusion.5
  67.9 0.3 fusion.6
  68.2 18.4 %all-gather = bf16[1024,256]{0,1:T(8,128)(2,1)S(1)} all-gather(bf16[128,256]{0,1:T(8,128)(2,1)S(1)} %pad_maximum_fusion.3), channel_id=2, replica_groups=mesh['z'=32,'p'=2,'q'=2,'x'=4,'c'=2] {'x','c'}, dimensions={0}, use_global_device_ids=true | all-gather | bytes 589824 | tf_op jit(solution)/shard_map/all_gather | solution.py:63
  86.5 0.1 copy.70
  86.6 0.1 copy.74
  86.8 1.0 copy-done.1
  87.8 0.3 fusion.10
  88.1 0.3 fusion.14
  88.4 0.8 copy-done.2
  89.1 0.3 fusion.7
  89.5 1.9 %collective-permute-start.1 = (bf16[128,768]{1,0:T(8,128)(2,1)S(1)}, bf16[128,768]{1,0:T(8,128)(2,1)S(1)}, u32[]{:S(2)}, u32[]{:S(2)}) collective-permute-start(bf16[128,768]{1,0:T(8,128)(2,1)S(1)} %fusion.16), channel_id=1, source_target_pairs={{0,8},{8,0},{1,9},{9,1},{2,10},{10,2},{3,11},{11,3},{4,12},{12,4},... | collective-permute-start | bytes 589832 | tf_op jit(solution)/shard_map/ppermute | solution.py:74
  91.4 0.7 copy-done.4
  92.1 5.6 %collective-permute-done.1 = bf16[128,768]{1,0:T(8,128)(2,1)S(1)} collective-permute-done((bf16[128,768]{1,0:T(8,128)(2,1)S(1)}, bf16[128,768]{1,0:T(8,128)(2,1)S(1)}, u32[]{:S(2)}, u32[]{:S(2)}) %collective-permute-start.1) | collective-permute-done | bytes 196640 | tf_op jit(solution)/shard_map/ppermute | solution.py:74
  97.8 0.1 multiply_convert_fusion.3
  97.9 0.3 fusion.12
  98.2 0.3 fusion.3
  98.5 0.2 copy.57
  98.8 0.1 copy.66
  99.0 0.1 pad_maximum_fusion
  99.1 0.9 copy.60
  100.0 4.3 %all-to-all-start.1 = ((bf16[8,144,128]{2,1,0:T(8,128)(2,1)}), bf16[8,144,128]{2,1,0:T(8,128)(2,1)S(1)}, u32[]{:S(2)}, u32[]{:S(2)}) async-start(bf16[8,144,128]{2,1,0:T(8,128)(2,1)} %copy.60), calls=%async_computation.1 | async-start | bytes 589824 | tf_op jit(solution)/shard_map/all_to_all | solution.py:97
  104.3 0.1 add.115
  104.4 0.1 add.116
  104.5 0.1 add.118
  104.6 1.1 fusion.2
  105.7 5.4 %all-to-all-done.1 = bf16[8,144,128]{2,1,0:T(8,128)(2,1)S(1)} async-done(((bf16[8,144,128]{2,1,0:T(8,128)(2,1)}), bf16[8,144,128]{2,1,0:T(8,128)(2,1)S(1)}, u32[]{:S(2)}, u32[]{:S(2)}) %all-to-all-start.1) | async-done | bytes 294944 | tf_op jit(solution)/shard_map/all_to_all | solution.py:97
  111.2 0.1 copy.67
  111.3 0.2 broadcast_select_fusion.1
  111.5 0.1 select_n.103
  111.7 0.1 select_n.99
  111.8 0.1 pad_maximum_fusion.2
  111.9 0.2 all_to_all.16
  112.0 0.5 broadcast.198
  112.5 1.4 reduce.7
  114.0 0.7 reshape.245
  114.6 6.2 %all-to-all-start.2 = ((bf16[128,2,256]{2,1,0:T(2,128)(2,1)}), bf16[128,2,256]{2,1,0:T(2,128)(2,1)S(1)}, u32[]{:S(2)}, u32[]{:S(2)}) async-start(bf16[128,2,256]{2,1,0:T(2,128)(2,1)} %reshape.245), calls=%async_computation.2 | async-start | bytes 262144 | tf_op jit(solution)/shard_map/all_to_all | solution.py:107
  120.8 0.1 copy.68
  120.9 0.1 copy.69
  121.0 0.1 add_reduce_fusion
  121.2 2.6 %collective-permute-start.2 = (f32[128]{0:T(128)S(1)}, f32[128]{0:T(128)S(1)}, u32[]{:S(2)}, u32[]{:S(2)}) collective-permute-start(f32[128]{0:T(128)S(1)} %add_reduce_fusion), channel_id=1, source_target_pairs={{0,8},{1,9},{2,10},{3,11},{4,12},{5,13},{6,14},{7,15},{16,24},{17,... | collective-permute-start | bytes 1544 | tf_op jit(solution)/shard_map/ppermute | solution.py:123
  123.7 1.1 fusion
  124.8 4.7 %collective-permute-start.3 = (f32[128]{0:T(128)S(1)}, f32[128]{0:T(128)S(1)}, u32[]{:S(2)}, u32[]{:S(2)}) collective-permute-start(f32[128]{0:T(128)S(1)} %broadcast_select_fusion.2), channel_id=1, source_target_pairs={{0,16},{16,0},{1,17},{17,1},{2,18},{18,2},{3,19},{19,3},{4,20},{20... | collective-permute-start | bytes 1544 | tf_op jit(solution)/shard_map/ppermute | solution.py:125
  129.6 1.1 fusion.1
  130.6 0.6 pad_maximum_fusion.5
  131.2 19.8 %all-to-all-done.2 = bf16[128,2,256]{2,1,0:T(2,128)(2,1)S(1)} async-done(((bf16[128,2,256]{2,1,0:T(2,128)(2,1)}), bf16[128,2,256]{2,1,0:T(2,128)(2,1)S(1)}, u32[]{:S(2)}, u32[]{:S(2)}) %all-to-all-start.2) | async-done | bytes 131104 | tf_op jit(solution)/shard_map/all_to_all | solution.py:107
  151.0 0.1 reshape.246
  151.1 0.8 reduce.3
  151.9 0.2 reshape.233
  152.1 0.9 convolution_convert_fusion.5
  (34 shorter events, 0.4 us)
Async XLA Ops:
  0.6 87.5 %copy-start = (bf16[1,1024,256]{2,1,0:T(8,128)(2,1)S(1)}, bf16[1,1024,256]{2,1,0:T(8,128)(2,1)}, u32[]{:S(2)}) copy-start(bf16[1,1024,256]{2,1,0:T(8,128)(2,1)} %param.9) | copy-start | bytes 1572868
  0.6 1.5 copy-start.3
  1.5 2.5 %collective-permute-start = (bf16[128,128]{0,1:T(8,128)(2,1)S(1)}, bf16[128,128]{0,1:T(8,128)(2,1)S(1)}, u32[]{:S(2)}, u32[]{:S(2)}) collective-permute-start(bf16[128,128]{0,1:T(8,128)(2,1)S(1)} %pad_maximum_fusion.4), channel_id=1, source_target_pairs={{0,0},{8,16},{16,8},{24,24},{1,1},{9,17},{17,9},{25,25},{2,2},{10,... | collective-permute-start | bytes 98312 | tf_op jit(solution)/shard_map/ppermute | solution.py:25
  4.9 62.8 %all-to-all-start = ((bf16[64,8,128]{2,1,0:T(8,128)(2,1)}), bf16[64,8,128]{2,1,0:T(8,128)(2,1)S(1)}, u32[]{:S(2)}, u32[]{:S(2)}) async-start(bf16[64,8,128]{2,1,0:T(8,128)(2,1)} %fusion.4), calls=%async_computation | async-start | bytes 262144 | tf_op jit(solution)/shard_map/all_to_all | solution.py:44
  86.8 1.0 copy-start.1
  88.1 1.0 copy-start.2
  89.5 8.2 %collective-permute-start.1 = (bf16[128,768]{1,0:T(8,128)(2,1)S(1)}, bf16[128,768]{1,0:T(8,128)(2,1)S(1)}, u32[]{:S(2)}, u32[]{:S(2)}) collective-permute-start(bf16[128,768]{1,0:T(8,128)(2,1)S(1)} %fusion.16), channel_id=1, source_target_pairs={{0,8},{8,0},{1,9},{9,1},{2,10},{10,2},{3,11},{11,3},{4,12},{12,4},... | collective-permute-start | bytes 589832 | tf_op jit(solution)/shard_map/ppermute | solution.py:74
  91.4 0.7 copy-start.4
  100.0 11.1 %all-to-all-start.1 = ((bf16[8,144,128]{2,1,0:T(8,128)(2,1)}), bf16[8,144,128]{2,1,0:T(8,128)(2,1)S(1)}, u32[]{:S(2)}, u32[]{:S(2)}) async-start(bf16[8,144,128]{2,1,0:T(8,128)(2,1)} %copy.60), calls=%async_computation.1 | async-start | bytes 589824 | tf_op jit(solution)/shard_map/all_to_all | solution.py:97
  114.6 36.4 %all-to-all-start.2 = ((bf16[128,2,256]{2,1,0:T(2,128)(2,1)}), bf16[128,2,256]{2,1,0:T(2,128)(2,1)S(1)}, u32[]{:S(2)}, u32[]{:S(2)}) async-start(bf16[128,2,256]{2,1,0:T(2,128)(2,1)} %reshape.245), calls=%async_computation.2 | async-start | bytes 262144 | tf_op jit(solution)/shard_map/all_to_all | solution.py:107
  121.2 3.7 %collective-permute-start.2 = (f32[128]{0:T(128)S(1)}, f32[128]{0:T(128)S(1)}, u32[]{:S(2)}, u32[]{:S(2)}) collective-permute-start(f32[128]{0:T(128)S(1)} %add_reduce_fusion), channel_id=1, source_target_pairs={{0,8},{1,9},{2,10},{3,11},{4,12},{5,13},{6,14},{7,15},{16,24},{17,... | collective-permute-start | bytes 1544 | tf_op jit(solution)/shard_map/ppermute | solution.py:123
  124.8 5.8 %collective-permute-start.3 = (f32[128]{0:T(128)S(1)}, f32[128]{0:T(128)S(1)}, u32[]{:S(2)}, u32[]{:S(2)}) collective-permute-start(f32[128]{0:T(128)S(1)} %broadcast_select_fusion.2), channel_id=1, source_target_pairs={{0,16},{16,0},{1,17},{17,1},{2,18},{18,2},{3,19},{19,3},{4,20},{20... | collective-permute-start | bytes 1544 | tf_op jit(solution)/shard_map/ppermute | solution.py:125

commit v2 on v1

v2 whole, which is shorter than its diff:
```python
import jax
import jax.numpy as jnp
from jax import lax
from jax.sharding import Mesh
from jax.sharding import PartitionSpec as P


def local(x_tokens, cotangent, w_gate, w_up, w_down, combine, indices):
    bf16 = jnp.bfloat16
    f32 = jnp.float32
    groups = lax.axis_size("z")
    spread = lax.axis_size("x") * lax.axis_size("c")
    tok_dev, part = x_tokens.shape
    experts, capacity = indices.shape
    exp_dev = experts // groups
    peer = 2 * capacity // groups
    z = lax.axis_index("z")
    p = lax.axis_index("p")
    q = lax.axis_index("q")
    wg = w_gate[0]
    wu = w_up[0]
    wd = w_down[0]

    table = jnp.concatenate([x_tokens, cotangent], axis=1)
    table = lax.ppermute(table, ("p", "q"), [(0, 0), (1, 2), (2, 1), (3, 3)])

    swap = [(0, 1), (1, 0)]
    wg_far = lax.ppermute(wg, "q", swap)
    wu_far = lax.ppermute(wu, "q", swap)
    wd_far = lax.ppermute(wd, "q", swap)

    slots = jnp.arange(capacity, dtype=jnp.int32)
    places = jnp.arange(peer, dtype=jnp.int32)
    tokens = jnp.arange(tok_dev, dtype=jnp.int32)
    ordered = jnp.transpose(indices.reshape(groups, exp_dev, capacity), (1, 0, 2)).reshape(
        experts, capacity
    )
    base = z * tok_dev
    start = jnp.sum(((ordered >= 0) & (ordered < base)).astype(jnp.int32), axis=1)
    want = start[:, None] + places[None, :]
    shifted = jnp.where(ordered >= 0, ordered - base + 1, 0)
    chosen = (
        jnp.sum(jnp.where(slots[None, None, :] == want[:, :, None], shifted[:, None, :], 0), axis=2)
        - 1
    )
    pick = (chosen[:, :, None] == tokens[None, None, :]).astype(bf16)
    pick = pick.reshape(experts * peer, tok_dev)
    send = jnp.dot(pick, table, preferred_element_type=f32).astype(bf16)
    recv = lax.all_to_all(
        send.reshape(experts, peer, 2 * part), ("p", "z"), split_axis=0, concat_axis=0, tiled=True
    )

    own = lax.dynamic_slice_in_dim(indices, z * exp_dev, exp_dev, 0)
    cells = jnp.arange(groups * peer, dtype=jnp.int32)
    cell_block = cells // peer
    earlier = (own[:, None, :] >= 0) & (own[:, None, :] < cell_block[None, :, None] * tok_dev)
    own_want = jnp.sum(earlier.astype(jnp.int32), axis=2) + cells % peer
    own_block = jnp.where(own >= 0, own // tok_dev, -1)
    place = jnp.where(own_block[:, :, None] == cell_block[None, None, :], own_want[:, None, :], -1)
    place = (place == slots[None, :, None]).astype(bf16)
    own_place = lax.dynamic_index_in_dim(place, p, 0, keepdims=False)
    recv, wg_far, wu_far, wd_far = lax.optimization_barrier((recv, wg_far, wu_far, wd_far))
    recv = recv.reshape(2, groups * peer, 2 * part)
    taken = [jnp.dot(own_place, recv[i], preferred_element_type=f32).astype(bf16) for i in range(2)]
    compact = jnp.concatenate(
        [taken[0][:, :part], taken[1][:, :part], taken[0][:, part:], taken[1][:, part:]], axis=1
    )
    half_cap = capacity // 2
    compact = compact.reshape(2, 1, half_cap, 4 * part)
    spreadout = jnp.broadcast_to(compact, (2, spread, half_cap, 4 * part))
    gathered = lax.all_to_all(
        spreadout.reshape(2 * spread, half_cap, 4 * part),
        ("q", "x", "c"),
        split_axis=0,
        concat_axis=0,
        tiled=True,
    ).reshape(2, spread, half_cap, 2, 2, part)

    def natural(block):
        return jnp.transpose(block, (2, 1, 3, 0, 4)).reshape(2, half_cap, 2 * spread * part)

    mine = natural(lax.dynamic_index_in_dim(gathered, q, 0, keepdims=False))
    theirs = natural(lax.dynamic_index_in_dim(gathered, 1 - q, 0, keepdims=False))

    def rows_by(first, second):
        return jnp.dot(mine[0], first, preferred_element_type=f32) + jnp.dot(
            theirs[0], second, preferred_element_type=f32
        )

    across = (((1,), (1,)), ((), ()))
    gate_pre = rows_by(wg, wg_far)
    up_pre = rows_by(wu, wu_far)
    back_grad = lax.dot_general(mine[1], wd, across, preferred_element_type=f32)
    back_grad = back_grad + lax.dot_general(theirs[1], wd_far, across, preferred_element_type=f32)

    weight = lax.dynamic_slice(combine, (p, q * half_cap), (1, half_cap)).reshape(half_cap, 1)
    sig = jax.nn.sigmoid(gate_pre)
    activation = (gate_pre * sig * up_pre).astype(bf16)
    term = jnp.sum(activation.astype(f32) * back_grad, axis=1)
    d_act = weight * back_grad
    d_gate = (d_act * up_pre * sig * (1.0 + gate_pre * (1.0 - sig))).astype(bf16)
    d_up = (d_act * gate_pre * sig).astype(bf16)

    def pieces_of(first, second):
        piece = lax.dot_general(d_gate, first, across, preferred_element_type=f32)
        piece = piece + lax.dot_general(d_up, second, across, preferred_element_type=f32)
        piece = piece.astype(bf16).reshape(2, half_cap // 2, 2, spread, part)
        piece = jnp.transpose(piece, (2, 3, 1, 0, 4))
        return piece.reshape(2 * spread, half_cap // 2, 2 * part)

    near = pieces_of(wg, wu)
    far = pieces_of(wg_far, wu_far)
    piece = jnp.concatenate([jnp.where(q == 0, near, far), jnp.where(q == 0, far, near)], axis=0)
    high = lax.reduce_precision(term, 8, 7)
    extra = jnp.concatenate([high.astype(bf16), (term - high).astype(bf16)]).reshape(1, 2 * half_cap)
    extra = jnp.pad(extra, ((0, 7), (0, 0)))
    piece = jnp.concatenate(
        [piece, jnp.broadcast_to(extra[None], (4 * spread,) + extra.shape)], axis=1
    )
    pieces = lax.all_to_all(piece, ("p", "q", "x", "c"), split_axis=0, concat_axis=0, tiled=True)
    pieces = pieces.reshape(2, 2, spread, half_cap // 2 + 8, 2 * part)
    summed = jnp.sum(pieces.astype(f32), axis=2)
    term_sum = summed[:, :, half_cap // 2]
    grad_combine = (term_sum[:, :, :half_cap] + term_sum[:, :, half_cap:]).reshape(
        exp_dev, capacity
    )
    summed = summed[:, :, : half_cap // 2].astype(bf16)
    summed = jnp.transpose(
        summed.reshape(exp_dev, 2, half_cap // 2, 2, part), (0, 1, 3, 2, 4)
    ).reshape(exp_dev, capacity, part)

    over_slots = (((0,), (0,)), ((), ()))
    back = jnp.concatenate(
        [
            lax.dot_general(place[i], summed[i], over_slots, preferred_element_type=f32).astype(bf16)
            for i in range(exp_dev)
        ],
        axis=1,
    )
    returned = lax.all_to_all(
        back.reshape(groups, peer, exp_dev * part), "z", split_axis=0, concat_axis=0, tiled=True
    ).reshape(groups * peer, exp_dev * part)
    pick = pick.reshape(exp_dev, groups * peer, tok_dev)
    grad_tokens = lax.dot_general(
        pick[0], returned[:, :part], over_slots, preferred_element_type=f32
    )
    grad_tokens = grad_tokens + lax.dot_general(
        pick[1], returned[:, part:], over_slots, preferred_element_type=f32
    )

    def scaled(rows):
        return (weight * rows.astype(f32)).astype(bf16)

    give = jnp.concatenate([theirs[0], scaled(theirs[1]), activation, d_gate, d_up], axis=1)
    got = lax.ppermute(give, "q", swap)
    keep = jnp.concatenate([mine[0], scaled(mine[1]), activation, d_gate, d_up], axis=1)
    both = jnp.concatenate([keep, got], axis=0)
    width = mine.shape[2]
    hidden = wg.shape[1]
    rows_in = both[:, :width]
    scaled_out = both[:, width : 2 * width]
    activation = both[:, 2 * width : 2 * width + hidden]
    d_gate = both[:, 2 * width + hidden : 2 * width + 2 * hidden]
    d_up = both[:, 2 * width + 2 * hidden :]
    grad_down = lax.dot_general(activation, scaled_out, over_slots, preferred_element_type=f32)
    grad_gate = lax.dot_general(rows_in, d_gate, over_slots, preferred_element_type=f32)
    grad_up = lax.dot_general(rows_in, d_up, over_slots, preferred_element_type=f32)
    return (
        grad_tokens.astype(bf16),
        grad_gate.astype(bf16)[None],
        grad_up.astype(bf16)[None],
        grad_down.astype(bf16)[None],
        grad_combine,
    )


def solution(mesh):
    groups, lanes = mesh.devices.shape
    split = Mesh(
        mesh.devices.reshape(groups, 2, 2, lanes // 8, 2), ("z", "p", "q", "x", "c")
    )
    mp = ("p", "q", "x", "c")
    placed = (
        P("z", mp),
        P("z", mp),
        P("z", None, mp),
        P("z", None, mp),
        P("z", mp, None),
        P("z", None),
        P(),
    )
    return jax.shard_map(
        local,
        mesh=split,
        in_specs=placed,
        out_specs=(
            P("z", mp),
            P("z", None, mp),
            P("z", None, mp),
            P("z", mp, None),
            P("z", None),
        ),
        check_vma=False,
    )
```

time: 154 us -> 157 us (1.019)
  blocking collectives: 18.4 us -> 0 us
  starting transfers between devices: 55 us -> 63.9 us
  waiting for transfers between devices: 58.6 us -> 64.2 us
  matrix products: 7.29 us -> 11.1 us
  local copies, waits for them, and re-layouts: 6.85 us -> 10.4 us
    all_gather x1 -> x0, blocking collectives: 18.4 us -> none  [local(): gathered = lax.all_gather(compact, ('x', 'c'), axis=0)]
    all_to_all x2 -> x3, waiting for transfers between devices: 25.2 us -> 36.6 us  [the longest x1 20.6 us: local(): lax.all_to_all(back.reshape(groups, peer, exp_dev * part), 'z', split_axi...]
    all_to_all x2 -> x3, starting transfers between devices: 10.4 us -> 18.7 us  [the longest x1 10.2 us: local(): lax.all_to_all(spreadout.reshape(2 * spread, half_cap, 4 * part), ('q', '...]
    ppermute x3 -> x4, starting transfers between devices: 9.23 us -> 15.2 us  [the longest x1 6.58 us: local(): wg_far = lax.ppermute(wg, 'q', swap)]
    ppermute x3 -> x4, waiting for transfers between devices: 5.63 us -> 0.01 us  [the longest x1 0.01 us: local(): wd_far = lax.ppermute(wd, 'q', swap)]
    all_to_all x1, starting transfers between devices: 34.7 us -> 29.3 us  [local(): lax.all_to_all(send.reshape(experts, peer, 2 * part), ('p', 'z'), split_a...]
    dot_general x9 -> x16, matrix products: 3.12 us -> 6.84 us  [the longest x1 1.36 us: local(): back_grad = lax.dot_general(mine[1], wd, across, preferred_element_type=f32)]
    all_to_all x2 -> x0, other arithmetic: 2.16 us -> none  [local(): lax.all_to_all(back.reshape(4 * groups, peer * part), ('p', 'q', 'z'), sp...]
  transfers between devices with their start and end apart: 7 -> 9, of which waited for: 4 -> 4; matrix products, arithmetic and copies ran while one was open for 4% -> 6% of each run, Pallas kernels for 0% -> 0%
where the time goes in v2:
time: 157 us
  waiting for transfers between devices  64.2 us (41%)
  starting transfers between devices  63.9 us (41%)
  matrix products  11.1 us (7%)
  local copies, waits for them, and re-layouts  10.4 us (7%)
  other arithmetic  5.83 us (4%)
    all_to_all x1, starting transfers between devices, local(): lax.all_to_all(send.reshape(experts, peer, 2 * part), ('p', 'z'), split_a...  29.3 us
    all_to_all x1, waiting for transfers between devices, local(): lax.all_to_all(send.reshape(experts, peer, 2 * part), ('p', 'z'), split_a...  27.6 us
    all_to_all x1, waiting for transfers between devices, local(): lax.all_to_all(back.reshape(groups, peer, exp_dev * part), 'z', split_axi...  20.6 us
    all_to_all x1, starting transfers between devices, local(): lax.all_to_all(spreadout.reshape(2 * spread, half_cap, 4 * part), ('q', '...  10.2 us
    all_to_all x1, waiting for transfers between devices, local(): lax.all_to_all(spreadout.reshape(2 * spread, half_cap, 4 * part), ('q', '...  9.8 us
    ppermute x1, starting transfers between devices, local(): wg_far = lax.ppermute(wg, 'q', swap)  6.58 us
    all_to_all x1, waiting for transfers between devices, local(): lax.all_to_all(piece, ('p', 'q', 'x', 'c'), split_axis=0, concat_axis=0,...  6.15 us
    all_to_all x1, starting transfers between devices, local(): lax.all_to_all(piece, ('p', 'q', 'x', 'c'), split_axis=0, concat_axis=0,...  4.74 us
  transfers between devices with their start and end apart: 9, of which 4 were waited for; matrix products, arithmetic and copies ran while one was open for 6% of the time, Pallas kernels for 0%

profile of v2, /device:TPU:1, one launch (start us, length us, event | category | flops | bytes accessed | tf_op | source)
XLA Modules:
  0.0 156.6 jit_solution(14631409441323730139)
XLA Ops:
  0.7 0.7 pad_maximum_fusion.5
  1.4 0.7 collective-permute-start
  2.1 6.6 %collective-permute-start.1 = (bf16[1024,256]{1,0:T(8,128)(2,1)}, bf16[1024,256]{1,0:T(8,128)(2,1)S(1)}, u32[]{:S(2)}, u32[]{:S(2)}) collective-permute-start(bf16[1024,256]{1,0:T(8,128)(2,1)} %bitcast.108), channel_id=1, source_target_pairs={{0,8},{8,0},{1,9},{9,1},{2,10},{10,2},{3,11},{11,3},{4,12},{12,4},... | collective-permute-start | bytes 1572872 | tf_op jit(solution)/shard_map/ppermute | solution.py:28
  8.7 1.9 %collective-permute-start.2 = (bf16[1024,256]{1,0:T(8,128)(2,1)}, bf16[1024,256]{1,0:T(8,128)(2,1)S(1)}, u32[]{:S(2)}, u32[]{:S(2)}) collective-permute-start(bf16[1024,256]{1,0:T(8,128)(2,1)} %bitcast.109), channel_id=1, source_target_pairs={{0,8},{8,0},{1,9},{9,1},{2,10},{10,2},{3,11},{11,3},{4,12},{12,4},... | collective-permute-start | bytes 1572872 | tf_op jit(solution)/shard_map/ppermute | solution.py:29
  10.6 3.4 %collective-permute-start.3 = (bf16[256,1024]{1,0:T(8,128)(2,1)}, bf16[256,1024]{1,0:T(8,128)(2,1)S(1)}, u32[]{:S(2)}, u32[]{:S(2)}) collective-permute-start(bf16[256,1024]{1,0:T(8,128)(2,1)} %bitcast.114), channel_id=1, source_target_pairs={{0,8},{8,0},{1,9},{9,1},{2,10},{10,2},{3,11},{11,3},{4,12},{12,4},... | collective-permute-start | bytes 1572872 | tf_op jit(solution)/shard_map/ppermute | solution.py:30
  14.5 1.2 select_reduce_fusion
  15.8 0.9 fusion.5
  16.7 29.3 %all-to-all-start = ((bf16[64,8,128]{2,1,0:T(8,128)(2,1)}), bf16[64,8,128]{2,1,0:T(8,128)(2,1)S(1)}, u32[]{:S(2)}, u32[]{:S(2)}) async-start(bf16[64,8,128]{2,1,0:T(8,128)(2,1)} %fusion.5), calls=%async_computation | async-start | bytes 262144 | tf_op jit(solution)/shard_map/all_to_all | solution.py:49
  46.1 0.2 convert_reduce_fusion.1
  46.5 27.6 %all-to-all-done = bf16[64,8,128]{2,1,0:T(8,128)(2,1)S(1)} async-done(((bf16[64,8,128]{2,1,0:T(8,128)(2,1)}), bf16[64,8,128]{2,1,0:T(8,128)(2,1)S(1)}, u32[]{:S(2)}, u32[]{:S(2)}) %all-to-all-start) | async-done | bytes 131104 | tf_op jit(solution)/shard_map/all_to_all | solution.py:49
  74.1 0.2 convolution_convert_fusion.7
  74.3 0.2 convolution_convert_fusion.6
  74.7 0.8 broadcast_in_dim.70
  75.6 10.2 %all-to-all-start.1 = ((bf16[16,64,256]{2,1,0:T(8,128)(2,1)}), bf16[16,64,256]{2,1,0:T(8,128)(2,1)S(1)}, u32[]{:S(2)}, u32[]{:S(2)}) async-start(bf16[16,64,256]{2,1,0:T(8,128)(2,1)} %bitcast.15), calls=%async_computation.1 | async-start | bytes 1048576 | tf_op jit(solution)/shard_map/all_to_all | solution.py:71
  85.8 9.8 %all-to-all-done.1 = bf16[16,64,256]{2,1,0:T(8,128)(2,1)S(1)} async-done(((bf16[16,64,256]{2,1,0:T(8,128)(2,1)}), bf16[16,64,256]{2,1,0:T(8,128)(2,1)S(1)}, u32[]{:S(2)}, u32[]{:S(2)}) %all-to-all-start.1) | async-done | bytes 524320 | tf_op jit(solution)/shard_map/all_to_all | solution.py:71
  95.6 0.4 reshape.202
  96.0 0.7 constant_dynamic-slice_fusion.2
  97.0 0.2 copy.48
  97.1 0.2 squeeze.77
  97.3 0.6 copy-done.1
  98.0 0.8 fusion.45
  98.8 0.2 copy-done.2
  99.0 0.2 fusion.41
  99.4 0.8 fusion.50
  100.1 0.2 copy.49
  100.3 0.2 squeeze.78
  100.5 0.7 constant_dynamic-update-slice_fusion.7
  101.2 0.2 copy.45
  101.4 0.2 squeeze.74
  101.6 0.7 copy-done.3
  102.3 0.2 copy.47
  102.5 0.2 squeeze.76
  102.7 1.4 fusion.38
  104.1 0.2 convolution_add_fusion.2
  104.3 0.8 fusion.9
  105.1 0.8 constant_dynamic-update-slice_fusion.6
  105.9 0.2 copy-done.5
  106.1 0.4 multiply_reduce_fusion
  106.5 0.7 constant_dynamic-update-slice_fusion.5
  107.2 0.7 constant_dynamic-update-slice_fusion.4
  107.9 0.3 fusion.54
  108.2 0.3 fusion.43
  108.4 0.3 fusion.3
  108.7 0.3 broadcast_select_fusion.1
  109.0 0.2 select_n.121
  109.2 0.3 copy.62
  109.5 0.1 select_n.123
  109.6 0.2 select_n.125
  109.8 0.3 copy.61
  110.4 0.8 pad_maximum_fusion
  111.1 4.7 %all-to-all-start.2 = ((bf16[32,40,128]{2,1,0:T(8,128)(2,1)}), bf16[32,40,128]{2,1,0:T(8,128)(2,1)S(1)}, u32[]{:S(2)}, u32[]{:S(2)}) async-start(bf16[32,40,128]{2,1,0:T(8,128)(2,1)} %pad_maximum_fusion), calls=%async_computation.2 | async-start | bytes 655360 | tf_op jit(solution)/shard_map/all_to_all | solution.py:120
  116.0 3.3 %collective-permute-start.4 = (bf16[64,2816]{1,0:T(8,128)(2,1)S(1)}, bf16[64,2816]{1,0:T(8,128)(2,1)S(1)}, u32[]{:S(2)}, u32[]{:S(2)}) collective-permute-start(bf16[64,2816]{1,0:T(8,128)(2,1)S(1)} %copy-done.7), channel_id=1, source_target_pairs={{0,8},{8,0},{1,9},{9,1},{2,10},{10,2},{3,11},{11,3},{4,12},{12,4},... | collective-permute-start | bytes 1081352 | tf_op jit(solution)/shard_map/ppermute | solution.py:155
  119.4 6.1 %all-to-all-done.2 = bf16[32,40,128]{2,1,0:T(8,128)(2,1)S(1)} async-done(((bf16[32,40,128]{2,1,0:T(8,128)(2,1)}), bf16[32,40,128]{2,1,0:T(8,128)(2,1)S(1)}, u32[]{:S(2)}, u32[]{:S(2)}) %all-to-all-start.2) | async-done | bytes 327712 | tf_op jit(solution)/shard_map/all_to_all | solution.py:120
  125.8 0.2 convolution_convert_fusion.5
  126.0 0.2 convolution_convert_fusion.4
  126.2 0.7 copy.54
  126.9 3.8 %all-to-all-start.3 = ((bf16[32,8,128]{2,1,0:T(8,128)(2,1)}), bf16[32,8,128]{2,1,0:T(8,128)(2,1)S(1)}, u32[]{:S(2)}, u32[]{:S(2)}) async-start(bf16[32,8,128]{2,1,0:T(8,128)(2,1)} %bitcast.30), calls=%async_computation.3 | async-start | bytes 131072 | tf_op jit(solution)/shard_map/all_to_all | solution.py:140
  130.9 0.6 reshape.207
  131.5 1.1 fusion.2
  132.6 1.1 fusion.1
  133.8 1.1 fusion
  134.9 20.6 %all-to-all-done.3 = bf16[32,8,128]{2,1,0:T(8,128)(2,1)S(1)} async-done(((bf16[32,8,128]{2,1,0:T(8,128)(2,1)}), bf16[32,8,128]{2,1,0:T(8,128)(2,1)S(1)}, u32[]{:S(2)}, u32[]{:S(2)}) %all-to-all-start.3) | async-done | bytes 65568 | tf_op jit(solution)/shard_map/all_to_all | solution.py:140
  155.5 0.2 fusion.12
  155.7 0.9 fusion.6
  (60 shorter events, 1.9 us)
Async XLA Ops:
  0.6 85.1 %copy-start = (f32[2,128]{1,0:T(2,128)S(1)}, f32[2,128]{1,0:T(2,128)}, u32[]{:S(2)}) copy-start(f32[2,128]{1,0:T(2,128)} %param.12) | copy-start | bytes 3076
  0.6 13.3 %copy-start.8 = (s32[64,128]{1,0:T(8,128)S(1)}, s32[64,128]{1,0:T(8,128)}, u32[]{:S(2)}) copy-start(s32[64,128]{1,0:T(8,128)} %param.13) | copy-start | bytes 98308
  1.4 14.4 %collective-permute-start = (bf16[128,128]{0,1:T(8,128)(2,1)S(1)}, bf16[128,128]{0,1:T(8,128)(2,1)S(1)}, u32[]{:S(2)}, u32[]{:S(2)}) collective-permute-start(bf16[128,128]{0,1:T(8,128)(2,1)S(1)} %pad_maximum_fusion.5), channel_id=1, source_target_pairs={{0,0},{8,16},{16,8},{24,24},{1,1},{9,17},{17,9},{25,25},{2,2},{10,... | collective-permute-start | bytes 98312 | tf_op jit(solution)/shard_map/ppermute | solution.py:25
  2.1 44.4 %collective-permute-start.1 = (bf16[1024,256]{1,0:T(8,128)(2,1)}, bf16[1024,256]{1,0:T(8,128)(2,1)S(1)}, u32[]{:S(2)}, u32[]{:S(2)}) collective-permute-start(bf16[1024,256]{1,0:T(8,128)(2,1)} %bitcast.108), channel_id=1, source_target_pairs={{0,8},{8,0},{1,9},{9,1},{2,10},{10,2},{3,11},{11,3},{4,12},{12,4},... | collective-permute-start | bytes 1572872 | tf_op jit(solution)/shard_map/ppermute | solution.py:28
  8.7 37.8 %collective-permute-start.2 = (bf16[1024,256]{1,0:T(8,128)(2,1)}, bf16[1024,256]{1,0:T(8,128)(2,1)S(1)}, u32[]{:S(2)}, u32[]{:S(2)}) collective-permute-start(bf16[1024,256]{1,0:T(8,128)(2,1)} %bitcast.109), channel_id=1, source_target_pairs={{0,8},{8,0},{1,9},{9,1},{2,10},{10,2},{3,11},{11,3},{4,12},{12,4},... | collective-permute-start | bytes 1572872 | tf_op jit(solution)/shard_map/ppermute | solution.py:29
  10.6 35.9 %collective-permute-start.3 = (bf16[256,1024]{1,0:T(8,128)(2,1)}, bf16[256,1024]{1,0:T(8,128)(2,1)S(1)}, u32[]{:S(2)}, u32[]{:S(2)}) collective-permute-start(bf16[256,1024]{1,0:T(8,128)(2,1)} %bitcast.114), channel_id=1, source_target_pairs={{0,8},{8,0},{1,9},{9,1},{2,10},{10,2},{3,11},{11,3},{4,12},{12,4},... | collective-permute-start | bytes 1572872 | tf_op jit(solution)/shard_map/ppermute | solution.py:30
  16.7 57.4 %all-to-all-start = ((bf16[64,8,128]{2,1,0:T(8,128)(2,1)}), bf16[64,8,128]{2,1,0:T(8,128)(2,1)S(1)}, u32[]{:S(2)}, u32[]{:S(2)}) async-start(bf16[64,8,128]{2,1,0:T(8,128)(2,1)} %fusion.5), calls=%async_computation | async-start | bytes 262144 | tf_op jit(solution)/shard_map/all_to_all | solution.py:49
  46.5 29.1 %copy-start.4 = (bf16[256,1024]{1,0:T(8,128)(2,1)}, bf16[256,1024]{1,0:T(8,128)(2,1)S(1)}, u32[]{:S(2)}) copy-start(bf16[256,1024]{1,0:T(8,128)(2,1)S(1)} %collective-permute-done.3) | copy-start | bytes 1572868
  75.6 20.0 %all-to-all-start.1 = ((bf16[16,64,256]{2,1,0:T(8,128)(2,1)}), bf16[16,64,256]{2,1,0:T(8,128)(2,1)S(1)}, u32[]{:S(2)}, u32[]{:S(2)}) async-start(bf16[16,64,256]{2,1,0:T(8,128)(2,1)} %bitcast.15), calls=%async_computation.1 | async-start | bytes 1048576 | tf_op jit(solution)/shard_map/all_to_all | solution.py:71
  96.9 1.0 copy-start.1
  98.0 1.0 copy-start.2
  101.4 1.0 copy-start.3
  102.7 1.4 copy-start.6
  105.1 1.0 copy-start.5
  111.1 4.9 %copy-start.7 = (bf16[64,2816]{1,0:T(8,128)(2,1)S(1)}, bf16[64,2816]{1,0:T(8,128)(2,1)}, u32[]{:S(2)}) copy-start(bf16[64,2816]{1,0:T(8,128)(2,1)} %get-tuple-element.13) | copy-start | bytes 1081348
  111.1 14.4 %all-to-all-start.2 = ((bf16[32,40,128]{2,1,0:T(8,128)(2,1)}), bf16[32,40,128]{2,1,0:T(8,128)(2,1)S(1)}, u32[]{:S(2)}, u32[]{:S(2)}) async-start(bf16[32,40,128]{2,1,0:T(8,128)(2,1)} %pad_maximum_fusion), calls=%async_computation.2 | async-start | bytes 655360 | tf_op jit(solution)/shard_map/all_to_all | solution.py:120
  116.0 15.5 %collective-permute-start.4 = (bf16[64,2816]{1,0:T(8,128)(2,1)S(1)}, bf16[64,2816]{1,0:T(8,128)(2,1)S(1)}, u32[]{:S(2)}, u32[]{:S(2)}) collective-permute-start(bf16[64,2816]{1,0:T(8,128)(2,1)S(1)} %copy-done.7), channel_id=1, source_target_pairs={{0,8},{8,0},{1,9},{9,1},{2,10},{10,2},{3,11},{11,3},{4,12},{12,4},... | collective-permute-start | bytes 1081352 | tf_op jit(solution)/shard_map/ppermute | solution.py:155
  126.9 28.6 %all-to-all-start.3 = ((bf16[32,8,128]{2,1,0:T(8,128)(2,1)}), bf16[32,8,128]{2,1,0:T(8,128)(2,1)S(1)}, u32[]{:S(2)}, u32[]{:S(2)}) async-start(bf16[32,8,128]{2,1,0:T(8,128)(2,1)} %bitcast.30), calls=%async_computation.3 | async-start | bytes 131072 | tf_op jit(solution)/shard_map/all_to_all | solution.py:140

commit v3 on v2

--- a/solution.py
+++ b/solution.py
@@ -1,8 +1,108 @@
 import jax
 import jax.numpy as jnp
 from jax import lax
+from jax.experimental import pallas as pl
+from jax.experimental.pallas import tpu as pltpu
 from jax.sharding import Mesh
 from jax.sharding import PartitionSpec as P
+
+
+def middle(
+    q_ref,
+    weight_ref,
+    rows_ref,
+    wg_far,
+    wu_far,
+    wd_far,
+    out_ref,
+    keep_ref,
+    give_ref,
+    nat_ref,
+    wg_ref,
+    wu_ref,
+    wd_ref,
+    sem,
+):
+    loads = [
+        pltpu.make_async_copy(far, near, sem.at[i])
+        for i, (far, near) in enumerate(((wg_far, wg_ref), (wu_far, wu_ref), (wd_far, wd_ref)))
+    ]
+    for load in loads:
+        load.start()
+    bf16 = jnp.bfloat16
+    f32 = jnp.float32
+    q = q_ref[0]
+    spread = rows_ref.shape[0] // 2
+    slots = rows_ref.shape[1]
+    width = wg_ref.shape[1]
+    hidden = wg_ref.shape[2]
+    weight = weight_ref[...]
+    low = lax.broadcasted_iota(jnp.int32, (slots, 128), 1) < 64
+
+    def halves(first, second):
+        return (
+            jnp.where(low[: first.shape[0]], first, pltpu.roll(second, 64, 1)),
+            jnp.where(low[: first.shape[0]], pltpu.roll(first, 64, 1), second),
+        )
+
+    for side in range(2):
+        for kind in range(2):
+            for i in range(spread // 2):
+                lanes = pl.ds(kind * 128, 128)
+                first = rows_ref[side * spread + 2 * i, :, lanes].astype(f32)
+                second = rows_ref[side * spread + 2 * i + 1, :, lanes].astype(f32)
+                for a, part in enumerate(halves(first, second)):
+                    at = kind * width + a * (width // 2) + i * 128
+                    nat_ref[side, :, pl.ds(at, 128)] = part.astype(bf16)
+
+    def over(side, kind):
+        return nat_ref[side, :, pl.ds(kind * width, width)]
+
+    across = (((1,), (1,)), ((), ()))
+    loads[0].wait()
+    gate_pre = jnp.dot(over(0, 0), wg_ref[0], preferred_element_type=f32)
+    gate_pre = gate_pre + jnp.dot(over(1, 0), wg_ref[1], preferred_element_type=f32)
+    loads[1].wait()
+    up_pre = jnp.dot(over(0, 0), wu_ref[0], preferred_element_type=f32)
+    up_pre = up_pre + jnp.dot(over(1, 0), wu_ref[1], preferred_element_type=f32)
+    loads[2].wait()
+    back_grad = lax.dot_general(over(0, 1), wd_ref[0], across, preferred_element_type=f32)
+    back_grad = back_grad + lax.dot_general(
+        over(1, 1), wd_ref[1], across, preferred_element_type=f32
+    )
+    sig = 1.0 / (1.0 + jnp.exp(-gate_pre))
+    activation = (gate_pre * sig * up_pre).astype(bf16)
+    term = jnp.sum(activation.astype(f32) * back_grad, axis=1, keepdims=True)
+    d_act = weight * back_grad
+    d_gate = (d_act * up_pre * sig * (1.0 + gate_pre * (1.0 - sig))).astype(bf16)
+    d_up = (d_act * gate_pre * sig).astype(bf16)
+
+    lane = lax.broadcasted_iota(jnp.int32, (slots, 128), 1)
+    slot = lax.broadcasted_iota(jnp.int32, (slots, 128), 0)
+    line = jnp.sum(jnp.where((lane & 63) == slot, term, 0.0), axis=0, keepdims=True)
+    rounded = line.astype(bf16).astype(f32)
+    line = jnp.where(low[:1], rounded, line - rounded)
+    extra = jnp.where(slot[:16] == 0, line, 0.0).astype(bf16)
+    half = slots // 2
+    for side in range(2):
+        piece = lax.dot_general(d_gate, wg_ref[side], across, preferred_element_type=f32)
+        piece = piece + lax.dot_general(d_up, wu_ref[side], across, preferred_element_type=f32)
+        for a in range(2):
+            for i in range(spread // 2):
+                at = a * (width // 2) + i * 128
+                top, bottom = piece[:half, at : at + 128], piece[half:, at : at + 128]
+                for j, part in enumerate(halves(top, bottom)):
+                    to = (side * 2 + a) * spread + 2 * i + j
+                    out_ref[to, pl.ds(0, half), :] = part.astype(bf16)
+                    out_ref[to, pl.ds(half, 16), :] = extra
+
+    for ref, side in ((keep_ref, q), (give_ref, 1 - q)):
+        ref[:, pl.ds(0, width)] = nat_ref[side, :, pl.ds(0, width)]
+        rows_out = nat_ref[side, :, pl.ds(width, width)].astype(f32)
+        ref[:, pl.ds(width, width)] = (weight * rows_out).astype(bf16)
+        ref[:, pl.ds(2 * width, hidden)] = activation
+        ref[:, pl.ds(2 * width + hidden, hidden)] = d_gate
+        ref[:, pl.ds(2 * width + 2 * hidden, hidden)] = d_up
 
 
 def local(x_tokens, cotangent, w_gate, w_up, w_down, combine, indices):
@@ -24,10 +124,9 @@
     table = jnp.concatenate([x_tokens, cotangent], axis=1)
     table = lax.ppermute(table, ("p", "q"), [(0, 0), (1, 2), (2, 1), (3, 3)])
 
-    swap = [(0, 1), (1, 0)]
-    wg_far = lax.ppermute(wg, "q", swap)
-    wu_far = lax.ppermute(wu, "q", swap)
-    wd_far = lax.ppermute(wd, "q", swap)
+    wg_both = lax.all_gather(wg, "q", axis=0)
+    wu_both = lax.all_gather(wu, "q", axis=0)
+    wd_both = lax.all_gather(wd, "q", axis=0)
 
     slots = jnp.arange(capacity, dtype=jnp.int32)
     places = jnp.arange(peer, dtype=jnp.int32)
@@ -59,7 +158,6 @@
     place = jnp.where(own_block[:, :, None] == cell_block[None, None, :], own_want[:, None, :], -1)
     place = (place == slots[None, :, None]).astype(bf16)
     own_place = lax.dynamic_index_in_dim(place, p, 0, keepdims=False)
-    recv, wg_far, wu_far, wd_far = lax.optimization_barrier((recv, wg_far, wu_far, wd_far))
     recv = recv.reshape(2, groups * peer, 2 * part)
     taken = [jnp.dot(own_place, recv[i], preferred_element_type=f32).astype(bf16) for i in range(2)]
     compact = jnp.concatenate(
@@ -74,51 +172,36 @@
         split_axis=0,
         concat_axis=0,
         tiled=True,
-    ).reshape(2, spread, half_cap, 2, 2, part)
-
-    def natural(block):
-        return jnp.transpose(block, (2, 1, 3, 0, 4)).reshape(2, half_cap, 2 * spread * part)
-
-    mine = natural(lax.dynamic_index_in_dim(gathered, q, 0, keepdims=False))
-    theirs = natural(lax.dynamic_index_in_dim(gathered, 1 - q, 0, keepdims=False))
-
-    def rows_by(first, second):
-        return jnp.dot(mine[0], first, preferred_element_type=f32) + jnp.dot(
-            theirs[0], second, preferred_element_type=f32
-        )
-
-    across = (((1,), (1,)), ((), ()))
-    gate_pre = rows_by(wg, wg_far)
-    up_pre = rows_by(wu, wu_far)
-    back_grad = lax.dot_general(mine[1], wd, across, preferred_element_type=f32)
-    back_grad = back_grad + lax.dot_general(theirs[1], wd_far, across, preferred_element_type=f32)
-
+    )
+    hidden = wg.shape[1]
+    width = wg.shape[0]
     weight = lax.dynamic_slice(combine, (p, q * half_cap), (1, half_cap)).reshape(half_cap, 1)
-    sig = jax.nn.sigmoid(gate_pre)
-    activation = (gate_pre * sig * up_pre).astype(bf16)
-    term = jnp.sum(activation.astype(f32) * back_grad, axis=1)
-    d_act = weight * back_grad
-    d_gate = (d_act * up_pre * sig * (1.0 + gate_pre * (1.0 - sig))).astype(bf16)
-    d_up = (d_act * gate_pre * sig).astype(bf16)
-
-    def pieces_of(first, second):
-        piece = lax.dot_general(d_gate, first, across, preferred_element_type=f32)
-        piece = piece + lax.dot_general(d_up, second, across, preferred_element_type=f32)
-        piece = piece.astype(bf16).reshape(2, half_cap // 2, 2, spread, part)
-        piece = jnp.transpose(piece, (2, 3, 1, 0, 4))
-        return piece.reshape(2 * spread, half_cap // 2, 2 * part)
-
-    near = pieces_of(wg, wu)
-    far = pieces_of(wg_far, wu_far)
-    piece = jnp.concatenate([jnp.where(q == 0, near, far), jnp.where(q == 0, far, near)], axis=0)
-    high = lax.reduce_precision(term, 8, 7)
-    extra = jnp.concatenate([high.astype(bf16), (term - high).astype(bf16)]).reshape(1, 2 * half_cap)
-    extra = jnp.pad(extra, ((0, 7), (0, 0)))
-    piece = jnp.concatenate(
-        [piece, jnp.broadcast_to(extra[None], (4 * spread,) + extra.shape)], axis=1
-    )
+    vmem = pl.BlockSpec(memory_space=pltpu.VMEM)
+    held = jax.ShapeDtypeStruct((half_cap, 2 * width + 3 * hidden), bf16)
+    piece, keep, give = pl.pallas_call(
+        middle,
+        out_shape=(
+            jax.ShapeDtypeStruct((4 * spread, half_cap // 2 + 16, 2 * part), bf16),
+            held,
+            held,
+        ),
+        in_specs=[pl.BlockSpec(memory_space=pltpu.SMEM)] + [vmem] * 2
+        + [pl.BlockSpec(memory_space=pltpu.HBM)] * 3,
+        out_specs=(vmem, vmem, vmem),
+        scratch_shapes=[
+            pltpu.VMEM((2, half_cap, 2 * width), bf16),
+            pltpu.VMEM(wg_both.shape, bf16),
+            pltpu.VMEM(wu_both.shape, bf16),
+            pltpu.VMEM(wd_both.shape, bf16),
+            pltpu.SemaphoreType.DMA((3,)),
+        ],
+        compiler_params=pltpu.CompilerParams(vmem_limit_bytes=52 * 1024 * 1024),
+        cost_estimate=pl.CostEstimate(
+            flops=20 * half_cap * width * hidden, bytes_accessed=5 << 20, transcendentals=0
+        ),
+    )(q.reshape(1), weight, gathered, wg_both, wu_both, wd_both)
     pieces = lax.all_to_all(piece, ("p", "q", "x", "c"), split_axis=0, concat_axis=0, tiled=True)
-    pieces = pieces.reshape(2, 2, spread, half_cap // 2 + 8, 2 * part)
+    pieces = pieces.reshape(2, 2, spread, half_cap // 2 + 16, 2 * part)
     summed = jnp.sum(pieces.astype(f32), axis=2)
     term_sum = summed[:, :, half_cap // 2]
     grad_combine = (term_sum[:, :, :half_cap] + term_sum[:, :, half_cap:]).reshape(
@@ -148,15 +231,10 @@
         pick[1], returned[:, part:], over_slots, preferred_element_type=f32
     )
 
-    def scaled(rows):
-        return (weight * rows.astype(f32)).astype(bf16)
-
-    give = jnp.concatenate([theirs[0], scaled(theirs[1]), activation, d_gate, d_up], axis=1)
-    got = lax.ppermute(give, "q", swap)
-    keep = jnp.concatenate([mine[0], scaled(mine[1]), activation, d_gate, d_up], axis=1)
+    give, _ = lax.optimization_barrier((give, back))
+    got = lax.all_gather(give, "q", axis=0)
+    got = lax.dynamic_index_in_dim(got, 1 - q, 0, keepdims=False)
     both = jnp.concatenate([keep, got], axis=0)
-    width = mine.shape[2]
-    hidden = wg.shape[1]
     rows_in = both[:, :width]
     scaled_out = both[:, width : 2 * width]
     activation = both[:, 2 * width : 2 * width + hidden]

time: 157 us -> 232 us (1.48)
  waiting for transfers between devices: 64.2 us -> 116 us
  between operations: 1.2 us -> 14.1 us
  starting transfers between devices: 63.9 us -> 74.8 us
  blocking collectives: 0 us -> 9.97 us
  local copies, waits for them, and re-layouts: 10.4 us -> 3.14 us
  matrix products: 11.1 us -> 6.15 us
  Pallas kernels: 0 us -> 4.7 us
  other arithmetic: 5.83 us -> 2.1 us
    all_gather x0 -> x3, waiting for transfers between devices: none -> 66.8 us  [the longest x1 45.3 us: local(): wd_both = lax.all_gather(wd, 'q', axis=0)]
    all_to_all x1, starting transfers between devices: 3.84 us -> 22.6 us  [local(): lax.all_to_all(back.reshape(groups, peer, exp_dev * part), 'z', split_axi...]
    ppermute x4 -> x0, starting transfers between devices: 15.2 us -> none  [the longest x1 6.58 us: local(): wg_far = lax.ppermute(wg, 'q', swap)]
    all_to_all x1, waiting for transfers between devices: 20.6 us -> 10.4 us  [local(): lax.all_to_all(back.reshape(groups, peer, exp_dev * part), 'z', split_axi...]
    all_gather x0 -> x1, blocking collectives: none -> 9.97 us  [local(): got = lax.all_gather(give, 'q', axis=0)]
    all_to_all x1, waiting for transfers between devices: 9.8 us -> 0.01 us  [local(): lax.all_to_all(spreadout.reshape(2 * spread, half_cap, 4 * part), ('q', '...]
    all_to_all x1, starting transfers between devices: 29.3 us -> 34.6 us  [local(): lax.all_to_all(send.reshape(experts, peer, 2 * part), ('p', 'z'), split_a...]
    dot_general x10 -> x0, matrix products: 4.95 us -> none  [the longest x1 1.36 us: local(): back_grad = lax.dot_general(mine[1], wd, across, preferred_element_type=f32)]
  transfers between devices with their start and end apart: 9 -> 8, of which waited for: 4 -> 5; matrix products, arithmetic and copies ran while one was open for 6% -> 4% of each run, Pallas kernels for 0% -> 0%
where the time goes in v3:
time: 232 us; the launch traced here: 231 us
  waiting for transfers between devices  116 us (50%)
  starting transfers between devices  74.8 us (32%)
  between operations  14.1 us (6%)
  blocking collectives  9.97 us (4%)
  matrix products  6.15 us (3%)
  Pallas kernels  4.7 us (2%)
  local copies, waits for them, and re-layouts  3.14 us (1%)
    all_gather x1, waiting for transfers between devices, local(): wd_both = lax.all_gather(wd, 'q', axis=0)  45.3 us
    all_to_all x1, starting transfers between devices, local(): lax.all_to_all(send.reshape(experts, peer, 2 * part), ('p', 'z'), split_a...  34.6 us
    all_to_all x1, waiting for transfers between devices, local(): lax.all_to_all(send.reshape(experts, peer, 2 * part), ('p', 'z'), split_a...  27.7 us
    all_to_all x1, starting transfers between devices, local(): lax.all_to_all(back.reshape(groups, peer, exp_dev * part), 'z', split_axi...  22.6 us
    all_gather x1, waiting for transfers between devices, local(): wu_both = lax.all_gather(wu, 'q', axis=0)  21.5 us
    all_to_all x1, waiting for transfers between devices, local(): lax.all_to_all(back.reshape(groups, peer, exp_dev * part), 'z', split_axi...  10.4 us
    all_to_all x1, waiting for transfers between devices, local(): lax.all_to_all(piece, ('p', 'q', 'x', 'c'), split_axis=0, concat_axis=0,...  10 us
    all_gather x1, blocking collectives, local(): got = lax.all_gather(give, 'q', axis=0)  9.97 us
  transfers between devices with their start and end apart: 8, of which 5 were waited for; matrix products, arithmetic and copies ran while one was open for 4% of the time, Pallas kernels for 0%

profile of v3, /device:TPU:1, one launch (start us, length us, event | category | flops | bytes accessed | tf_op | source)
XLA Modules:
  0.0 231.3 jit_solution(12265499325801424927)
XLA Ops:
  7.2 0.0 copy-start
  7.2 0.0 all-gather.5.cloned.1.call-start
  7.2 0.7 all-gather.5.cloned.1.call-update
  7.9 0.0 copy-start.2
  7.9 0.0 copy-start.3
  7.9 0.0 all-gather.7.cloned.1.call-start
  8.0 0.7 all-gather.7.cloned.1.call-update
  8.7 0.0 all-gather.9.cloned.1.call-start
  8.7 0.0 copy-done.2
  8.7 0.0 copy-done.3
  8.8 0.0 copy-start.1
  8.8 0.7 collective-permute-start
  9.4 0.0 all-gather.9.cloned.1.call-update
  9.5 0.0 copy-done.1
  9.5 0.1 convert_reduce_fusion.2
  9.6 0.1 reshape.187
  9.7 0.1 copy.33
  9.8 0.1 add.95
  9.9 0.1 iota_add_fusion
  10.0 1.2 select_reduce_fusion
  11.3 0.1 sub.38
  11.4 0.0 collective-permute-done
  11.4 0.9 fusion.3
  12.3 34.6 %all-to-all-start = ((bf16[64,8,128]{2,1,0:T(8,128)(2,1)}), bf16[64,8,128]{2,1,0:T(8,128)(2,1)S(1)}, u32[]{:S(2)}, u32[]{:S(2)}) async-start(bf16[64,8,128]{2,1,0:T(8,128)(2,1)} %fusion.3), calls=%async_computation | async-start | bytes 262144 | tf_op jit(solution)/shard_map/all_to_all | solution.py:148
  46.9 0.2 convert_reduce_fusion.1
  47.2 0.1 iota_compare_fusion.1
  47.3 27.7 %all-to-all-done = bf16[64,8,128]{2,1,0:T(8,128)(2,1)S(1)} async-done(((bf16[64,8,128]{2,1,0:T(8,128)(2,1)}), bf16[64,8,128]{2,1,0:T(8,128)(2,1)S(1)}, u32[]{:S(2)}, u32[]{:S(2)}) %all-to-all-start) | async-done | bytes 131104 | tf_op jit(solution)/shard_map/all_to_all | solution.py:148
  75.0 0.2 convolution_convert_fusion.7
  75.2 0.2 convolution_convert_fusion.6
  75.5 0.1 copy.35
  75.6 0.8 broadcast_in_dim.64
  76.5 9.6 %all-to-all-start.1 = ((bf16[16,64,256]{2,1,0:T(8,128)(2,1)}), bf16[16,64,256]{2,1,0:T(8,128)(2,1)S(1)}, u32[]{:S(2)}, u32[]{:S(2)}) async-start(bf16[16,64,256]{2,1,0:T(8,128)(2,1)} %bitcast.13), calls=%async_computation.1 | async-start | bytes 1048576 | tf_op jit(solution)/shard_map/all_to_all | solution.py:169
  86.0 0.0 copy-done
  86.0 0.1 dynamic-slice_bitcast_fusion.1
  86.1 0.1 copy.36.weight_ref
  86.2 0.0 all-gather.5.cloned.1.call-done.wg_far
  86.2 21.5 %all-gather.7.cloned.1.call-done.wu_far = bf16[2,1024,256]{2,1,0:T(8,128)(2,1)} async-done(((bf16[1,1024,256]{2,1,0:T(8,128)(2,1)}), bf16[2,1024,256]{2,1,0:T(8,128)(2,1)}) %all-gather.7.cloned.1.call-update) | async-done | bytes 1048592 | tf_op jit(solution)/shard_map/all_gather | solution.py:128
  107.7 45.3 %all-gather.9.cloned.1.call-done.wd_far = bf16[2,256,1024]{2,1,0:T(8,128)(2,1)} async-done(((bf16[1,256,1024]{2,1,0:T(8,128)(2,1)}), bf16[2,256,1024]{2,1,0:T(8,128)(2,1)}) %all-gather.9.cloned.1.call-update) | async-done | bytes 1048592 | tf_op jit(solution)/shard_map/all_gather | solution.py:129
  153.0 0.0 all-to-all-done.1.rows_ref
  153.0 4.7 %shard_map.110 = (bf16[32,48,128]{2,1,0:T(8,128)(2,1)}, bf16[64,2816]{1,0:T(8,128)(2,1)S(1)}, bf16[64,2816]{1,0:T(8,128)(2,1)S(1)}) custom-call(s32[1]{0:T(128)} %bitcast.6.q_ref, f32[64,1]{1,0:T(8,128)S(1)} %copy.36.weight_ref, bf16[16,64,256]{2,1,0:T(8,128)(2,1)S(1)} %all-to-all-done.1.rows_ref, bf16[2,1024,256]{2,1,0:T(8,128)(2,1)} %all-gather.5.cloned.1.call-done.wg_far, ...), custom_call_target="tpu_custom_call" | custom-call | flops 335544320 | bytes 5242880 | tf_op jit(solution)/shard_map/pallas_call | solution.py:181
  157.7 7.2 %all-to-all-start.2 = ((bf16[32,48,128]{2,1,0:T(8,128)(2,1)}), bf16[32,48,128]{2,1,0:T(8,128)(2,1)S(1)}, u32[]{:S(2)}, u32[]{:S(2)}) async-start(bf16[32,48,128]{2,1,0:T(8,128)(2,1)} %get-tuple-element.9), calls=%async_computation.2 | async-start | bytes 786432 | tf_op jit(solution)/shard_map/all_to_all | solution.py:203
  164.9 0.1 iota_compare_fusion.2
  165.1 10.0 %all-to-all-done.2 = bf16[32,48,128]{2,1,0:T(8,128)(2,1)S(1)} async-done(((bf16[32,48,128]{2,1,0:T(8,128)(2,1)}), bf16[32,48,128]{2,1,0:T(8,128)(2,1)S(1)}, u32[]{:S(2)}, u32[]{:S(2)}) %all-to-all-start.2) | async-done | bytes 393248 | tf_op jit(solution)/shard_map/all_to_all | solution.py:203
  175.1 0.1 convert_reduce_fusion
  175.2 0.1 reshape.179
  175.4 0.2 convolution_convert_fusion.5
  175.6 0.2 convolution_convert_fusion.4
  175.8 0.7 copy.39
  176.5 22.6 %all-to-all-start.3 = ((bf16[32,8,128]{2,1,0:T(8,128)(2,1)}), bf16[32,8,128]{2,1,0:T(8,128)(2,1)S(1)}, u32[]{:S(2)}, u32[]{:S(2)}) async-start(bf16[32,8,128]{2,1,0:T(8,128)(2,1)} %bitcast.19), calls=%async_computation.3 | async-start | bytes 131072 | tf_op jit(solution)/shard_map/all_to_all | solution.py:223
  199.2 0.1 slice_add_fusion
  199.3 0.6 reshape.182
  199.9 10.0 %all-gather = bf16[128,2816]{1,0:T(8,128)(2,1)S(1)} all-gather(bf16[64,2816]{1,0:T(8,128)(2,1)S(1)} %get-tuple-element.12), channel_id=2, replica_groups=mesh['z'=32,'p'=2,'q'=2,'x'=4,'c'=2] {'q'}, dimensions={0}, use_global_device_ids=true | all-gather | bytes 1081344 | tf_op jit(solution)/shard_map/all_gather | solution.py:235
  209.9 1.1 fusion.2
  211.0 1.1 fusion.1
  212.1 1.1 fusion
  213.2 10.4 %all-to-all-done.3 = bf16[32,8,128]{2,1,0:T(8,128)(2,1)S(1)} async-done(((bf16[32,8,128]{2,1,0:T(8,128)(2,1)}), bf16[32,8,128]{2,1,0:T(8,128)(2,1)S(1)}, u32[]{:S(2)}, u32[]{:S(2)}) %all-to-all-start.3) | async-done | bytes 65568 | tf_op jit(solution)/shard_map/all_to_all | solution.py:223
  223.7 0.2 fusion.8
  223.9 0.9 fusion.4
  (18 shorter events, 0.2 us)
Async XLA Ops:
  7.2 78.9 %copy-start = (f32[2,128]{1,0:T(2,128)S(1)}, f32[2,128]{1,0:T(2,128)}, u32[]{:S(2)}) copy-start(f32[2,128]{1,0:T(2,128)} %param.12) | copy-start | bytes 3076
  7.2 79.0 %all-gather.5.cloned.1.call-start = ((), (), s32[]{:S(2)}) async-start(), calls=%async_computation.4 | async-start | bytes 1572864 | tf_op jit(solution)/shard_map/all_gather | solution.py:127
  7.9 0.8 copy-start.2
  7.9 0.8 copy-start.3
  7.9 99.8 %all-gather.7.cloned.1.call-start = ((), (), s32[]{:S(2)}) async-start(), calls=%async_computation.5 | async-start | bytes 1572864 | tf_op jit(solution)/shard_map/all_gather | solution.py:128
  8.7 144.3 %all-gather.9.cloned.1.call-start = ((), (), s32[]{:S(2)}) async-start(), calls=%async_computation.6 | async-start | bytes 1572864 | tf_op jit(solution)/shard_map/all_gather | solution.py:129
  8.8 0.8 copy-start.1
  8.8 2.6 %collective-permute-start = (bf16[128,128]{0,1:T(8,128)(2,1)S(1)}, bf16[128,128]{0,1:T(8,128)(2,1)S(1)}, u32[]{:S(2)}, u32[]{:S(2)}) collective-permute-start(bf16[128,128]{0,1:T(8,128)(2,1)S(1)} %pad_maximum_fusion.4), channel_id=1, source_target_pairs={{0,0},{8,16},{16,8},{24,24},{1,1},{9,17},{17,9},{25,25},{2,2},{10,... | collective-permute-start | bytes 98312 | tf_op jit(solution)/shard_map/ppermute | solution.py:125
  12.3 62.7 %all-to-all-start = ((bf16[64,8,128]{2,1,0:T(8,128)(2,1)}), bf16[64,8,128]{2,1,0:T(8,128)(2,1)S(1)}, u32[]{:S(2)}, u32[]{:S(2)}) async-start(bf16[64,8,128]{2,1,0:T(8,128)(2,1)} %fusion.3), calls=%async_computation | async-start | bytes 262144 | tf_op jit(solution)/shard_map/all_to_all | solution.py:148
  76.5 76.5 %all-to-all-start.1 = ((bf16[16,64,256]{2,1,0:T(8,128)(2,1)}), bf16[16,64,256]{2,1,0:T(8,128)(2,1)S(1)}, u32[]{:S(2)}, u32[]{:S(2)}) async-start(bf16[16,64,256]{2,1,0:T(8,128)(2,1)} %bitcast.13), calls=%async_computation.1 | async-start | bytes 1048576 | tf_op jit(solution)/shard_map/all_to_all | solution.py:169
  157.7 17.4 %all-to-all-start.2 = ((bf16[32,48,128]{2,1,0:T(8,128)(2,1)}), bf16[32,48,128]{2,1,0:T(8,128)(2,1)S(1)}, u32[]{:S(2)}, u32[]{:S(2)}) async-start(bf16[32,48,128]{2,1,0:T(8,128)(2,1)} %get-tuple-element.9), calls=%async_computation.2 | async-start | bytes 786432 | tf_op jit(solution)/shard_map/all_to_all | solution.py:203
  176.5 47.1 %all-to-all-start.3 = ((bf16[32,8,128]{2,1,0:T(8,128)(2,1)}), bf16[32,8,128]{2,1,0:T(8,128)(2,1)S(1)}, u32[]{:S(2)}, u32[]{:S(2)}) async-start(bf16[32,8,128]{2,1,0:T(8,128)(2,1)} %bitcast.19), calls=%async_computation.3 | async-start | bytes 131072 | tf_op jit(solution)/shard_map/all_to_all | solution.py:223
Sparse Core Ops, SparseCore 0:
  10.7 50.9 all-gather.4
  64.4 43.2 all-gather.6
  110.4 42.5 all-gather.8

commit v4 on v3

--- a/solution.py
+++ b/solution.py
@@ -11,6 +11,9 @@
     q_ref,
     weight_ref,
     rows_ref,
+    wg_own,
+    wu_own,
+    wd_own,
     wg_far,
     wu_far,
     wd_far,
@@ -23,15 +26,21 @@
     wd_ref,
     sem,
 ):
-    loads = [
-        pltpu.make_async_copy(far, near, sem.at[i])
-        for i, (far, near) in enumerate(((wg_far, wg_ref), (wu_far, wu_ref), (wd_far, wd_ref)))
-    ]
-    for load in loads:
-        load.start()
+    q = q_ref[0]
+    loads = []
+    for i, (own, far, near) in enumerate(
+        ((wg_own, wg_far, wg_ref), (wu_own, wu_far, wu_ref), (wd_own, wd_far, wd_ref))
+    ):
+        loads.append(
+            (
+                pltpu.make_async_copy(own, near.at[q], sem.at[2 * i]),
+                pltpu.make_async_copy(far, near.at[1 - q], sem.at[2 * i + 1]),
+            )
+        )
+        loads[i][0].start()
+        loads[i][1].start()
     bf16 = jnp.bfloat16
     f32 = jnp.float32
-    q = q_ref[0]
     spread = rows_ref.shape[0] // 2
     slots = rows_ref.shape[1]
     width = wg_ref.shape[1]
@@ -59,13 +68,16 @@
         return nat_ref[side, :, pl.ds(kind * width, width)]
 
     across = (((1,), (1,)), ((), ()))
-    loads[0].wait()
+    loads[0][0].wait()
+    loads[0][1].wait()
     gate_pre = jnp.dot(over(0, 0), wg_ref[0], preferred_element_type=f32)
     gate_pre = gate_pre + jnp.dot(over(1, 0), wg_ref[1], preferred_element_type=f32)
-    loads[1].wait()
+    loads[1][0].wait()
+    loads[1][1].wait()
     up_pre = jnp.dot(over(0, 0), wu_ref[0], preferred_element_type=f32)
     up_pre = up_pre + jnp.dot(over(1, 0), wu_ref[1], preferred_element_type=f32)
-    loads[2].wait()
+    loads[2][0].wait()
+    loads[2][1].wait()
     back_grad = lax.dot_general(over(0, 1), wd_ref[0], across, preferred_element_type=f32)
     back_grad = back_grad + lax.dot_general(
         over(1, 1), wd_ref[1], across, preferred_element_type=f32
@@ -124,9 +136,7 @@
     table = jnp.concatenate([x_tokens, cotangent], axis=1)
     table = lax.ppermute(table, ("p", "q"), [(0, 0), (1, 2), (2, 1), (3, 3)])
 
-    wg_both = lax.all_gather(wg, "q", axis=0)
-    wu_both = lax.all_gather(wu, "q", axis=0)
-    wd_both = lax.all_gather(wd, "q", axis=0)
+    swap = [(0, 1), (1, 0)]
 
     slots = jnp.arange(capacity, dtype=jnp.int32)
     places = jnp.arange(peer, dtype=jnp.int32)
@@ -145,6 +155,9 @@
     pick = (chosen[:, :, None] == tokens[None, None, :]).astype(bf16)
     pick = pick.reshape(experts * peer, tok_dev)
     send = jnp.dot(pick, table, preferred_element_type=f32).astype(bf16)
+    send, wg_give, wu_give = lax.optimization_barrier((send, wg, wu))
+    wg_far = lax.ppermute(wg_give, "q", swap)
+    wu_far = lax.ppermute(wu_give, "q", swap)
     recv = lax.all_to_all(
         send.reshape(experts, peer, 2 * part), ("p", "z"), split_axis=0, concat_axis=0, tiled=True
     )
@@ -158,6 +171,7 @@
     place = jnp.where(own_block[:, :, None] == cell_block[None, None, :], own_want[:, None, :], -1)
     place = (place == slots[None, :, None]).astype(bf16)
     own_place = lax.dynamic_index_in_dim(place, p, 0, keepdims=False)
+    recv, wg_far, wu_far = lax.optimization_barrier((recv, wg_far, wu_far))
     recv = recv.reshape(2, groups * peer, 2 * part)
     taken = [jnp.dot(own_place, recv[i], preferred_element_type=f32).astype(bf16) for i in range(2)]
     compact = jnp.concatenate(
@@ -166,6 +180,7 @@
     half_cap = capacity // 2
     compact = compact.reshape(2, 1, half_cap, 4 * part)
     spreadout = jnp.broadcast_to(compact, (2, spread, half_cap, 4 * part))
+    wd_far = lax.ppermute(wd, "q", swap)
     gathered = lax.all_to_all(
         spreadout.reshape(2 * spread, half_cap, 4 * part),
         ("q", "x", "c"),
@@ -186,20 +201,20 @@
             held,
         ),
         in_specs=[pl.BlockSpec(memory_space=pltpu.SMEM)] + [vmem] * 2
-        + [pl.BlockSpec(memory_space=pltpu.HBM)] * 3,
+        + [pl.BlockSpec(memory_space=pltpu.HBM)] * 6,
         out_specs=(vmem, vmem, vmem),
         scratch_shapes=[
             pltpu.VMEM((2, half_cap, 2 * width), bf16),
-            pltpu.VMEM(wg_both.shape, bf16),
-            pltpu.VMEM(wu_both.shape, bf16),
-            pltpu.VMEM(wd_both.shape, bf16),
-            pltpu.SemaphoreType.DMA((3,)),
+            pltpu.VMEM((2,) + wg.shape, bf16),
+            pltpu.VMEM((2,) + wu.shape, bf16),
+            pltpu.VMEM((2,) + wd.shape, bf16),
+            pltpu.SemaphoreType.DMA((6,)),
         ],
         compiler_params=pltpu.CompilerParams(vmem_limit_bytes=52 * 1024 * 1024),
         cost_estimate=pl.CostEstimate(
             flops=20 * half_cap * width * hidden, bytes_accessed=5 << 20, transcendentals=0
         ),
-    )(q.reshape(1), weight, gathered, wg_both, wu_both, wd_both)
+    )(q.reshape(1), weight, gathered, wg, wu, wd, wg_far, wu_far, wd_far)
     pieces = lax.all_to_all(piece, ("p", "q", "x", "c"), split_axis=0, concat_axis=0, tiled=True)
     pieces = pieces.reshape(2, 2, spread, half_cap // 2 + 16, 2 * part)
     summed = jnp.sum(pieces.astype(f32), axis=2)

time: 232 us -> 155 us (0.67)
  waiting for transfers between devices: 116 us -> 53.8 us
  between operations: 14.1 us -> 0.98 us
    all_gather x3 -> x0, waiting for transfers between devices: 66.8 us -> none  [the longest x1 45.3 us: local(): wd_both = lax.all_gather(wd, 'q', axis=0)]
    all_to_all x1, waiting for transfers between devices: 27.7 us -> 2.37 us  [local(): lax.all_to_all(send.reshape(experts, peer, 2 * part), ('p', 'z'), split_a...]
    ppermute x0 -> x3, waiting for transfers between devices: none -> 21.2 us  [the longest x1 11.7 us: local(): wu_far = lax.ppermute(wu_give, 'q', swap)]
    ppermute x0 -> x3, starting transfers between devices: none -> 11.9 us  [the longest x1 6.58 us: local(): wd_far = lax.ppermute(wd, 'q', swap)]
    all_to_all x1, waiting for transfers between devices: 0.01 us -> 9.69 us  [local(): lax.all_to_all(spreadout.reshape(2 * spread, half_cap, 4 * part), ('q', '...]
    all_to_all x1, starting transfers between devices: 34.6 us -> 29.3 us  [local(): lax.all_to_all(send.reshape(experts, peer, 2 * part), ('p', 'z'), split_a...]
    all_to_all x1, starting transfers between devices: 22.6 us -> 17.8 us  [local(): lax.all_to_all(back.reshape(groups, peer, exp_dev * part), 'z', split_axi...]
    all_to_all x1, starting transfers between devices: 7.24 us -> 4.62 us  [local(): lax.all_to_all(piece, ('p', 'q', 'x', 'c'), split_axis=0, concat_axis=0,...]
  transfers between devices with their start and end apart: 8 -> 8, of which waited for: 5 -> 6; matrix products, arithmetic and copies ran while one was open for 4% -> 6% of each run, Pallas kernels for 0% -> 0%
where the time goes in v4:
time: 155 us
  starting transfers between devices  73.2 us (47%)
  waiting for transfers between devices  53.8 us (35%)
  blocking collectives  9.97 us (6%)
  matrix products  6.15 us (4%)
  Pallas kernels  4.55 us (3%)
  local copies, waits for them, and re-layouts  3.1 us (2%)
  other arithmetic  2.88 us (2%)
    all_to_all x1, starting transfers between devices, local(): lax.all_to_all(send.reshape(experts, peer, 2 * part), ('p', 'z'), split_a...  29.3 us
    all_to_all x1, starting transfers between devices, local(): lax.all_to_all(back.reshape(groups, peer, exp_dev * part), 'z', split_axi...  17.8 us
    ppermute x1, waiting for transfers between devices, local(): wu_far = lax.ppermute(wu_give, 'q', swap)  11.7 us
    all_to_all x1, waiting for transfers between devices, local(): lax.all_to_all(back.reshape(groups, peer, exp_dev * part), 'z', split_axi...  10.4 us
    all_to_all x1, waiting for transfers between devices, local(): lax.all_to_all(piece, ('p', 'q', 'x', 'c'), split_axis=0, concat_axis=0,...  10.1 us
    all_gather x1, blocking collectives, local(): got = lax.all_gather(give, 'q', axis=0)  9.97 us
    all_to_all x1, waiting for transfers between devices, local(): lax.all_to_all(spreadout.reshape(2 * spread, half_cap, 4 * part), ('q', '...  9.69 us
    ppermute x1, waiting for transfers between devices, local(): wg_far = lax.ppermute(wg_give, 'q', swap)  9.44 us
  transfers between devices with their start and end apart: 8, of which 6 were waited for; matrix products, arithmetic and copies ran while one was open for 6% of the time, Pallas kernels for 0%

profile of v4, /device:TPU:1, one launch (start us, length us, event | category | flops | bytes accessed | tf_op | source)
XLA Modules:
  0.0 154.7 jit_solution(12301867982060287522)
XLA Ops:
  0.6 0.0 copy-start
  0.6 0.0 copy-start.5
  0.7 0.0 copy-start.1
  0.7 0.8 pad_maximum_fusion.4
  1.5 0.7 collective-permute-start
  2.1 6.6 %collective-permute-start.3 = (bf16[256,1024]{1,0:T(8,128)(2,1)}, bf16[256,1024]{1,0:T(8,128)(2,1)S(1)}, u32[]{:S(2)}, u32[]{:S(2)}) collective-permute-start(bf16[256,1024]{1,0:T(8,128)(2,1)} %bitcast.65), channel_id=1, source_target_pairs={{0,8},{8,0},{1,9},{9,1},{2,10},{10,2},{3,11},{11,3},{4,12},{12,4},... | collective-permute-start | bytes 1572872 | tf_op jit(solution)/shard_map/ppermute | solution.py:183
  8.7 0.0 copy-done.5
  8.7 0.1 convert_reduce_fusion.2
  8.8 0.1 reshape.187
  8.9 0.1 copy.26
  9.0 0.1 add.95
  9.1 0.1 iota_add_fusion
  9.2 1.2 select_reduce_fusion
  10.5 0.1 sub.38
  10.6 0.0 collective-permute-done
  10.6 0.9 convolution_convert_fusion.3
  11.5 29.3 %all-to-all-start = ((bf16[64,8,128]{2,1,0:T(8,128)(2,1)}), bf16[64,8,128]{2,1,0:T(8,128)(2,1)S(1)}, u32[]{:S(2)}, u32[]{:S(2)}) async-start(bf16[64,8,128]{2,1,0:T(8,128)(2,1)} %bitcast.11), calls=%async_computation | async-start | bytes 262144 | tf_op jit(solution)/shard_map/all_to_all | solution.py:161
  40.8 0.2 convert_reduce_fusion.1
  41.1 0.0 copy-done.1
  41.1 2.8 %collective-permute-start.1 = (bf16[1024,256]{1,0:T(8,128)(2,1)S(1)}, bf16[1024,256]{1,0:T(8,128)(2,1)S(1)}, u32[]{:S(2)}, u32[]{:S(2)}) collective-permute-start(bf16[1024,256]{1,0:T(8,128)(2,1)S(1)} %bitcast.62), channel_id=1, source_target_pairs={{0,8},{8,0},{1,9},{9,1},{2,10},{10,2},{3,11},{11,3},{4,12},{12,4},... | collective-permute-start | bytes 1572872 | tf_op jit(solution)/shard_map/ppermute | solution.py:159
  43.8 2.5 %collective-permute-start.2 = (bf16[1024,256]{1,0:T(8,128)(2,1)}, bf16[1024,256]{1,0:T(8,128)(2,1)S(1)}, u32[]{:S(2)}, u32[]{:S(2)}) collective-permute-start(bf16[1024,256]{1,0:T(8,128)(2,1)} %bitcast.63), channel_id=1, source_target_pairs={{0,8},{8,0},{1,9},{9,1},{2,10},{10,2},{3,11},{11,3},{4,12},{12,4},... | collective-permute-start | bytes 1572872 | tf_op jit(solution)/shard_map/ppermute | solution.py:160
  46.4 0.1 iota_compare_fusion.1
  46.5 9.4 %collective-permute-done.1.wg_far = bf16[1024,256]{1,0:T(8,128)(2,1)S(1)} collective-permute-done((bf16[1024,256]{1,0:T(8,128)(2,1)S(1)}, bf16[1024,256]{1,0:T(8,128)(2,1)S(1)}, u32[]{:S(2)}, u32[]{:S(2)}) %collective-permute-start.1) | collective-permute-done | bytes 524320 | tf_op jit(solution)/shard_map/ppermute | solution.py:159
  56.0 0.0 copy-start.3
  56.0 11.7 %collective-permute-done.2.wu_far = bf16[1024,256]{1,0:T(8,128)(2,1)S(1)} collective-permute-done((bf16[1024,256]{1,0:T(8,128)(2,1)}, bf16[1024,256]{1,0:T(8,128)(2,1)S(1)}, u32[]{:S(2)}, u32[]{:S(2)}) %collective-permute-start.2) | collective-permute-done | bytes 524320 | tf_op jit(solution)/shard_map/ppermute | solution.py:160
  67.7 0.0 copy-start.4
  67.7 2.4 %all-to-all-done = bf16[64,8,128]{2,1,0:T(8,128)(2,1)S(1)} async-done(((bf16[64,8,128]{2,1,0:T(8,128)(2,1)}), bf16[64,8,128]{2,1,0:T(8,128)(2,1)S(1)}, u32[]{:S(2)}, u32[]{:S(2)}) %all-to-all-start) | async-done | bytes 131104 | tf_op jit(solution)/shard_map/all_to_all | solution.py:161
  70.1 0.2 convolution_convert_fusion.7
  70.3 0.2 convolution_convert_fusion.6
  70.5 0.1 copy.28
  70.7 0.8 broadcast_in_dim.64
  71.5 0.0 copy-done.3
  71.5 0.0 copy-done.4
  71.5 9.0 %all-to-all-start.1 = ((bf16[16,64,256]{2,1,0:T(8,128)(2,1)}), bf16[16,64,256]{2,1,0:T(8,128)(2,1)S(1)}, u32[]{:S(2)}, u32[]{:S(2)}) async-start(bf16[16,64,256]{2,1,0:T(8,128)(2,1)} %bitcast.15), calls=%async_computation.1 | async-start | bytes 1048576 | tf_op jit(solution)/shard_map/all_to_all | solution.py:184
  80.5 0.0 copy-done
  80.6 0.1 dynamic-slice_bitcast_fusion.1
  80.6 0.1 copy.29.weight_ref
  80.7 0.0 collective-permute-done.3.wd_far
  80.7 0.0 copy-start.2
  80.7 9.7 %all-to-all-done.1.rows_ref = bf16[16,64,256]{2,1,0:T(8,128)(2,1)S(1)} async-done(((bf16[16,64,256]{2,1,0:T(8,128)(2,1)}), bf16[16,64,256]{2,1,0:T(8,128)(2,1)S(1)}, u32[]{:S(2)}, u32[]{:S(2)}) %all-to-all-start.1) | async-done | bytes 524320 | tf_op jit(solution)/shard_map/all_to_all | solution.py:184
  90.4 0.0 copy-done.2
  90.4 4.6 %shard_map.110 = (bf16[32,48,128]{2,1,0:T(8,128)(2,1)}, bf16[64,2816]{1,0:T(8,128)(2,1)S(1)}, bf16[64,2816]{1,0:T(8,128)(2,1)S(1)}) custom-call(s32[1]{0:T(128)} %bitcast.6.q_ref, f32[64,1]{1,0:T(8,128)S(1)} %copy.29.weight_ref, bf16[16,64,256]{2,1,0:T(8,128)(2,1)S(1)} %all-to-all-done.1.rows_ref, bf16[1024,256]{1,0:T(8,128)(2,1)} %bitcast.61, ...), custom_call_target="tpu_custom_call" | custom-call | flops 335544320 | bytes 5242880 | tf_op jit(solution)/shard_map/pallas_call | solution.py:196
  95.0 4.6 %all-to-all-start.2 = ((bf16[32,48,128]{2,1,0:T(8,128)(2,1)}), bf16[32,48,128]{2,1,0:T(8,128)(2,1)S(1)}, u32[]{:S(2)}, u32[]{:S(2)}) async-start(bf16[32,48,128]{2,1,0:T(8,128)(2,1)} %get-tuple-element.21), calls=%async_computation.2 | async-start | bytes 786432 | tf_op jit(solution)/shard_map/all_to_all | solution.py:218
  99.6 0.1 iota_compare_fusion.2
  99.8 10.1 %all-to-all-done.2 = bf16[32,48,128]{2,1,0:T(8,128)(2,1)S(1)} async-done(((bf16[32,48,128]{2,1,0:T(8,128)(2,1)}), bf16[32,48,128]{2,1,0:T(8,128)(2,1)S(1)}, u32[]{:S(2)}, u32[]{:S(2)}) %all-to-all-start.2) | async-done | bytes 393248 | tf_op jit(solution)/shard_map/all_to_all | solution.py:218
  109.9 0.1 convert_reduce_fusion
  110.0 0.1 reshape.179
  110.2 0.2 convolution_convert_fusion.5
  110.4 0.2 convolution_convert_fusion.4
  110.6 0.7 copy.32
  111.3 17.8 %all-to-all-start.3 = ((bf16[32,8,128]{2,1,0:T(8,128)(2,1)}), bf16[32,8,128]{2,1,0:T(8,128)(2,1)S(1)}, u32[]{:S(2)}, u32[]{:S(2)}) async-start(bf16[32,8,128]{2,1,0:T(8,128)(2,1)} %bitcast.22), calls=%async_computation.3 | async-start | bytes 131072 | tf_op jit(solution)/shard_map/all_to_all | solution.py:238
  129.1 0.1 slice_add_fusion
  129.2 0.6 reshape.182
  129.8 10.0 %all-gather = bf16[128,2816]{1,0:T(8,128)(2,1)S(1)} all-gather(bf16[64,2816]{1,0:T(8,128)(2,1)S(1)} %get-tuple-element.24), channel_id=2, replica_groups=mesh['z'=32,'p'=2,'q'=2,'x'=4,'c'=2] {'q'}, dimensions={0}, use_global_device_ids=true | all-gather | bytes 1081344 | tf_op jit(solution)/shard_map/all_gather | solution.py:250
  139.8 1.1 fusion.2
  140.9 1.1 fusion.1
  142.0 1.1 fusion
  143.2 10.4 %all-to-all-done.3 = bf16[32,8,128]{2,1,0:T(8,128)(2,1)S(1)} async-done(((bf16[32,8,128]{2,1,0:T(8,128)(2,1)}), bf16[32,8,128]{2,1,0:T(8,128)(2,1)S(1)}, u32[]{:S(2)}, u32[]{:S(2)}) %all-to-all-start.3) | async-done | bytes 65568 | tf_op jit(solution)/shard_map/all_to_all | solution.py:238
  153.6 0.2 fusion.7
  153.8 0.9 fusion.3
  (17 shorter events, 0.2 us)
Async XLA Ops:
  0.6 79.9 %copy-start = (f32[2,128]{1,0:T(2,128)S(1)}, f32[2,128]{1,0:T(2,128)}, u32[]{:S(2)}) copy-start(f32[2,128]{1,0:T(2,128)} %param.12) | copy-start | bytes 3076
  0.6 8.1 %copy-start.5 = (s32[64,128]{1,0:T(8,128)S(1)}, s32[64,128]{1,0:T(8,128)}, u32[]{:S(2)}) copy-start(s32[64,128]{1,0:T(8,128)} %param.13) | copy-start | bytes 98308
  0.7 40.4 %copy-start.1 = (bf16[1,1024,256]{2,1,0:T(8,128)(2,1)S(1)}, bf16[1,1024,256]{2,1,0:T(8,128)(2,1)}, u32[]{:S(2)}) copy-start(bf16[1,1024,256]{2,1,0:T(8,128)(2,1)} %param.9) | copy-start | bytes 1572868
  1.5 9.1 %collective-permute-start = (bf16[128,128]{0,1:T(8,128)(2,1)S(1)}, bf16[128,128]{0,1:T(8,128)(2,1)S(1)}, u32[]{:S(2)}, u32[]{:S(2)}) collective-permute-start(bf16[128,128]{0,1:T(8,128)(2,1)S(1)} %pad_maximum_fusion.4), channel_id=1, source_target_pairs={{0,0},{8,16},{16,8},{24,24},{1,1},{9,17},{17,9},{25,25},{2,2},{10,... | collective-permute-start | bytes 98312 | tf_op jit(solution)/shard_map/ppermute | solution.py:137
  2.1 78.6 %collective-permute-start.3 = (bf16[256,1024]{1,0:T(8,128)(2,1)}, bf16[256,1024]{1,0:T(8,128)(2,1)S(1)}, u32[]{:S(2)}, u32[]{:S(2)}) collective-permute-start(bf16[256,1024]{1,0:T(8,128)(2,1)} %bitcast.65), channel_id=1, source_target_pairs={{0,8},{8,0},{1,9},{9,1},{2,10},{10,2},{3,11},{11,3},{4,12},{12,4},... | collective-permute-start | bytes 1572872 | tf_op jit(solution)/shard_map/ppermute | solution.py:183
  11.5 58.6 %all-to-all-start = ((bf16[64,8,128]{2,1,0:T(8,128)(2,1)}), bf16[64,8,128]{2,1,0:T(8,128)(2,1)S(1)}, u32[]{:S(2)}, u32[]{:S(2)}) async-start(bf16[64,8,128]{2,1,0:T(8,128)(2,1)} %bitcast.11), calls=%async_computation | async-start | bytes 262144 | tf_op jit(solution)/shard_map/all_to_all | solution.py:161
  41.1 14.9 %collective-permute-start.1 = (bf16[1024,256]{1,0:T(8,128)(2,1)S(1)}, bf16[1024,256]{1,0:T(8,128)(2,1)S(1)}, u32[]{:S(2)}, u32[]{:S(2)}) collective-permute-start(bf16[1024,256]{1,0:T(8,128)(2,1)S(1)} %bitcast.62), channel_id=1, source_target_pairs={{0,8},{8,0},{1,9},{9,1},{2,10},{10,2},{3,11},{11,3},{4,12},{12,4},... | collective-permute-start | bytes 1572872 | tf_op jit(solution)/shard_map/ppermute | solution.py:159
  43.8 23.9 %collective-permute-start.2 = (bf16[1024,256]{1,0:T(8,128)(2,1)}, bf16[1024,256]{1,0:T(8,128)(2,1)S(1)}, u32[]{:S(2)}, u32[]{:S(2)}) collective-permute-start(bf16[1024,256]{1,0:T(8,128)(2,1)} %bitcast.63), channel_id=1, source_target_pairs={{0,8},{8,0},{1,9},{9,1},{2,10},{10,2},{3,11},{11,3},{4,12},{12,4},... | collective-permute-start | bytes 1572872 | tf_op jit(solution)/shard_map/ppermute | solution.py:160
  56.0 15.5 %copy-start.3 = (bf16[1024,256]{1,0:T(8,128)(2,1)}, bf16[1024,256]{1,0:T(8,128)(2,1)S(1)}, u32[]{:S(2)}) copy-start(bf16[1024,256]{1,0:T(8,128)(2,1)S(1)} %collective-permute-done.1.wg_far) | copy-start | bytes 1572868
  67.7 3.8 %copy-start.4 = (bf16[1024,256]{1,0:T(8,128)(2,1)}, bf16[1024,256]{1,0:T(8,128)(2,1)S(1)}, u32[]{:S(2)}) copy-start(bf16[1024,256]{1,0:T(8,128)(2,1)S(1)} %collective-permute-done.2.wu_far) | copy-start | bytes 1572868
  71.5 18.9 %all-to-all-start.1 = ((bf16[16,64,256]{2,1,0:T(8,128)(2,1)}), bf16[16,64,256]{2,1,0:T(8,128)(2,1)S(1)}, u32[]{:S(2)}, u32[]{:S(2)}) async-start(bf16[16,64,256]{2,1,0:T(8,128)(2,1)} %bitcast.15), calls=%async_computation.1 | async-start | bytes 1048576 | tf_op jit(solution)/shard_map/all_to_all | solution.py:184
  80.7 9.7 %copy-start.2 = (bf16[256,1024]{1,0:T(8,128)(2,1)}, bf16[256,1024]{1,0:T(8,128)(2,1)S(1)}, u32[]{:S(2)}) copy-start(bf16[256,1024]{1,0:T(8,128)(2,1)S(1)} %collective-permute-done.3.wd_far) | copy-start | bytes 1572868
  95.0 14.9 %all-to-all-start.2 = ((bf16[32,48,128]{2,1,0:T(8,128)(2,1)}), bf16[32,48,128]{2,1,0:T(8,128)(2,1)S(1)}, u32[]{:S(2)}, u32[]{:S(2)}) async-start(bf16[32,48,128]{2,1,0:T(8,128)(2,1)} %get-tuple-element.21), calls=%async_computation.2 | async-start | bytes 786432 | tf_op jit(solution)/shard_map/all_to_all | solution.py:218
  111.3 42.3 %all-to-all-start.3 = ((bf16[32,8,128]{2,1,0:T(8,128)(2,1)}), bf16[32,8,128]{2,1,0:T(8,128)(2,1)S(1)}, u32[]{:S(2)}, u32[]{:S(2)}) async-start(bf16[32,8,128]{2,1,0:T(8,128)(2,1)} %bitcast.22), calls=%async_computation.3 | async-start | bytes 131072 | tf_op jit(solution)/shard_map/all_to_all | solution.py:238

commit v5 on v4

--- a/solution.py
+++ b/solution.py
@@ -14,9 +14,7 @@
     wg_own,
     wu_own,
     wd_own,
-    wg_far,
-    wu_far,
-    wd_far,
+    far_ref,
     out_ref,
     keep_ref,
     give_ref,
@@ -27,18 +25,25 @@
     sem,
 ):
     q = q_ref[0]
+    chunk = wg_own.shape[1]
+    far = 1 - q
+    pairs = [
+        [(wg_own, wg_ref.at[q]), (far_ref.at[0], wg_ref.at[far])],
+        [(wu_own, wu_ref.at[q]), (far_ref.at[1], wu_ref.at[far])],
+        [(wd_own, wd_ref.at[q])]
+        + [
+            (far_ref.at[2, pl.ds(i * chunk, chunk)], wd_ref.at[far, :, pl.ds(i * chunk, chunk)])
+            for i in range(wd_own.shape[1] // chunk)
+        ],
+    ]
     loads = []
-    for i, (own, far, near) in enumerate(
-        ((wg_own, wg_far, wg_ref), (wu_own, wu_far, wu_ref), (wd_own, wd_far, wd_ref))
-    ):
-        loads.append(
-            (
-                pltpu.make_async_copy(own, near.at[q], sem.at[2 * i]),
-                pltpu.make_async_copy(far, near.at[1 - q], sem.at[2 * i + 1]),
-            )
-        )
-        loads[i][0].start()
-        loads[i][1].start()
+    count = 0
+    for group in pairs:
+        loads.append([])
+        for source, target in group:
+            loads[-1].append(pltpu.make_async_copy(source, target, sem.at[count]))
+            loads[-1][-1].start()
+            count += 1
     bf16 = jnp.bfloat16
     f32 = jnp.float32
     spread = rows_ref.shape[0] // 2
@@ -68,16 +73,16 @@
         return nat_ref[side, :, pl.ds(kind * width, width)]
 
     across = (((1,), (1,)), ((), ()))
-    loads[0][0].wait()
-    loads[0][1].wait()
+    for load in loads[0]:
+        load.wait()
     gate_pre = jnp.dot(over(0, 0), wg_ref[0], preferred_element_type=f32)
     gate_pre = gate_pre + jnp.dot(over(1, 0), wg_ref[1], preferred_element_type=f32)
-    loads[1][0].wait()
-    loads[1][1].wait()
+    for load in loads[1]:
+        load.wait()
     up_pre = jnp.dot(over(0, 0), wu_ref[0], preferred_element_type=f32)
     up_pre = up_pre + jnp.dot(over(1, 0), wu_ref[1], preferred_element_type=f32)
-    loads[2][0].wait()
-    loads[2][1].wait()
+    for load in loads[2]:
+        load.wait()
     back_grad = lax.dot_general(over(0, 1), wd_ref[0], across, preferred_element_type=f32)
     back_grad = back_grad + lax.dot_general(
         over(1, 1), wd_ref[1], across, preferred_element_type=f32
@@ -117,6 +122,22 @@
         ref[:, pl.ds(2 * width + 2 * hidden, hidden)] = d_up
 
 
+def pack(wg_ref, wu_ref, wd_ref, out_ref, sem):
+    chunk = wg_ref.shape[1]
+    pairs = [(wg_ref, out_ref.at[0]), (wu_ref, out_ref.at[1])] + [
+        (wd_ref.at[:, pl.ds(i * chunk, chunk)], out_ref.at[2, pl.ds(i * chunk, chunk)])
+        for i in range(wd_ref.shape[1] // chunk)
+    ]
+    copies = [
+        pltpu.make_async_copy(source, target, sem.at[i])
+        for i, (source, target) in enumerate(pairs)
+    ]
+    for copy in copies:
+        copy.start()
+    for copy in copies:
+        copy.wait()
+
+
 def local(x_tokens, cotangent, w_gate, w_up, w_down, combine, indices):
     bf16 = jnp.bfloat16
     f32 = jnp.float32
@@ -137,6 +158,16 @@
     table = lax.ppermute(table, ("p", "q"), [(0, 0), (1, 2), (2, 1), (3, 3)])
 
     swap = [(0, 1), (1, 0)]
+    here = pl.BlockSpec(memory_space=pltpu.HBM)
+    packed = pl.pallas_call(
+        pack,
+        out_shape=jax.ShapeDtypeStruct((3,) + wg.shape, bf16),
+        in_specs=[here] * 3,
+        out_specs=here,
+        scratch_shapes=[pltpu.SemaphoreType.DMA((6,))],
+        cost_estimate=pl.CostEstimate(flops=0, bytes_accessed=3 << 20, transcendentals=0),
+    )(wg, wu, wd)
+    far = lax.ppermute(packed, "q", swap)
 
     slots = jnp.arange(capacity, dtype=jnp.int32)
     places = jnp.arange(peer, dtype=jnp.int32)
@@ -155,9 +186,6 @@
     pick = (chosen[:, :, None] == tokens[None, None, :]).astype(bf16)
     pick = pick.reshape(experts * peer, tok_dev)
     send = jnp.dot(pick, table, preferred_element_type=f32).astype(bf16)
-    send, wg_give, wu_give = lax.optimization_barrier((send, wg, wu))
-    wg_far = lax.ppermute(wg_give, "q", swap)
-    wu_far = lax.ppermute(wu_give, "q", swap)
     recv = lax.all_to_all(
         send.reshape(experts, peer, 2 * part), ("p", "z"), split_axis=0, concat_axis=0, tiled=True
     )
@@ -171,7 +199,7 @@
     place = jnp.where(own_block[:, :, None] == cell_block[None, None, :], own_want[:, None, :], -1)
     place = (place == slots[None, :, None]).astype(bf16)
     own_place = lax.dynamic_index_in_dim(place, p, 0, keepdims=False)
-    recv, wg_far, wu_far = lax.optimization_barrier((recv, wg_far, wu_far))
+    recv, far = lax.optimization_barrier((recv, far))
     recv = recv.reshape(2, groups * peer, 2 * part)
     taken = [jnp.dot(own_place, recv[i], preferred_element_type=f32).astype(bf16) for i in range(2)]
     compact = jnp.concatenate(
@@ -180,7 +208,6 @@
     half_cap = capacity // 2
     compact = compact.reshape(2, 1, half_cap, 4 * part)
     spreadout = jnp.broadcast_to(compact, (2, spread, half_cap, 4 * part))
-    wd_far = lax.ppermute(wd, "q", swap)
     gathered = lax.all_to_all(
         spreadout.reshape(2 * spread, half_cap, 4 * part),
         ("q", "x", "c"),
@@ -201,20 +228,20 @@
             held,
         ),
         in_specs=[pl.BlockSpec(memory_space=pltpu.SMEM)] + [vmem] * 2
-        + [pl.BlockSpec(memory_space=pltpu.HBM)] * 6,
+        + [here] * 4,
         out_specs=(vmem, vmem, vmem),
         scratch_shapes=[
             pltpu.VMEM((2, half_cap, 2 * width), bf16),
             pltpu.VMEM((2,) + wg.shape, bf16),
             pltpu.VMEM((2,) + wu.shape, bf16),
             pltpu.VMEM((2,) + wd.shape, bf16),
-            pltpu.SemaphoreType.DMA((6,)),
+            pltpu.SemaphoreType.DMA((5 + width // hidden,)),
         ],
         compiler_params=pltpu.CompilerParams(vmem_limit_bytes=52 * 1024 * 1024),
         cost_estimate=pl.CostEstimate(
             flops=20 * half_cap * width * hidden, bytes_accessed=5 << 20, transcendentals=0
         ),
-    )(q.reshape(1), weight, gathered, wg, wu, wd, wg_far, wu_far, wd_far)
+    )(q.reshape(1), weight, gathered, wg, wu, wd, far)
     pieces = lax.all_to_all(piece, ("p", "q", "x", "c"), split_axis=0, concat_axis=0, tiled=True)
     pieces = pieces.reshape(2, 2, spread, half_cap // 2 + 16, 2 * part)
     summed = jnp.sum(pieces.astype(f32), axis=2)

time: 155 us -> 190 us (1.23)
  Pallas kernels: 4.55 us -> 53.4 us
  starting transfers between devices: 73.2 us -> 54 us
  waiting for transfers between devices: 53.8 us -> 58.9 us
    pallas_call x0 -> x1, Pallas kernels: none -> 48.8 us  [local(): pl.pallas_call(pack, out_shape=jax.ShapeDtypeStruct((3,) + wg.shape, bf16...]
    all_to_all x1, waiting for transfers between devices: 2.37 us -> 28.8 us  [local(): lax.all_to_all(send.reshape(experts, peer, 2 * part), ('p', 'z'), split_a...]
    ppermute x3 -> x1, waiting for transfers between devices: 21.2 us -> 0.01 us  [local(): far = lax.ppermute(packed, 'q', swap)]
    all_to_all x1, starting transfers between devices: 17.8 us -> 3.86 us  [local(): lax.all_to_all(back.reshape(groups, peer, exp_dev * part), 'z', split_axi...]
    ppermute x3 -> x1, starting transfers between devices: 11.9 us -> 6.58 us  [local(): far = lax.ppermute(packed, 'q', swap)]
  transfers between devices with their start and end apart: 8 -> 6, of which waited for: 6 -> 4; matrix products, arithmetic and copies ran while one was open for 6% -> 4% of each run, Pallas kernels for 0% -> 26%
where the time goes in v5:
time: 190 us
  waiting for transfers between devices  58.9 us (31%)
  starting transfers between devices  54 us (28%)
  Pallas kernels  53.4 us (28%)
  blocking collectives  10.3 us (5%)
  matrix products  6.15 us (3%)
  local copies, waits for them, and re-layouts  3.09 us (2%)
  other arithmetic  2.83 us (1%)
    pallas_call x1, Pallas kernels, local(): pl.pallas_call(pack, out_shape=jax.ShapeDtypeStruct((3,) + wg.shape, bf16...  48.8 us
    all_to_all x1, starting transfers between devices, local(): lax.all_to_all(send.reshape(experts, peer, 2 * part), ('p', 'z'), split_a...  29.3 us
    all_to_all x1, waiting for transfers between devices, local(): lax.all_to_all(send.reshape(experts, peer, 2 * part), ('p', 'z'), split_a...  28.8 us
    all_gather x1, blocking collectives, local(): got = lax.all_gather(give, 'q', axis=0)  10.3 us
    all_to_all x1, waiting for transfers between devices, local(): lax.all_to_all(back.reshape(groups, peer, exp_dev * part), 'z', split_axi...  10.2 us
    all_to_all x1, waiting for transfers between devices, local(): lax.all_to_all(piece, ('p', 'q', 'x', 'c'), split_axis=0, concat_axis=0,...  10.1 us
    all_to_all x1, waiting for transfers between devices, local(): lax.all_to_all(spreadout.reshape(2 * spread, half_cap, 4 * part), ('q', '...  9.7 us
    all_to_all x1, starting transfers between devices, local(): lax.all_to_all(spreadout.reshape(2 * spread, half_cap, 4 * part), ('q', '...  9.04 us
  transfers between devices with their start and end apart: 6, of which 4 were waited for; matrix products, arithmetic and copies ran while one was open for 4% of the time, Pallas kernels for 26%

profile of v5, /device:TPU:1, one launch (start us, length us, event | category | flops | bytes accessed | tf_op | source)
XLA Modules:
  0.0 189.6 jit_solution(12572659466191824350)
XLA Ops:
  0.6 0.0 copy-start
  0.6 0.7 pad_maximum_fusion.4
  1.4 0.7 collective-permute-start
  2.0 0.0 copy-start.2
  2.1 48.8 %shard_map.110 = bf16[3,1024,256]{2,1,0:T(8,128)(2,1)} custom-call(bf16[1024,256]{1,0:T(8,128)(2,1)} %bitcast.61, bf16[1024,256]{1,0:T(8,128)(2,1)} %bitcast.63, bf16[256,1024]{1,0:T(8,128)(2,1)} %bitcast.65), custom_call_target="tpu_custom_call" | custom-call | bytes 3145728 | tf_op jit(solution)/shard_map/pallas_call | solution.py:162
  50.9 6.6 %collective-permute-start.1 = (bf16[3,1024,256]{2,1,0:T(8,128)(2,1)}, bf16[3,1024,256]{2,1,0:T(8,128)(2,1)S(1)}, u32[]{:S(2)}, u32[]{:S(2)}) collective-permute-start(bf16[3,1024,256]{2,1,0:T(8,128)(2,1)} %shard_map.110), channel_id=1, source_target_pairs={{0,8},{8,0},{1,9},{9,1},{2,10},{10,2},{3,11},{11,3},{4,12},{12,4},... | collective-permute-start | bytes 4718600 | tf_op jit(solution)/shard_map/ppermute | solution.py:170
  57.5 0.0 copy-done.2
  57.5 0.1 convert_reduce_fusion.2
  57.6 0.1 reshape.187
  57.7 0.1 copy.26
  57.8 0.1 add.95
  57.9 0.1 iota_add_fusion
  58.0 1.2 select_reduce_fusion
  59.2 0.1 sub.38
  59.3 0.0 collective-permute-done
  59.3 0.9 fusion.3
  60.2 29.3 %all-to-all-start = ((bf16[64,8,128]{2,1,0:T(8,128)(2,1)}), bf16[64,8,128]{2,1,0:T(8,128)(2,1)S(1)}, u32[]{:S(2)}, u32[]{:S(2)}) async-start(bf16[64,8,128]{2,1,0:T(8,128)(2,1)} %fusion.3), calls=%async_computation | async-start | bytes 262144 | tf_op jit(solution)/shard_map/all_to_all | solution.py:189
  89.6 0.2 convert_reduce_fusion.1
  89.8 0.1 iota_compare_fusion.1
  90.0 28.8 %all-to-all-done = bf16[64,8,128]{2,1,0:T(8,128)(2,1)S(1)} async-done(((bf16[64,8,128]{2,1,0:T(8,128)(2,1)}), bf16[64,8,128]{2,1,0:T(8,128)(2,1)S(1)}, u32[]{:S(2)}, u32[]{:S(2)}) %all-to-all-start) | async-done | bytes 131104 | tf_op jit(solution)/shard_map/all_to_all | solution.py:189
  118.8 0.0 collective-permute-done.1.far_ref
  118.8 0.0 copy-start.1
  118.8 0.2 convolution_convert_fusion.7
  119.0 0.2 convolution_convert_fusion.6
  119.3 0.1 copy.28
  119.4 0.8 broadcast_in_dim.64
  120.2 9.0 %all-to-all-start.1 = ((bf16[16,64,256]{2,1,0:T(8,128)(2,1)}), bf16[16,64,256]{2,1,0:T(8,128)(2,1)S(1)}, u32[]{:S(2)}, u32[]{:S(2)}) async-start(bf16[16,64,256]{2,1,0:T(8,128)(2,1)} %bitcast.16), calls=%async_computation.1 | async-start | bytes 1048576 | tf_op jit(solution)/shard_map/all_to_all | solution.py:211
  129.3 0.0 copy-done
  129.3 0.1 dynamic-slice_bitcast_fusion.1
  129.4 0.1 copy.29.weight_ref
  129.5 9.7 %all-to-all-done.1.rows_ref = bf16[16,64,256]{2,1,0:T(8,128)(2,1)S(1)} async-done(((bf16[16,64,256]{2,1,0:T(8,128)(2,1)}), bf16[16,64,256]{2,1,0:T(8,128)(2,1)S(1)}, u32[]{:S(2)}, u32[]{:S(2)}) %all-to-all-start.1) | async-done | bytes 524320 | tf_op jit(solution)/shard_map/all_to_all | solution.py:211
  139.2 0.0 copy-done.1
  139.2 4.6 %shard_map.111 = (bf16[32,48,128]{2,1,0:T(8,128)(2,1)}, bf16[64,2816]{1,0:T(8,128)(2,1)S(1)}, bf16[64,2816]{1,0:T(8,128)(2,1)S(1)}) custom-call(s32[1]{0:T(128)} %bitcast.6.q_ref, f32[64,1]{1,0:T(8,128)S(1)} %copy.29.weight_ref, bf16[16,64,256]{2,1,0:T(8,128)(2,1)S(1)} %all-to-all-done.1.rows_ref, bf16[1024,256]{1,0:T(8,128)(2,1)} %bitcast.62, ...), custom_call_target="tpu_custom_call" | custom-call | flops 335544320 | bytes 5242880 | tf_op jit(solution)/shard_map/pallas_call | solution.py:223
  143.8 4.6 %all-to-all-start.2 = ((bf16[32,48,128]{2,1,0:T(8,128)(2,1)}), bf16[32,48,128]{2,1,0:T(8,128)(2,1)S(1)}, u32[]{:S(2)}, u32[]{:S(2)}) async-start(bf16[32,48,128]{2,1,0:T(8,128)(2,1)} %get-tuple-element.13), calls=%async_computation.2 | async-start | bytes 786432 | tf_op jit(solution)/shard_map/all_to_all | solution.py:245
  148.4 0.1 iota_compare_fusion.2
  148.5 10.1 %all-to-all-done.2 = bf16[32,48,128]{2,1,0:T(8,128)(2,1)S(1)} async-done(((bf16[32,48,128]{2,1,0:T(8,128)(2,1)}), bf16[32,48,128]{2,1,0:T(8,128)(2,1)S(1)}, u32[]{:S(2)}, u32[]{:S(2)}) %all-to-all-start.2) | async-done | bytes 393248 | tf_op jit(solution)/shard_map/all_to_all | solution.py:245
  158.7 0.1 convert_reduce_fusion
  158.8 0.1 reshape.179
  158.9 0.2 convolution_convert_fusion.5
  159.2 0.2 convolution_convert_fusion.4
  159.4 0.7 copy.32
  160.1 3.9 %all-to-all-start.3 = ((bf16[32,8,128]{2,1,0:T(8,128)(2,1)}), bf16[32,8,128]{2,1,0:T(8,128)(2,1)S(1)}, u32[]{:S(2)}, u32[]{:S(2)}) async-start(bf16[32,8,128]{2,1,0:T(8,128)(2,1)} %bitcast.22), calls=%async_computation.3 | async-start | bytes 131072 | tf_op jit(solution)/shard_map/all_to_all | solution.py:265
  164.0 0.1 slice_add_fusion
  164.0 0.6 reshape.182
  164.7 10.3 %all-gather = bf16[128,2816]{1,0:T(8,128)(2,1)S(1)} all-gather(bf16[64,2816]{1,0:T(8,128)(2,1)S(1)} %get-tuple-element.16), channel_id=2, replica_groups=mesh['z'=32,'p'=2,'q'=2,'x'=4,'c'=2] {'q'}, dimensions={0}, use_global_device_ids=true | all-gather | bytes 1081344 | tf_op jit(solution)/shard_map/all_gather | solution.py:277
  175.0 1.1 fusion.2
  176.1 1.1 fusion.1
  177.2 1.1 fusion
  178.4 10.2 %all-to-all-done.3 = bf16[32,8,128]{2,1,0:T(8,128)(2,1)S(1)} async-done(((bf16[32,8,128]{2,1,0:T(8,128)(2,1)}), bf16[32,8,128]{2,1,0:T(8,128)(2,1)S(1)}, u32[]{:S(2)}, u32[]{:S(2)}) %all-to-all-start.3) | async-done | bytes 65568 | tf_op jit(solution)/shard_map/all_to_all | solution.py:265
  188.6 0.2 fusion.8
  188.8 0.9 fusion.4
  (17 shorter events, 0.2 us)
Async XLA Ops:
  0.6 128.7 %copy-start = (f32[2,128]{1,0:T(2,128)S(1)}, f32[2,128]{1,0:T(2,128)}, u32[]{:S(2)}) copy-start(f32[2,128]{1,0:T(2,128)} %param.12) | copy-start | bytes 3076
  1.4 57.9 %collective-permute-start = (bf16[128,128]{0,1:T(8,128)(2,1)S(1)}, bf16[128,128]{0,1:T(8,128)(2,1)S(1)}, u32[]{:S(2)}, u32[]{:S(2)}) collective-permute-start(bf16[128,128]{0,1:T(8,128)(2,1)S(1)} %pad_maximum_fusion.4), channel_id=1, source_target_pairs={{0,0},{8,16},{16,8},{24,24},{1,1},{9,17},{17,9},{25,25},{2,2},{10,... | collective-permute-start | bytes 98312 | tf_op jit(solution)/shard_map/ppermute | solution.py:158
  2.0 55.4 %copy-start.2 = (s32[64,128]{1,0:T(8,128)S(1)}, s32[64,128]{1,0:T(8,128)}, u32[]{:S(2)}) copy-start(s32[64,128]{1,0:T(8,128)} %param.13) | copy-start | bytes 98308
  50.9 67.9 %collective-permute-start.1 = (bf16[3,1024,256]{2,1,0:T(8,128)(2,1)}, bf16[3,1024,256]{2,1,0:T(8,128)(2,1)S(1)}, u32[]{:S(2)}, u32[]{:S(2)}) collective-permute-start(bf16[3,1024,256]{2,1,0:T(8,128)(2,1)} %shard_map.110), channel_id=1, source_target_pairs={{0,8},{8,0},{1,9},{9,1},{2,10},{10,2},{3,11},{11,3},{4,12},{12,4},... | collective-permute-start | bytes 4718600 | tf_op jit(solution)/shard_map/ppermute | solution.py:170
  60.2 58.6 %all-to-all-start = ((bf16[64,8,128]{2,1,0:T(8,128)(2,1)}), bf16[64,8,128]{2,1,0:T(8,128)(2,1)S(1)}, u32[]{:S(2)}, u32[]{:S(2)}) async-start(bf16[64,8,128]{2,1,0:T(8,128)(2,1)} %fusion.3), calls=%async_computation | async-start | bytes 262144 | tf_op jit(solution)/shard_map/all_to_all | solution.py:189
  118.8 20.4 %copy-start.1 = (bf16[3,1024,256]{2,1,0:T(8,128)(2,1)}, bf16[3,1024,256]{2,1,0:T(8,128)(2,1)S(1)}, u32[]{:S(2)}) copy-start(bf16[3,1024,256]{2,1,0:T(8,128)(2,1)S(1)} %collective-permute-done.1.far_ref) | copy-start | bytes 4718596
  120.2 18.9 %all-to-all-start.1 = ((bf16[16,64,256]{2,1,0:T(8,128)(2,1)}), bf16[16,64,256]{2,1,0:T(8,128)(2,1)S(1)}, u32[]{:S(2)}, u32[]{:S(2)}) async-start(bf16[16,64,256]{2,1,0:T(8,128)(2,1)} %bitcast.16), calls=%async_computation.1 | async-start | bytes 1048576 | tf_op jit(solution)/shard_map/all_to_all | solution.py:211
  143.8 14.9 %all-to-all-start.2 = ((bf16[32,48,128]{2,1,0:T(8,128)(2,1)}), bf16[32,48,128]{2,1,0:T(8,128)(2,1)S(1)}, u32[]{:S(2)}, u32[]{:S(2)}) async-start(bf16[32,48,128]{2,1,0:T(8,128)(2,1)} %get-tuple-element.13), calls=%async_computation.2 | async-start | bytes 786432 | tf_op jit(solution)/shard_map/all_to_all | solution.py:245
  160.1 28.5 %all-to-all-start.3 = ((bf16[32,8,128]{2,1,0:T(8,128)(2,1)}), bf16[32,8,128]{2,1,0:T(8,128)(2,1)S(1)}, u32[]{:S(2)}, u32[]{:S(2)}) async-start(bf16[32,8,128]{2,1,0:T(8,128)(2,1)} %bitcast.22), calls=%async_computation.3 | async-start | bytes 131072 | tf_op jit(solution)/shard_map/all_to_all | solution.py:265

commit v6 on v5

--- a/solution.py
+++ b/solution.py
@@ -163,7 +163,7 @@
         pack,
         out_shape=jax.ShapeDtypeStruct((3,) + wg.shape, bf16),
         in_specs=[here] * 3,
-        out_specs=here,
+        out_specs=pl.BlockSpec(memory_space=pltpu.VMEM),
         scratch_shapes=[pltpu.SemaphoreType.DMA((6,))],
         cost_estimate=pl.CostEstimate(flops=0, bytes_accessed=3 << 20, transcendentals=0),
     )(wg, wu, wd)

time: 190 us -> 144 us (0.76)
  Pallas kernels: 53.4 us -> 7.14 us
    pallas_call x1, Pallas kernels: 48.8 us -> 2.55 us  [local(): pl.pallas_call(pack, out_shape=jax.ShapeDtypeStruct((3,) + wg.shape, bf16...]
  transfers between devices with their start and end apart: 6 -> 6, of which waited for: 4 -> 4; matrix products, arithmetic and copies ran while one was open for 4% -> 5% of each run, Pallas kernels for 26% -> 2%
where the time goes in v6:
time: 144 us; the launch traced here: 143 us
  waiting for transfers between devices  58.9 us (41%)
  starting transfers between devices  54 us (38%)
  blocking collectives  10.3 us (7%)
  Pallas kernels  7.14 us (5%)
  matrix products  6.16 us (4%)
  local copies, waits for them, and re-layouts  3.09 us (2%)
  other arithmetic  2.83 us (2%)
    all_to_all x1, starting transfers between devices, local(): lax.all_to_all(send.reshape(experts, peer, 2 * part), ('p', 'z'), split_a...  29.3 us
    all_to_all x1, waiting for transfers between devices, local(): lax.all_to_all(send.reshape(experts, peer, 2 * part), ('p', 'z'), split_a...  28.8 us
    all_gather x1, blocking collectives, local(): got = lax.all_gather(give, 'q', axis=0)  10.3 us
    all_to_all x1, waiting for transfers between devices, local(): lax.all_to_all(back.reshape(groups, peer, exp_dev * part), 'z', split_axi...  10.2 us
    all_to_all x1, waiting for transfers between devices, local(): lax.all_to_all(piece, ('p', 'q', 'x', 'c'), split_axis=0, concat_axis=0,...  10.1 us
    all_to_all x1, waiting for transfers between devices, local(): lax.all_to_all(spreadout.reshape(2 * spread, half_cap, 4 * part), ('q', '...  9.7 us
    all_to_all x1, starting transfers between devices, local(): lax.all_to_all(spreadout.reshape(2 * spread, half_cap, 4 * part), ('q', '...  9.04 us
    ppermute x1, starting transfers between devices, local(): far = lax.ppermute(packed, 'q', swap)  6.58 us
  transfers between devices with their start and end apart: 6, of which 4 were waited for; matrix products, arithmetic and copies ran while one was open for 5% of the time, Pallas kernels for 2%

profile of v6, /device:TPU:1, one launch (start us, length us, event | category | flops | bytes accessed | tf_op | source)
XLA Modules:
  0.0 143.4 jit_solution(1240955486041466503)
XLA Ops:
  0.6 0.0 copy-start
  0.6 0.7 pad_maximum_fusion.4
  1.4 0.7 collective-permute-start
  2.0 0.0 copy-start.2
  2.1 2.5 %shard_map.110 = bf16[3,1024,256]{2,1,0:T(8,128)(2,1)} custom-call(bf16[1024,256]{1,0:T(8,128)(2,1)} %bitcast.61, bf16[1024,256]{1,0:T(8,128)(2,1)} %bitcast.63, bf16[256,1024]{1,0:T(8,128)(2,1)} %bitcast.65), custom_call_target="tpu_custom_call" | custom-call | bytes 3145728 | tf_op jit(solution)/shard_map/pallas_call | solution.py:162
  4.6 6.6 %collective-permute-start.1 = (bf16[3,1024,256]{2,1,0:T(8,128)(2,1)}, bf16[3,1024,256]{2,1,0:T(8,128)(2,1)S(1)}, u32[]{:S(2)}, u32[]{:S(2)}) collective-permute-start(bf16[3,1024,256]{2,1,0:T(8,128)(2,1)} %shard_map.110), channel_id=1, source_target_pairs={{0,8},{8,0},{1,9},{9,1},{2,10},{10,2},{3,11},{11,3},{4,12},{12,4},... | collective-permute-start | bytes 4718600 | tf_op jit(solution)/shard_map/ppermute | solution.py:170
  11.2 0.0 copy-done.2
  11.2 0.1 convert_reduce_fusion.2
  11.3 0.1 reshape.187
  11.4 0.1 copy.26
  11.5 0.1 add.95
  11.6 0.1 iota_add_fusion
  11.7 1.2 select_reduce_fusion
  13.0 0.1 sub.38
  13.0 0.0 collective-permute-done
  13.1 0.9 fusion.3
  14.0 29.3 %all-to-all-start = ((bf16[64,8,128]{2,1,0:T(8,128)(2,1)}), bf16[64,8,128]{2,1,0:T(8,128)(2,1)S(1)}, u32[]{:S(2)}, u32[]{:S(2)}) async-start(bf16[64,8,128]{2,1,0:T(8,128)(2,1)} %fusion.3), calls=%async_computation | async-start | bytes 262144 | tf_op jit(solution)/shard_map/all_to_all | solution.py:189
  43.3 0.2 convert_reduce_fusion.1
  43.6 0.1 iota_compare_fusion.1
  43.7 28.8 %all-to-all-done = bf16[64,8,128]{2,1,0:T(8,128)(2,1)S(1)} async-done(((bf16[64,8,128]{2,1,0:T(8,128)(2,1)}), bf16[64,8,128]{2,1,0:T(8,128)(2,1)S(1)}, u32[]{:S(2)}, u32[]{:S(2)}) %all-to-all-start) | async-done | bytes 131104 | tf_op jit(solution)/shard_map/all_to_all | solution.py:189
  72.5 0.0 collective-permute-done.1.far_ref
  72.5 0.0 copy-start.1
  72.6 0.2 convolution_convert_fusion.7
  72.8 0.2 convolution_convert_fusion.6
  73.0 0.1 copy.28
  73.1 0.8 broadcast_in_dim.64
  74.0 9.0 %all-to-all-start.1 = ((bf16[16,64,256]{2,1,0:T(8,128)(2,1)}), bf16[16,64,256]{2,1,0:T(8,128)(2,1)S(1)}, u32[]{:S(2)}, u32[]{:S(2)}) async-start(bf16[16,64,256]{2,1,0:T(8,128)(2,1)} %bitcast.16), calls=%async_computation.1 | async-start | bytes 1048576 | tf_op jit(solution)/shard_map/all_to_all | solution.py:211
  83.0 0.0 copy-done
  83.0 0.1 dynamic-slice_bitcast_fusion.1
  83.1 0.1 copy.29.weight_ref
  83.2 9.7 %all-to-all-done.1.rows_ref = bf16[16,64,256]{2,1,0:T(8,128)(2,1)S(1)} async-done(((bf16[16,64,256]{2,1,0:T(8,128)(2,1)}), bf16[16,64,256]{2,1,0:T(8,128)(2,1)S(1)}, u32[]{:S(2)}, u32[]{:S(2)}) %all-to-all-start.1) | async-done | bytes 524320 | tf_op jit(solution)/shard_map/all_to_all | solution.py:211
  92.9 0.0 copy-done.1
  92.9 4.6 %shard_map.111 = (bf16[32,48,128]{2,1,0:T(8,128)(2,1)}, bf16[64,2816]{1,0:T(8,128)(2,1)S(1)}, bf16[64,2816]{1,0:T(8,128)(2,1)S(1)}) custom-call(s32[1]{0:T(128)} %bitcast.6.q_ref, f32[64,1]{1,0:T(8,128)S(1)} %copy.29.weight_ref, bf16[16,64,256]{2,1,0:T(8,128)(2,1)S(1)} %all-to-all-done.1.rows_ref, bf16[1024,256]{1,0:T(8,128)(2,1)} %bitcast.62, ...), custom_call_target="tpu_custom_call" | custom-call | flops 335544320 | bytes 5242880 | tf_op jit(solution)/shard_map/pallas_call | solution.py:223
  97.5 4.6 %all-to-all-start.2 = ((bf16[32,48,128]{2,1,0:T(8,128)(2,1)}), bf16[32,48,128]{2,1,0:T(8,128)(2,1)S(1)}, u32[]{:S(2)}, u32[]{:S(2)}) async-start(bf16[32,48,128]{2,1,0:T(8,128)(2,1)} %get-tuple-element.13), calls=%async_computation.2 | async-start | bytes 786432 | tf_op jit(solution)/shard_map/all_to_all | solution.py:245
  102.1 0.1 iota_compare_fusion.2
  102.3 10.1 %all-to-all-done.2 = bf16[32,48,128]{2,1,0:T(8,128)(2,1)S(1)} async-done(((bf16[32,48,128]{2,1,0:T(8,128)(2,1)}), bf16[32,48,128]{2,1,0:T(8,128)(2,1)S(1)}, u32[]{:S(2)}, u32[]{:S(2)}) %all-to-all-start.2) | async-done | bytes 393248 | tf_op jit(solution)/shard_map/all_to_all | solution.py:245
  112.4 0.1 convert_reduce_fusion
  112.5 0.1 reshape.179
  112.7 0.2 convolution_convert_fusion.5
  112.9 0.2 convolution_convert_fusion.4
  113.1 0.7 copy.32
  113.9 3.9 %all-to-all-start.3 = ((bf16[32,8,128]{2,1,0:T(8,128)(2,1)}), bf16[32,8,128]{2,1,0:T(8,128)(2,1)S(1)}, u32[]{:S(2)}, u32[]{:S(2)}) async-start(bf16[32,8,128]{2,1,0:T(8,128)(2,1)} %bitcast.22), calls=%async_computation.3 | async-start | bytes 131072 | tf_op jit(solution)/shard_map/all_to_all | solution.py:265
  117.7 0.1 slice_add_fusion
  117.8 0.6 reshape.182
  118.4 10.3 %all-gather = bf16[128,2816]{1,0:T(8,128)(2,1)S(1)} all-gather(bf16[64,2816]{1,0:T(8,128)(2,1)S(1)} %get-tuple-element.16), channel_id=2, replica_groups=mesh['z'=32,'p'=2,'q'=2,'x'=4,'c'=2] {'q'}, dimensions={0}, use_global_device_ids=true | all-gather | bytes 1081344 | tf_op jit(solution)/shard_map/all_gather | solution.py:277
  128.8 1.1 fusion.2
  129.9 1.1 fusion.1
  131.0 1.1 fusion
  132.1 10.2 %all-to-all-done.3 = bf16[32,8,128]{2,1,0:T(8,128)(2,1)S(1)} async-done(((bf16[32,8,128]{2,1,0:T(8,128)(2,1)}), bf16[32,8,128]{2,1,0:T(8,128)(2,1)S(1)}, u32[]{:S(2)}, u32[]{:S(2)}) %all-to-all-start.3) | async-done | bytes 65568 | tf_op jit(solution)/shard_map/all_to_all | solution.py:265
  142.3 0.2 fusion.8
  142.5 0.9 fusion.4
  (17 shorter events, 0.2 us)
Async XLA Ops:
  0.6 82.4 %copy-start = (f32[2,128]{1,0:T(2,128)S(1)}, f32[2,128]{1,0:T(2,128)}, u32[]{:S(2)}) copy-start(f32[2,128]{1,0:T(2,128)} %param.12) | copy-start | bytes 3076
  1.4 11.7 %collective-permute-start = (bf16[128,128]{0,1:T(8,128)(2,1)S(1)}, bf16[128,128]{0,1:T(8,128)(2,1)S(1)}, u32[]{:S(2)}, u32[]{:S(2)}) collective-permute-start(bf16[128,128]{0,1:T(8,128)(2,1)S(1)} %pad_maximum_fusion.4), channel_id=1, source_target_pairs={{0,0},{8,16},{16,8},{24,24},{1,1},{9,17},{17,9},{25,25},{2,2},{10,... | collective-permute-start | bytes 98312 | tf_op jit(solution)/shard_map/ppermute | solution.py:158
  2.0 9.2 %copy-start.2 = (s32[64,128]{1,0:T(8,128)S(1)}, s32[64,128]{1,0:T(8,128)}, u32[]{:S(2)}) copy-start(s32[64,128]{1,0:T(8,128)} %param.13) | copy-start | bytes 98308
  4.6 67.9 %collective-permute-start.1 = (bf16[3,1024,256]{2,1,0:T(8,128)(2,1)}, bf16[3,1024,256]{2,1,0:T(8,128)(2,1)S(1)}, u32[]{:S(2)}, u32[]{:S(2)}) collective-permute-start(bf16[3,1024,256]{2,1,0:T(8,128)(2,1)} %shard_map.110), channel_id=1, source_target_pairs={{0,8},{8,0},{1,9},{9,1},{2,10},{10,2},{3,11},{11,3},{4,12},{12,4},... | collective-permute-start | bytes 4718600 | tf_op jit(solution)/shard_map/ppermute | solution.py:170
  14.0 58.6 %all-to-all-start = ((bf16[64,8,128]{2,1,0:T(8,128)(2,1)}), bf16[64,8,128]{2,1,0:T(8,128)(2,1)S(1)}, u32[]{:S(2)}, u32[]{:S(2)}) async-start(bf16[64,8,128]{2,1,0:T(8,128)(2,1)} %fusion.3), calls=%async_computation | async-start | bytes 262144 | tf_op jit(solution)/shard_map/all_to_all | solution.py:189
  72.5 20.4 %copy-start.1 = (bf16[3,1024,256]{2,1,0:T(8,128)(2,1)}, bf16[3,1024,256]{2,1,0:T(8,128)(2,1)S(1)}, u32[]{:S(2)}) copy-start(bf16[3,1024,256]{2,1,0:T(8,128)(2,1)S(1)} %collective-permute-done.1.far_ref) | copy-start | bytes 4718596
  74.0 18.9 %all-to-all-start.1 = ((bf16[16,64,256]{2,1,0:T(8,128)(2,1)}), bf16[16,64,256]{2,1,0:T(8,128)(2,1)S(1)}, u32[]{:S(2)}, u32[]{:S(2)}) async-start(bf16[16,64,256]{2,1,0:T(8,128)(2,1)} %bitcast.16), calls=%async_computation.1 | async-start | bytes 1048576 | tf_op jit(solution)/shard_map/all_to_all | solution.py:211
  97.5 14.9 %all-to-all-start.2 = ((bf16[32,48,128]{2,1,0:T(8,128)(2,1)}), bf16[32,48,128]{2,1,0:T(8,128)(2,1)S(1)}, u32[]{:S(2)}, u32[]{:S(2)}) async-start(bf16[32,48,128]{2,1,0:T(8,128)(2,1)} %get-tuple-element.13), calls=%async_computation.2 | async-start | bytes 786432 | tf_op jit(solution)/shard_map/all_to_all | solution.py:245
  113.9 28.5 %all-to-all-start.3 = ((bf16[32,8,128]{2,1,0:T(8,128)(2,1)}), bf16[32,8,128]{2,1,0:T(8,128)(2,1)S(1)}, u32[]{:S(2)}, u32[]{:S(2)}) async-start(bf16[32,8,128]{2,1,0:T(8,128)(2,1)} %bitcast.22), calls=%async_computation.3 | async-start | bytes 131072 | tf_op jit(solution)/shard_map/all_to_all | solution.py:265

commit v7 on v6

--- a/solution.py
+++ b/solution.py
@@ -157,6 +157,24 @@
     table = jnp.concatenate([x_tokens, cotangent], axis=1)
     table = lax.ppermute(table, ("p", "q"), [(0, 0), (1, 2), (2, 1), (3, 3)])
 
+    slots = jnp.arange(capacity, dtype=jnp.int32)
+    places = jnp.arange(peer, dtype=jnp.int32)
+    tokens = jnp.arange(tok_dev, dtype=jnp.int32)
+    ordered = jnp.transpose(indices.reshape(groups, exp_dev, capacity), (1, 0, 2)).reshape(
+        experts, capacity
+    )
+    base = z * tok_dev
+    start = jnp.sum(((ordered >= 0) & (ordered < base)).astype(jnp.int32), axis=1)
+    want = start[:, None] + places[None, :]
+    shifted = jnp.where(ordered >= 0, ordered - base + 1, 0)
+    chosen = (
+        jnp.sum(jnp.where(slots[None, None, :] == want[:, :, None], shifted[:, None, :], 0), axis=2)
+        - 1
+    )
+    pick = (chosen[:, :, None] == tokens[None, None, :]).astype(bf16)
+    pick = pick.reshape(experts * peer, tok_dev)
+    send = jnp.dot(pick, table, preferred_element_type=f32).astype(bf16)
+    send, *give_weights = lax.optimization_barrier((send, wg, wu, wd))
     swap = [(0, 1), (1, 0)]
     here = pl.BlockSpec(memory_space=pltpu.HBM)
     packed = pl.pallas_call(
@@ -166,26 +184,8 @@
         out_specs=pl.BlockSpec(memory_space=pltpu.VMEM),
         scratch_shapes=[pltpu.SemaphoreType.DMA((6,))],
         cost_estimate=pl.CostEstimate(flops=0, bytes_accessed=3 << 20, transcendentals=0),
-    )(wg, wu, wd)
+    )(*give_weights)
     far = lax.ppermute(packed, "q", swap)
-
-    slots = jnp.arange(capacity, dtype=jnp.int32)
-    places = jnp.arange(peer, dtype=jnp.int32)
-    tokens = jnp.arange(tok_dev, dtype=jnp.int32)
-    ordered = jnp.transpose(indices.reshape(groups, exp_dev, capacity), (1, 0, 2)).reshape(
-        experts, capacity
-    )
-    base = z * tok_dev
-    start = jnp.sum(((ordered >= 0) & (ordered < base)).astype(jnp.int32), axis=1)
-    want = start[:, None] + places[None, :]
-    shifted = jnp.where(ordered >= 0, ordered - base + 1, 0)
-    chosen = (
-        jnp.sum(jnp.where(slots[None, None, :] == want[:, :, None], shifted[:, None, :], 0), axis=2)
-        - 1
-    )
-    pick = (chosen[:, :, None] == tokens[None, None, :]).astype(bf16)
-    pick = pick.reshape(experts * peer, tok_dev)
-    send = jnp.dot(pick, table, preferred_element_type=f32).astype(bf16)
     recv = lax.all_to_all(
         send.reshape(experts, peer, 2 * part), ("p", "z"), split_axis=0, concat_axis=0, tiled=True
     )
@@ -199,7 +199,6 @@
     place = jnp.where(own_block[:, :, None] == cell_block[None, None, :], own_want[:, None, :], -1)
     place = (place == slots[None, :, None]).astype(bf16)
     own_place = lax.dynamic_index_in_dim(place, p, 0, keepdims=False)
-    recv, far = lax.optimization_barrier((recv, far))
     recv = recv.reshape(2, groups * peer, 2 * part)
     taken = [jnp.dot(own_place, recv[i], preferred_element_type=f32).astype(bf16) for i in range(2)]
     compact = jnp.concatenate(
@@ -228,7 +227,7 @@
             held,
         ),
         in_specs=[pl.BlockSpec(memory_space=pltpu.SMEM)] + [vmem] * 2
-        + [here] * 4,
+        + [pl.BlockSpec(memory_space=pl.ANY)] * 4,
         out_specs=(vmem, vmem, vmem),
         scratch_shapes=[
             pltpu.VMEM((2, half_cap, 2 * width), bf16),
@@ -237,7 +236,7 @@
             pltpu.VMEM((2,) + wd.shape, bf16),
             pltpu.SemaphoreType.DMA((5 + width // hidden,)),
         ],
-        compiler_params=pltpu.CompilerParams(vmem_limit_bytes=52 * 1024 * 1024),
+        compiler_params=pltpu.CompilerParams(vmem_limit_bytes=40 * 1024 * 1024),
         cost_estimate=pl.CostEstimate(
             flops=20 * half_cap * width * hidden, bytes_accessed=5 << 20, transcendentals=0
         ),

time: 144 us -> 158 us (1.097)
  starting transfers between devices: 54 us -> 73.7 us
  waiting for transfers between devices: 58.9 us -> 52.5 us
    all_to_all x1, starting transfers between devices: 3.86 us -> 20.7 us  [local(): lax.all_to_all(back.reshape(groups, peer, exp_dev * part), 'z', split_axi...]
    all_to_all x1, waiting for transfers between devices: 28.8 us -> 22.4 us  [local(): lax.all_to_all(send.reshape(experts, peer, 2 * part), ('p', 'z'), split_a...]
    all_to_all x1, starting transfers between devices: 29.3 us -> 33.9 us  [local(): lax.all_to_all(send.reshape(experts, peer, 2 * part), ('p', 'z'), split_a...]
    ppermute x1, starting transfers between devices: 6.58 us -> 2.05 us  [local(): far = lax.ppermute(packed, 'q', swap)]
    all_to_all x1, starting transfers between devices: 4.61 us -> 6.58 us  [local(): lax.all_to_all(piece, ('p', 'q', 'x', 'c'), split_axis=0, concat_axis=0,...]
  transfers between devices with their start and end apart: 6 -> 6, of which waited for: 4 -> 4; matrix products, arithmetic and copies ran while one was open for 5% -> 6% of each run, Pallas kernels for 2% -> 2%
where the time goes in v7:
time: 158 us
  starting transfers between devices  73.7 us (47%)
  waiting for transfers between devices  52.5 us (33%)
  blocking collectives  9.97 us (6%)
  Pallas kernels  7 us (4%)
  matrix products  6.16 us (4%)
  other arithmetic  4.28 us (3%)
  local copies, waits for them, and re-layouts  3.09 us (2%)
    all_to_all x1, starting transfers between devices, local(): lax.all_to_all(send.reshape(experts, peer, 2 * part), ('p', 'z'), split_a...  33.9 us
    all_to_all x1, waiting for transfers between devices, local(): lax.all_to_all(send.reshape(experts, peer, 2 * part), ('p', 'z'), split_a...  22.4 us
    all_to_all x1, starting transfers between devices, local(): lax.all_to_all(back.reshape(groups, peer, exp_dev * part), 'z', split_axi...  20.7 us
    all_to_all x1, waiting for transfers between devices, local(): lax.all_to_all(back.reshape(groups, peer, exp_dev * part), 'z', split_axi...  10.4 us
    all_to_all x1, waiting for transfers between devices, local(): lax.all_to_all(piece, ('p', 'q', 'x', 'c'), split_axis=0, concat_axis=0,...  10 us
    all_gather x1, blocking collectives, local(): got = lax.all_gather(give, 'q', axis=0)  9.97 us
    all_to_all x1, waiting for transfers between devices, local(): lax.all_to_all(spreadout.reshape(2 * spread, half_cap, 4 * part), ('q', '...  9.7 us
    all_to_all x1, starting transfers between devices, local(): lax.all_to_all(spreadout.reshape(2 * spread, half_cap, 4 * part), ('q', '...  9.68 us
  transfers between devices with their start and end apart: 6, of which 4 were waited for; matrix products, arithmetic and copies ran while one was open for 6% of the time, Pallas kernels for 2%

profile of v7, /device:TPU:1, one launch (start us, length us, event | category | flops | bytes accessed | tf_op | source)
XLA Modules:
  0.0 157.6 jit_solution(11715914103743714744)
XLA Ops:
  0.6 0.0 copy-start
  0.6 0.7 pad_maximum_fusion.4
  1.4 0.7 collective-permute-start
  2.1 0.9 convert_reduce_fusion.2
  2.9 0.1 reshape.187
  3.0 0.1 copy.26
  3.1 0.1 add.95
  3.2 0.1 iota_add_fusion
  3.3 1.2 select_reduce_fusion
  4.6 0.1 sub.38
  4.7 0.0 collective-permute-done
  4.7 0.9 convolution_convert_fusion.3
  5.6 33.9 %all-to-all-start = ((bf16[64,8,128]{2,1,0:T(8,128)(2,1)}), bf16[64,8,128]{2,1,0:T(8,128)(2,1)S(1)}, u32[]{:S(2)}, u32[]{:S(2)}) async-start(bf16[64,8,128]{2,1,0:T(8,128)(2,1)} %bitcast.12), calls=%async_computation | async-start | bytes 262144 | tf_op jit(solution)/shard_map/all_to_all | solution.py:189
  39.5 0.7 fusion.22
  40.3 0.2 convert_reduce_fusion.1
  40.5 2.5 %shard_map.110 = bf16[3,1024,256]{2,1,0:T(8,128)(2,1)} custom-call(bf16[1024,256]{1,0:T(8,128)(2,1)} %bitcast.60, bf16[1024,256]{1,0:T(8,128)(2,1)} %bitcast.62, bf16[256,1024]{1,0:T(8,128)(2,1)} %bitcast.64), custom_call_target="tpu_custom_call" | custom-call | bytes 3145728 | tf_op jit(solution)/shard_map/pallas_call | solution.py:180
  43.1 0.0 copy-start.1
  43.1 0.0 copy-start.2
  43.1 0.0 copy-start.3
  43.1 2.1 %collective-permute-start.1 = (bf16[3,1024,256]{2,1,0:T(8,128)(2,1)}, bf16[3,1024,256]{2,1,0:T(8,128)(2,1)}, u32[]{:S(2)}, u32[]{:S(2)}) collective-permute-start(bf16[3,1024,256]{2,1,0:T(8,128)(2,1)} %shard_map.110), channel_id=1, source_target_pairs={{0,8},{8,0},{1,9},{9,1},{2,10},{10,2},{3,11},{11,3},{4,12},{12,4},... | collective-permute-start | bytes 4718600 | tf_op jit(solution)/shard_map/ppermute | solution.py:188
  45.1 0.1 iota_compare_fusion.1
  45.3 22.4 %all-to-all-done = bf16[64,8,128]{2,1,0:T(8,128)(2,1)S(1)} async-done(((bf16[64,8,128]{2,1,0:T(8,128)(2,1)}), bf16[64,8,128]{2,1,0:T(8,128)(2,1)S(1)}, u32[]{:S(2)}, u32[]{:S(2)}) %all-to-all-start) | async-done | bytes 131104 | tf_op jit(solution)/shard_map/all_to_all | solution.py:189
  67.6 0.2 convolution_convert_fusion.7
  67.9 0.2 convolution_convert_fusion.6
  68.1 0.1 copy.28
  68.2 0.8 broadcast_in_dim.64
  69.1 9.7 %all-to-all-start.1 = ((bf16[16,64,256]{2,1,0:T(8,128)(2,1)}), bf16[16,64,256]{2,1,0:T(8,128)(2,1)S(1)}, u32[]{:S(2)}, u32[]{:S(2)}) async-start(bf16[16,64,256]{2,1,0:T(8,128)(2,1)} %bitcast.16), calls=%async_computation.1 | async-start | bytes 1048576 | tf_op jit(solution)/shard_map/all_to_all | solution.py:210
  78.8 0.0 copy-done
  78.8 0.1 dynamic-slice_bitcast_fusion.1
  78.8 0.1 copy.29.weight_ref
  78.9 9.7 %all-to-all-done.1.rows_ref = bf16[16,64,256]{2,1,0:T(8,128)(2,1)S(1)} async-done(((bf16[16,64,256]{2,1,0:T(8,128)(2,1)}), bf16[16,64,256]{2,1,0:T(8,128)(2,1)S(1)}, u32[]{:S(2)}, u32[]{:S(2)}) %all-to-all-start.1) | async-done | bytes 524320 | tf_op jit(solution)/shard_map/all_to_all | solution.py:210
  88.7 0.0 collective-permute-done.1.far_ref
  88.7 0.0 copy-done.1
  88.7 0.0 copy-done.2
  88.7 0.0 copy-done.3
  88.7 4.5 %shard_map.111 = (bf16[32,48,128]{2,1,0:T(8,128)(2,1)}, bf16[64,2816]{1,0:T(8,128)(2,1)S(1)}, bf16[64,2816]{1,0:T(8,128)(2,1)S(1)}) custom-call(s32[1]{0:T(128)} %bitcast.6.q_ref, f32[64,1]{1,0:T(8,128)S(1)} %copy.29.weight_ref, bf16[16,64,256]{2,1,0:T(8,128)(2,1)S(1)} %all-to-all-done.1.rows_ref, bf16[1024,256]{1,0:T(8,128)(2,1)S(1)} %bitcast.61, ...), custom_call_target="tpu_custom_call" | custom-call | flops 335544320 | bytes 5242880 | tf_op jit(solution)/shard_map/pallas_call | solution.py:222
  93.1 6.6 %all-to-all-start.2 = ((bf16[32,48,128]{2,1,0:T(8,128)(2,1)}), bf16[32,48,128]{2,1,0:T(8,128)(2,1)S(1)}, u32[]{:S(2)}, u32[]{:S(2)}) async-start(bf16[32,48,128]{2,1,0:T(8,128)(2,1)} %get-tuple-element.17), calls=%async_computation.2 | async-start | bytes 786432 | tf_op jit(solution)/shard_map/all_to_all | solution.py:244
  99.7 0.1 iota_compare_fusion.2
  99.9 10.0 %all-to-all-done.2 = bf16[32,48,128]{2,1,0:T(8,128)(2,1)S(1)} async-done(((bf16[32,48,128]{2,1,0:T(8,128)(2,1)}), bf16[32,48,128]{2,1,0:T(8,128)(2,1)S(1)}, u32[]{:S(2)}, u32[]{:S(2)}) %all-to-all-start.2) | async-done | bytes 393248 | tf_op jit(solution)/shard_map/all_to_all | solution.py:244
  109.9 0.1 convert_reduce_fusion
  110.0 0.1 reshape.179
  110.1 0.2 convolution_convert_fusion.5
  110.4 0.2 convolution_convert_fusion.4
  110.6 0.7 copy.32
  111.3 20.7 %all-to-all-start.3 = ((bf16[32,8,128]{2,1,0:T(8,128)(2,1)}), bf16[32,8,128]{2,1,0:T(8,128)(2,1)S(1)}, u32[]{:S(2)}, u32[]{:S(2)}) async-start(bf16[32,8,128]{2,1,0:T(8,128)(2,1)} %bitcast.22), calls=%async_computation.3 | async-start | bytes 131072 | tf_op jit(solution)/shard_map/all_to_all | solution.py:264
  132.1 0.1 slice_add_fusion
  132.1 0.6 reshape.182
  132.8 10.0 %all-gather = bf16[128,2816]{1,0:T(8,128)(2,1)S(1)} all-gather(bf16[64,2816]{1,0:T(8,128)(2,1)S(1)} %get-tuple-element.20), channel_id=2, replica_groups=mesh['z'=32,'p'=2,'q'=2,'x'=4,'c'=2] {'q'}, dimensions={0}, use_global_device_ids=true | all-gather | bytes 1081344 | tf_op jit(solution)/shard_map/all_gather | solution.py:276
  142.8 1.1 fusion.2
  143.9 1.1 fusion.1
  145.0 1.1 fusion
  146.1 10.4 %all-to-all-done.3 = bf16[32,8,128]{2,1,0:T(8,128)(2,1)S(1)} async-done(((bf16[32,8,128]{2,1,0:T(8,128)(2,1)}), bf16[32,8,128]{2,1,0:T(8,128)(2,1)S(1)}, u32[]{:S(2)}, u32[]{:S(2)}) %all-to-all-start.3) | async-done | bytes 65568 | tf_op jit(solution)/shard_map/all_to_all | solution.py:264
  156.5 0.2 fusion.7
  156.7 0.9 fusion.3
  (16 shorter events, 0.2 us)
Async XLA Ops:
  0.6 78.1 %copy-start = (f32[2,128]{1,0:T(2,128)S(1)}, f32[2,128]{1,0:T(2,128)}, u32[]{:S(2)}) copy-start(f32[2,128]{1,0:T(2,128)} %param.12) | copy-start | bytes 3076
  1.4 3.3 %collective-permute-start = (bf16[128,128]{0,1:T(8,128)(2,1)S(1)}, bf16[128,128]{0,1:T(8,128)(2,1)S(1)}, u32[]{:S(2)}, u32[]{:S(2)}) collective-permute-start(bf16[128,128]{0,1:T(8,128)(2,1)S(1)} %pad_maximum_fusion.4), channel_id=1, source_target_pairs={{0,0},{8,16},{16,8},{24,24},{1,1},{9,17},{17,9},{25,25},{2,2},{10,... | collective-permute-start | bytes 98312 | tf_op jit(solution)/shard_map/ppermute | solution.py:158
  5.6 62.1 %all-to-all-start = ((bf16[64,8,128]{2,1,0:T(8,128)(2,1)}), bf16[64,8,128]{2,1,0:T(8,128)(2,1)S(1)}, u32[]{:S(2)}, u32[]{:S(2)}) async-start(bf16[64,8,128]{2,1,0:T(8,128)(2,1)} %bitcast.12), calls=%async_computation | async-start | bytes 262144 | tf_op jit(solution)/shard_map/all_to_all | solution.py:189
  43.1 45.6 %copy-start.1 = (bf16[1,1024,256]{2,1,0:T(8,128)(2,1)S(1)}, bf16[1,1024,256]{2,1,0:T(8,128)(2,1)}, u32[]{:S(2)}) copy-start(bf16[1,1024,256]{2,1,0:T(8,128)(2,1)} %param.9) | copy-start | bytes 1572868
  43.1 45.6 %copy-start.2 = (bf16[1,1024,256]{2,1,0:T(8,128)(2,1)S(1)}, bf16[1,1024,256]{2,1,0:T(8,128)(2,1)}, u32[]{:S(2)}) copy-start(bf16[1,1024,256]{2,1,0:T(8,128)(2,1)} %param.10) | copy-start | bytes 1572868
  43.1 45.6 %copy-start.3 = (bf16[1,256,1024]{2,1,0:T(8,128)(2,1)S(1)}, bf16[1,256,1024]{2,1,0:T(8,128)(2,1)}, u32[]{:S(2)}) copy-start(bf16[1,256,1024]{2,1,0:T(8,128)(2,1)} %param.11) | copy-start | bytes 1572868
  43.1 45.6 %collective-permute-start.1 = (bf16[3,1024,256]{2,1,0:T(8,128)(2,1)}, bf16[3,1024,256]{2,1,0:T(8,128)(2,1)}, u32[]{:S(2)}, u32[]{:S(2)}) collective-permute-start(bf16[3,1024,256]{2,1,0:T(8,128)(2,1)} %shard_map.110), channel_id=1, source_target_pairs={{0,8},{8,0},{1,9},{9,1},{2,10},{10,2},{3,11},{11,3},{4,12},{12,4},... | collective-permute-start | bytes 4718600 | tf_op jit(solution)/shard_map/ppermute | solution.py:188
  69.1 19.6 %all-to-all-start.1 = ((bf16[16,64,256]{2,1,0:T(8,128)(2,1)}), bf16[16,64,256]{2,1,0:T(8,128)(2,1)S(1)}, u32[]{:S(2)}, u32[]{:S(2)}) async-start(bf16[16,64,256]{2,1,0:T(8,128)(2,1)} %bitcast.16), calls=%async_computation.1 | async-start | bytes 1048576 | tf_op jit(solution)/shard_map/all_to_all | solution.py:210
  93.1 16.8 %all-to-all-start.2 = ((bf16[32,48,128]{2,1,0:T(8,128)(2,1)}), bf16[32,48,128]{2,1,0:T(8,128)(2,1)S(1)}, u32[]{:S(2)}, u32[]{:S(2)}) async-start(bf16[32,48,128]{2,1,0:T(8,128)(2,1)} %get-tuple-element.17), calls=%async_computation.2 | async-start | bytes 786432 | tf_op jit(solution)/shard_map/all_to_all | solution.py:244
  111.3 45.2 %all-to-all-start.3 = ((bf16[32,8,128]{2,1,0:T(8,128)(2,1)}), bf16[32,8,128]{2,1,0:T(8,128)(2,1)S(1)}, u32[]{:S(2)}, u32[]{:S(2)}) async-start(bf16[32,8,128]{2,1,0:T(8,128)(2,1)} %bitcast.22), calls=%async_computation.3 | async-start | bytes 131072 | tf_op jit(solution)/shard_map/all_to_all | solution.py:264

commit v8 on v6

--- a/solution.py
+++ b/solution.py
@@ -122,7 +122,7 @@
         ref[:, pl.ds(2 * width + 2 * hidden, hidden)] = d_up
 
 
-def pack(wg_ref, wu_ref, wd_ref, out_ref, sem):
+def prepare(base_ref, indices_ref, wg_ref, wu_ref, wd_ref, out_ref, pick_ref, sem):
     chunk = wg_ref.shape[1]
     pairs = [(wg_ref, out_ref.at[0]), (wu_ref, out_ref.at[1])] + [
         (wd_ref.at[:, pl.ds(i * chunk, chunk)], out_ref.at[2, pl.ds(i * chunk, chunk)])
@@ -134,6 +134,23 @@
     ]
     for copy in copies:
         copy.start()
+    f32 = jnp.float32
+    experts, capacity = indices_ref.shape
+    groups = experts // 2
+    peer = pick_ref.shape[0] // experts
+    base = base_ref[0]
+    lane = lax.broadcasted_iota(jnp.int32, (groups, capacity), 1).astype(f32)
+    for member in range(2):
+        tokens = indices_ref[pl.ds(member, groups, stride=2), :]
+        live = tokens >= 0
+        before = jnp.where(live & (tokens < base), 1.0, 0.0)
+        start = jnp.sum(before, axis=1, keepdims=True)
+        shifted = jnp.where(live, tokens - base + 1, 0).astype(f32)
+        for place in range(peer):
+            at_place = jnp.where(lane == start + place, shifted, 0.0)
+            chosen = jnp.sum(at_place, axis=1, keepdims=True) - 1.0
+            rows = pl.ds(member * groups * peer + place, groups, stride=peer)
+            pick_ref[rows, :] = jnp.where(lane == chosen, 1.0, 0.0)
     for copy in copies:
         copy.wait()
 
@@ -159,32 +176,23 @@
 
     swap = [(0, 1), (1, 0)]
     here = pl.BlockSpec(memory_space=pltpu.HBM)
-    packed = pl.pallas_call(
-        pack,
-        out_shape=jax.ShapeDtypeStruct((3,) + wg.shape, bf16),
-        in_specs=[here] * 3,
-        out_specs=pl.BlockSpec(memory_space=pltpu.VMEM),
+    whole = pl.BlockSpec(memory_space=pltpu.VMEM)
+    packed, pick = pl.pallas_call(
+        prepare,
+        out_shape=(
+            jax.ShapeDtypeStruct((3,) + wg.shape, bf16),
+            jax.ShapeDtypeStruct((experts * peer, tok_dev), f32),
+        ),
+        in_specs=[pl.BlockSpec(memory_space=pltpu.SMEM), whole] + [here] * 3,
+        out_specs=(whole, whole),
         scratch_shapes=[pltpu.SemaphoreType.DMA((6,))],
         cost_estimate=pl.CostEstimate(flops=0, bytes_accessed=3 << 20, transcendentals=0),
-    )(wg, wu, wd)
+    )((z * tok_dev).reshape(1), indices, wg, wu, wd)
+    pick = pick.astype(bf16)
+    packed, table = lax.optimization_barrier((packed, table))
     far = lax.ppermute(packed, "q", swap)
 
     slots = jnp.arange(capacity, dtype=jnp.int32)
-    places = jnp.arange(peer, dtype=jnp.int32)
-    tokens = jnp.arange(tok_dev, dtype=jnp.int32)
-    ordered = jnp.transpose(indices.reshape(groups, exp_dev, capacity), (1, 0, 2)).reshape(
-        experts, capacity
-    )
-    base = z * tok_dev
-    start = jnp.sum(((ordered >= 0) & (ordered < base)).astype(jnp.int32), axis=1)
-    want = start[:, None] + places[None, :]
-    shifted = jnp.where(ordered >= 0, ordered - base + 1, 0)
-    chosen = (
-        jnp.sum(jnp.where(slots[None, None, :] == want[:, :, None], shifted[:, None, :], 0), axis=2)
-        - 1
-    )
-    pick = (chosen[:, :, None] == tokens[None, None, :]).astype(bf16)
-    pick = pick.reshape(experts * peer, tok_dev)
     send = jnp.dot(pick, table, preferred_element_type=f32).astype(bf16)
     recv = lax.all_to_all(
         send.reshape(experts, peer, 2 * part), ("p", "z"), split_axis=0, concat_axis=0, tiled=True

time: 144 us -> 144 us (level)
  no operation moved by 1% of the time
where the time goes in v8:
time: 144 us; the launch traced here: 143 us
  waiting for transfers between devices  58.4 us (41%)
  starting transfers between devices  54 us (38%)
  blocking collectives  10.3 us (7%)
  Pallas kernels  7.96 us (6%)
  matrix products  6.09 us (4%)
  other arithmetic  2.92 us (2%)
  local copies, waits for them, and re-layouts  2.71 us (2%)
    all_to_all x1, starting transfers between devices, local(): lax.all_to_all(send.reshape(experts, peer, 2 * part), ('p', 'z'), split_a...  29.3 us
    all_to_all x1, waiting for transfers between devices, local(): lax.all_to_all(send.reshape(experts, peer, 2 * part), ('p', 'z'), split_a...  28.2 us
    all_gather x1, blocking collectives, local(): got = lax.all_gather(give, 'q', axis=0)  10.3 us
    all_to_all x1, waiting for transfers between devices, local(): lax.all_to_all(piece, ('p', 'q', 'x', 'c'), split_axis=0, concat_axis=0,...  10.3 us
    all_to_all x1, waiting for transfers between devices, local(): lax.all_to_all(back.reshape(groups, peer, exp_dev * part), 'z', split_axi...  10.2 us
    all_to_all x1, waiting for transfers between devices, local(): lax.all_to_all(spreadout.reshape(2 * spread, half_cap, 4 * part), ('q', '...  9.7 us
    all_to_all x1, starting transfers between devices, local(): lax.all_to_all(spreadout.reshape(2 * spread, half_cap, 4 * part), ('q', '...  9.04 us
    ppermute x1, starting transfers between devices, local(): far = lax.ppermute(packed, 'q', swap)  6.58 us
  transfers between devices with their start and end apart: 6, of which 4 were waited for; matrix products, arithmetic and copies ran while one was open for 5% of the time, Pallas kernels for 2%

profile of v8, /device:TPU:1, one launch (start us, length us, event | category | flops | bytes accessed | tf_op | source)
XLA Modules:
  0.0 143.2 jit_solution(8837212626238367476)
XLA Ops:
  0.6 0.0 copy-start
  0.6 0.7 pad_maximum_fusion.4
  1.4 0.7 collective-permute-start
  2.1 3.4 %shard_map.110 = (bf16[3,1024,256]{2,1,0:T(8,128)(2,1)}, f32[512,128]{1,0:T(8,128)}) custom-call(s32[1]{0:T(128)} %bitcast.base_ref, s32[64,128]{1,0:T(8,128)} %indices_ref.1, bf16[1024,256]{1,0:T(8,128)(2,1)} %bitcast.52, bf16[1024,256]{1,0:T(8,128)(2,1)} %bitcast.54, bf16[256,1024]{1,0:T(8,128)(2,1)} %bitcast.56), custom_call_target="tpu_custom_call" | custom-call | bytes 3145728 | tf_op jit(solution)/shard_map/pallas_call | solution.py:180
  5.4 0.0 collective-permute-done
  5.5 6.6 %collective-permute-start.1 = (bf16[3,1024,256]{2,1,0:T(8,128)(2,1)}, bf16[3,1024,256]{2,1,0:T(8,128)(2,1)S(1)}, u32[]{:S(2)}, u32[]{:S(2)}) collective-permute-start(bf16[3,1024,256]{2,1,0:T(8,128)(2,1)} %get-tuple-element.18), channel_id=1, source_target_pairs={{0,8},{8,0},{1,9},{9,1},{2,10},{10,2},{3,11},{11,3},{4,12},{12,4},... | collective-permute-start | bytes 4718600 | tf_op jit(solution)/shard_map/ppermute | solution.py:193
  12.0 1.0 convert_element_type.41
  13.0 0.8 fusion.3
  13.9 29.3 %all-to-all-start = ((bf16[64,8,128]{2,1,0:T(8,128)(2,1)}), bf16[64,8,128]{2,1,0:T(8,128)(2,1)S(1)}, u32[]{:S(2)}, u32[]{:S(2)}) async-start(bf16[64,8,128]{2,1,0:T(8,128)(2,1)} %fusion.3), calls=%async_computation | async-start | bytes 262144 | tf_op jit(solution)/shard_map/all_to_all | solution.py:197
  43.2 0.7 fusion.28
  43.9 0.2 convert_reduce_fusion.1
  44.1 0.1 iota_compare_fusion
  44.3 28.2 %all-to-all-done = bf16[64,8,128]{2,1,0:T(8,128)(2,1)S(1)} async-done(((bf16[64,8,128]{2,1,0:T(8,128)(2,1)}), bf16[64,8,128]{2,1,0:T(8,128)(2,1)S(1)}, u32[]{:S(2)}, u32[]{:S(2)}) %all-to-all-start) | async-done | bytes 131104 | tf_op jit(solution)/shard_map/all_to_all | solution.py:197
  72.4 0.0 collective-permute-done.1.far_ref
  72.4 0.0 copy-start.1
  72.4 0.2 convolution_convert_fusion.7
  72.7 0.2 convolution_convert_fusion.6
  72.9 0.1 copy.22
  73.0 0.8 broadcast_in_dim.41
  73.9 9.0 %all-to-all-start.1 = ((bf16[16,64,256]{2,1,0:T(8,128)(2,1)}), bf16[16,64,256]{2,1,0:T(8,128)(2,1)S(1)}, u32[]{:S(2)}, u32[]{:S(2)}) async-start(bf16[16,64,256]{2,1,0:T(8,128)(2,1)} %bitcast.12), calls=%async_computation.1 | async-start | bytes 1048576 | tf_op jit(solution)/shard_map/all_to_all | solution.py:219
  82.9 0.0 copy-done
  82.9 0.1 dynamic-slice_bitcast_fusion.1
  83.0 0.1 copy.23.weight_ref
  83.1 9.7 %all-to-all-done.1.rows_ref = bf16[16,64,256]{2,1,0:T(8,128)(2,1)S(1)} async-done(((bf16[16,64,256]{2,1,0:T(8,128)(2,1)}), bf16[16,64,256]{2,1,0:T(8,128)(2,1)S(1)}, u32[]{:S(2)}, u32[]{:S(2)}) %all-to-all-start.1) | async-done | bytes 524320 | tf_op jit(solution)/shard_map/all_to_all | solution.py:219
  92.8 0.0 copy-done.1
  92.8 4.6 %shard_map.111 = (bf16[32,48,128]{2,1,0:T(8,128)(2,1)}, bf16[64,2816]{1,0:T(8,128)(2,1)S(1)}, bf16[64,2816]{1,0:T(8,128)(2,1)S(1)}) custom-call(s32[1]{0:T(128)} %bitcast.5.q_ref, f32[64,1]{1,0:T(8,128)S(1)} %copy.23.weight_ref, bf16[16,64,256]{2,1,0:T(8,128)(2,1)S(1)} %all-to-all-done.1.rows_ref, bf16[1024,256]{1,0:T(8,128)(2,1)} %bitcast.53, ...), custom_call_target="tpu_custom_call" | custom-call | flops 335544320 | bytes 5242880 | tf_op jit(solution)/shard_map/pallas_call | solution.py:231
  97.4 4.6 %all-to-all-start.2 = ((bf16[32,48,128]{2,1,0:T(8,128)(2,1)}), bf16[32,48,128]{2,1,0:T(8,128)(2,1)S(1)}, u32[]{:S(2)}, u32[]{:S(2)}) async-start(bf16[32,48,128]{2,1,0:T(8,128)(2,1)} %get-tuple-element.21), calls=%async_computation.2 | async-start | bytes 786432 | tf_op jit(solution)/shard_map/all_to_all | solution.py:253
  102.0 10.3 %all-to-all-done.2 = bf16[32,48,128]{2,1,0:T(8,128)(2,1)S(1)} async-done(((bf16[32,48,128]{2,1,0:T(8,128)(2,1)}), bf16[32,48,128]{2,1,0:T(8,128)(2,1)S(1)}, u32[]{:S(2)}, u32[]{:S(2)}) %all-to-all-start.2) | async-done | bytes 393248 | tf_op jit(solution)/shard_map/all_to_all | solution.py:253
  112.3 0.1 convert_reduce_fusion
  112.4 0.1 reshape.117
  112.6 0.2 convolution_convert_fusion.5
  112.8 0.2 convolution_convert_fusion.4
  113.0 0.7 copy.26
  113.7 3.8 %all-to-all-start.3 = ((bf16[32,8,128]{2,1,0:T(8,128)(2,1)}), bf16[32,8,128]{2,1,0:T(8,128)(2,1)S(1)}, u32[]{:S(2)}, u32[]{:S(2)}) async-start(bf16[32,8,128]{2,1,0:T(8,128)(2,1)} %bitcast.18), calls=%async_computation.3 | async-start | bytes 131072 | tf_op jit(solution)/shard_map/all_to_all | solution.py:273
  117.6 0.1 slice_add_fusion
  117.6 0.6 reshape.120
  118.3 10.3 %all-gather = bf16[128,2816]{1,0:T(8,128)(2,1)S(1)} all-gather(bf16[64,2816]{1,0:T(8,128)(2,1)S(1)} %get-tuple-element.24), channel_id=2, replica_groups=mesh['z'=32,'p'=2,'q'=2,'x'=4,'c'=2] {'q'}, dimensions={0}, use_global_device_ids=true | all-gather | bytes 1081344 | tf_op jit(solution)/shard_map/all_gather | solution.py:285
  128.6 1.1 fusion.2
  129.7 1.1 fusion.1
  130.8 1.1 fusion
  132.0 10.2 %all-to-all-done.3 = bf16[32,8,128]{2,1,0:T(8,128)(2,1)S(1)} async-done(((bf16[32,8,128]{2,1,0:T(8,128)(2,1)}), bf16[32,8,128]{2,1,0:T(8,128)(2,1)S(1)}, u32[]{:S(2)}, u32[]{:S(2)}) %all-to-all-start.3) | async-done | bytes 65568 | tf_op jit(solution)/shard_map/all_to_all | solution.py:273
  142.2 0.2 fusion.19
  142.4 0.9 fusion.4
  (14 shorter events, 0.1 us)
Async XLA Ops:
  0.6 82.3 %copy-start = (f32[2,128]{1,0:T(2,128)S(1)}, f32[2,128]{1,0:T(2,128)}, u32[]{:S(2)}) copy-start(f32[2,128]{1,0:T(2,128)} %param.12) | copy-start | bytes 3076
  1.4 4.1 %collective-permute-start = (bf16[128,128]{0,1:T(8,128)(2,1)S(1)}, bf16[128,128]{0,1:T(8,128)(2,1)S(1)}, u32[]{:S(2)}, u32[]{:S(2)}) collective-permute-start(bf16[128,128]{0,1:T(8,128)(2,1)S(1)} %pad_maximum_fusion.4), channel_id=1, source_target_pairs={{0,0},{8,16},{16,8},{24,24},{1,1},{9,17},{17,9},{25,25},{2,2},{10,... | collective-permute-start | bytes 98312 | tf_op jit(solution)/shard_map/ppermute | solution.py:175
  5.5 67.0 %collective-permute-start.1 = (bf16[3,1024,256]{2,1,0:T(8,128)(2,1)}, bf16[3,1024,256]{2,1,0:T(8,128)(2,1)S(1)}, u32[]{:S(2)}, u32[]{:S(2)}) collective-permute-start(bf16[3,1024,256]{2,1,0:T(8,128)(2,1)} %get-tuple-element.18), channel_id=1, source_target_pairs={{0,8},{8,0},{1,9},{9,1},{2,10},{10,2},{3,11},{11,3},{4,12},{12,4},... | collective-permute-start | bytes 4718600 | tf_op jit(solution)/shard_map/ppermute | solution.py:193
  13.9 58.6 %all-to-all-start = ((bf16[64,8,128]{2,1,0:T(8,128)(2,1)}), bf16[64,8,128]{2,1,0:T(8,128)(2,1)S(1)}, u32[]{:S(2)}, u32[]{:S(2)}) async-start(bf16[64,8,128]{2,1,0:T(8,128)(2,1)} %fusion.3), calls=%async_computation | async-start | bytes 262144 | tf_op jit(solution)/shard_map/all_to_all | solution.py:197
  72.4 20.4 %copy-start.1 = (bf16[3,1024,256]{2,1,0:T(8,128)(2,1)}, bf16[3,1024,256]{2,1,0:T(8,128)(2,1)S(1)}, u32[]{:S(2)}) copy-start(bf16[3,1024,256]{2,1,0:T(8,128)(2,1)S(1)} %collective-permute-done.1.far_ref) | copy-start | bytes 4718596
  73.9 18.9 %all-to-all-start.1 = ((bf16[16,64,256]{2,1,0:T(8,128)(2,1)}), bf16[16,64,256]{2,1,0:T(8,128)(2,1)S(1)}, u32[]{:S(2)}, u32[]{:S(2)}) async-start(bf16[16,64,256]{2,1,0:T(8,128)(2,1)} %bitcast.12), calls=%async_computation.1 | async-start | bytes 1048576 | tf_op jit(solution)/shard_map/all_to_all | solution.py:219
  97.4 14.9 %all-to-all-start.2 = ((bf16[32,48,128]{2,1,0:T(8,128)(2,1)}), bf16[32,48,128]{2,1,0:T(8,128)(2,1)S(1)}, u32[]{:S(2)}, u32[]{:S(2)}) async-start(bf16[32,48,128]{2,1,0:T(8,128)(2,1)} %get-tuple-element.21), calls=%async_computation.2 | async-start | bytes 786432 | tf_op jit(solution)/shard_map/all_to_all | solution.py:253
  113.7 28.4 %all-to-all-start.3 = ((bf16[32,8,128]{2,1,0:T(8,128)(2,1)}), bf16[32,8,128]{2,1,0:T(8,128)(2,1)S(1)}, u32[]{:S(2)}, u32[]{:S(2)}) async-start(bf16[32,8,128]{2,1,0:T(8,128)(2,1)} %bitcast.18), calls=%async_computation.3 | async-start | bytes 131072 | tf_op jit(solution)/shard_map/all_to_all | solution.py:273

commit v9 on v8

--- a/solution.py
+++ b/solution.py
@@ -122,7 +122,7 @@
         ref[:, pl.ds(2 * width + 2 * hidden, hidden)] = d_up
 
 
-def prepare(base_ref, indices_ref, wg_ref, wu_ref, wd_ref, out_ref, pick_ref, sem):
+def prepare(base_ref, indices_ref, wg_ref, wu_ref, wd_ref, out_ref, pick_ref, wide_ref, sem):
     chunk = wg_ref.shape[1]
     pairs = [(wg_ref, out_ref.at[0]), (wu_ref, out_ref.at[1])] + [
         (wd_ref.at[:, pl.ds(i * chunk, chunk)], out_ref.at[2, pl.ds(i * chunk, chunk)])
@@ -150,7 +150,8 @@
             at_place = jnp.where(lane == start + place, shifted, 0.0)
             chosen = jnp.sum(at_place, axis=1, keepdims=True) - 1.0
             rows = pl.ds(member * groups * peer + place, groups, stride=peer)
-            pick_ref[rows, :] = jnp.where(lane == chosen, 1.0, 0.0)
+            wide_ref[rows, :] = jnp.where(lane == chosen, 1.0, 0.0)
+    pick_ref[...] = wide_ref[...].astype(pick_ref.dtype)
     for copy in copies:
         copy.wait()
 
@@ -181,14 +182,16 @@
         prepare,
         out_shape=(
             jax.ShapeDtypeStruct((3,) + wg.shape, bf16),
-            jax.ShapeDtypeStruct((experts * peer, tok_dev), f32),
+            jax.ShapeDtypeStruct((experts * peer, tok_dev), bf16),
         ),
         in_specs=[pl.BlockSpec(memory_space=pltpu.SMEM), whole] + [here] * 3,
         out_specs=(whole, whole),
-        scratch_shapes=[pltpu.SemaphoreType.DMA((6,))],
+        scratch_shapes=[
+            pltpu.VMEM((experts * peer, tok_dev), f32),
+            pltpu.SemaphoreType.DMA((6,)),
+        ],
         cost_estimate=pl.CostEstimate(flops=0, bytes_accessed=3 << 20, transcendentals=0),
     )((z * tok_dev).reshape(1), indices, wg, wu, wd)
-    pick = pick.astype(bf16)
     packed, table = lax.optimization_barrier((packed, table))
     far = lax.ppermute(packed, "q", swap)
 

time: 144 us -> 144 us (level)
  no operation moved by 1% of the time
where the time goes in v9:
time: 144 us; the launch traced here: 143 us
  waiting for transfers between devices  58.4 us (41%)
  starting transfers between devices  54 us (38%)
  blocking collectives  10.3 us (7%)
  Pallas kernels  7.94 us (6%)
  matrix products  7 us (5%)
  local copies, waits for them, and re-layouts  2.71 us (2%)
  other arithmetic  1.96 us (1%)
    all_to_all x1, starting transfers between devices, local(): lax.all_to_all(send.reshape(experts, peer, 2 * part), ('p', 'z'), split_a...  29.3 us
    all_to_all x1, waiting for transfers between devices, local(): lax.all_to_all(send.reshape(experts, peer, 2 * part), ('p', 'z'), split_a...  28.2 us
    all_gather x1, blocking collectives, local(): got = lax.all_gather(give, 'q', axis=0)  10.3 us
    all_to_all x1, waiting for transfers between devices, local(): lax.all_to_all(piece, ('p', 'q', 'x', 'c'), split_axis=0, concat_axis=0,...  10.3 us
    all_to_all x1, waiting for transfers between devices, local(): lax.all_to_all(back.reshape(groups, peer, exp_dev * part), 'z', split_axi...  10.2 us
    all_to_all x1, waiting for transfers between devices, local(): lax.all_to_all(spreadout.reshape(2 * spread, half_cap, 4 * part), ('q', '...  9.7 us
    all_to_all x1, starting transfers between devices, local(): lax.all_to_all(spreadout.reshape(2 * spread, half_cap, 4 * part), ('q', '...  9.04 us
    ppermute x1, starting transfers between devices, local(): far = lax.ppermute(packed, 'q', swap)  6.58 us
  transfers between devices with their start and end apart: 6, of which 4 were waited for; matrix products, arithmetic and copies ran while one was open for 5% of the time, Pallas kernels for 2%

profile of v9, /device:TPU:1, one launch (start us, length us, event | category | flops | bytes accessed | tf_op | source)
XLA Modules:
  0.0 143.2 jit_solution(17946983528973416039)
XLA Ops:
  0.6 0.0 copy-start
  0.6 0.7 pad_maximum_fusion.4
  1.4 0.7 collective-permute-start
  2.1 3.4 %shard_map.110 = (bf16[3,1024,256]{2,1,0:T(8,128)(2,1)}, bf16[512,128]{1,0:T(8,128)(2,1)}) custom-call(s32[1]{0:T(128)} %bitcast.base_ref, s32[64,128]{1,0:T(8,128)} %indices_ref.1, bf16[1024,256]{1,0:T(8,128)(2,1)} %bitcast.52, bf16[1024,256]{1,0:T(8,128)(2,1)} %bitcast.54, bf16[256,1024]{1,0:T(8,128)(2,1)} %bitcast.56), custom_call_target="tpu_custom_call" | custom-call | bytes 3145728 | tf_op jit(solution)/shard_map/pallas_call | solution.py:181
  5.4 0.0 collective-permute-done
  5.4 6.6 %collective-permute-start.1 = (bf16[3,1024,256]{2,1,0:T(8,128)(2,1)}, bf16[3,1024,256]{2,1,0:T(8,128)(2,1)S(1)}, u32[]{:S(2)}, u32[]{:S(2)}) collective-permute-start(bf16[3,1024,256]{2,1,0:T(8,128)(2,1)} %get-tuple-element.18), channel_id=1, source_target_pairs={{0,8},{8,0},{1,9},{9,1},{2,10},{10,2},{3,11},{11,3},{4,12},{12,4},... | collective-permute-start | bytes 4718600 | tf_op jit(solution)/shard_map/ppermute | solution.py:196
  12.0 1.8 %fusion.3 = bf16[64,8,128]{2,1,0:T(8,128)(2,1)} fusion(bf16[512,128]{1,0:T(8,128)(2,1)} %get-tuple-element.15, bf16[128,128]{0,1:T(8,128)(2,1)S(1)} %collective-permute-done), kind=kOutput, calls=%fused_computation.7 | convolution fusion | flops 16842752 | bytes 294912 | tf_op jit(solution)/shard_map/dot_general | solution.py:199
  13.8 29.3 %all-to-all-start = ((bf16[64,8,128]{2,1,0:T(8,128)(2,1)}), bf16[64,8,128]{2,1,0:T(8,128)(2,1)S(1)}, u32[]{:S(2)}, u32[]{:S(2)}) async-start(bf16[64,8,128]{2,1,0:T(8,128)(2,1)} %fusion.3), calls=%async_computation | async-start | bytes 262144 | tf_op jit(solution)/shard_map/all_to_all | solution.py:200
  43.1 0.7 fusion.28
  43.8 0.2 convert_reduce_fusion.1
  44.1 0.1 iota_compare_fusion
  44.2 28.2 %all-to-all-done = bf16[64,8,128]{2,1,0:T(8,128)(2,1)S(1)} async-done(((bf16[64,8,128]{2,1,0:T(8,128)(2,1)}), bf16[64,8,128]{2,1,0:T(8,128)(2,1)S(1)}, u32[]{:S(2)}, u32[]{:S(2)}) %all-to-all-start) | async-done | bytes 131104 | tf_op jit(solution)/shard_map/all_to_all | solution.py:200
  72.3 0.0 collective-permute-done.1.far_ref
  72.4 0.0 copy-start.1
  72.4 0.2 convolution_convert_fusion.7
  72.6 0.2 convolution_convert_fusion.6
  72.8 0.1 copy.22
  73.0 0.8 broadcast_in_dim.41
  73.8 9.0 %all-to-all-start.1 = ((bf16[16,64,256]{2,1,0:T(8,128)(2,1)}), bf16[16,64,256]{2,1,0:T(8,128)(2,1)S(1)}, u32[]{:S(2)}, u32[]{:S(2)}) async-start(bf16[16,64,256]{2,1,0:T(8,128)(2,1)} %bitcast.12), calls=%async_computation.1 | async-start | bytes 1048576 | tf_op jit(solution)/shard_map/all_to_all | solution.py:222
  82.8 0.0 copy-done
  82.8 0.1 dynamic-slice_bitcast_fusion.1
  82.9 0.1 copy.23.weight_ref
  83.0 9.7 %all-to-all-done.1.rows_ref = bf16[16,64,256]{2,1,0:T(8,128)(2,1)S(1)} async-done(((bf16[16,64,256]{2,1,0:T(8,128)(2,1)}), bf16[16,64,256]{2,1,0:T(8,128)(2,1)S(1)}, u32[]{:S(2)}, u32[]{:S(2)}) %all-to-all-start.1) | async-done | bytes 524320 | tf_op jit(solution)/shard_map/all_to_all | solution.py:222
  92.7 0.0 copy-done.1
  92.7 4.6 %shard_map.111 = (bf16[32,48,128]{2,1,0:T(8,128)(2,1)}, bf16[64,2816]{1,0:T(8,128)(2,1)S(1)}, bf16[64,2816]{1,0:T(8,128)(2,1)S(1)}) custom-call(s32[1]{0:T(128)} %bitcast.5.q_ref, f32[64,1]{1,0:T(8,128)S(1)} %copy.23.weight_ref, bf16[16,64,256]{2,1,0:T(8,128)(2,1)S(1)} %all-to-all-done.1.rows_ref, bf16[1024,256]{1,0:T(8,128)(2,1)} %bitcast.53, ...), custom_call_target="tpu_custom_call" | custom-call | flops 335544320 | bytes 5242880 | tf_op jit(solution)/shard_map/pallas_call | solution.py:234
  97.3 4.6 %all-to-all-start.2 = ((bf16[32,48,128]{2,1,0:T(8,128)(2,1)}), bf16[32,48,128]{2,1,0:T(8,128)(2,1)S(1)}, u32[]{:S(2)}, u32[]{:S(2)}) async-start(bf16[32,48,128]{2,1,0:T(8,128)(2,1)} %get-tuple-element.21), calls=%async_computation.2 | async-start | bytes 786432 | tf_op jit(solution)/shard_map/all_to_all | solution.py:256
  102.0 10.3 %all-to-all-done.2 = bf16[32,48,128]{2,1,0:T(8,128)(2,1)S(1)} async-done(((bf16[32,48,128]{2,1,0:T(8,128)(2,1)}), bf16[32,48,128]{2,1,0:T(8,128)(2,1)S(1)}, u32[]{:S(2)}, u32[]{:S(2)}) %all-to-all-start.2) | async-done | bytes 393248 | tf_op jit(solution)/shard_map/all_to_all | solution.py:256
  112.2 0.1 convert_reduce_fusion
  112.3 0.1 reshape.117
  112.5 0.2 convolution_convert_fusion.5
  112.7 0.2 convolution_convert_fusion.4
  112.9 0.7 copy.26
  113.6 3.8 %all-to-all-start.3 = ((bf16[32,8,128]{2,1,0:T(8,128)(2,1)}), bf16[32,8,128]{2,1,0:T(8,128)(2,1)S(1)}, u32[]{:S(2)}, u32[]{:S(2)}) async-start(bf16[32,8,128]{2,1,0:T(8,128)(2,1)} %bitcast.18), calls=%async_computation.3 | async-start | bytes 131072 | tf_op jit(solution)/shard_map/all_to_all | solution.py:276
  117.5 0.1 slice_add_fusion
  117.6 0.6 reshape.120
  118.2 10.3 %all-gather = bf16[128,2816]{1,0:T(8,128)(2,1)S(1)} all-gather(bf16[64,2816]{1,0:T(8,128)(2,1)S(1)} %get-tuple-element.24), channel_id=2, replica_groups=mesh['z'=32,'p'=2,'q'=2,'x'=4,'c'=2] {'q'}, dimensions={0}, use_global_device_ids=true | all-gather | bytes 1081344 | tf_op jit(solution)/shard_map/all_gather | solution.py:288
  128.5 1.1 fusion.2
  129.6 0.0 copy-start.2
  129.6 1.1 fusion.1
  130.8 1.1 fusion
  131.9 10.2 %all-to-all-done.3 = bf16[32,8,128]{2,1,0:T(8,128)(2,1)S(1)} async-done(((bf16[32,8,128]{2,1,0:T(8,128)(2,1)}), bf16[32,8,128]{2,1,0:T(8,128)(2,1)S(1)}, u32[]{:S(2)}, u32[]{:S(2)}) %all-to-all-start.3) | async-done | bytes 65568 | tf_op jit(solution)/shard_map/all_to_all | solution.py:276
  142.1 0.0 copy-done.2
  142.1 0.2 fusion.18
  142.3 0.9 fusion.4
  (14 shorter events, 0.1 us)
Async XLA Ops:
  0.6 82.2 %copy-start = (f32[2,128]{1,0:T(2,128)S(1)}, f32[2,128]{1,0:T(2,128)}, u32[]{:S(2)}) copy-start(f32[2,128]{1,0:T(2,128)} %param.12) | copy-start | bytes 3076
  1.4 4.0 %collective-permute-start = (bf16[128,128]{0,1:T(8,128)(2,1)S(1)}, bf16[128,128]{0,1:T(8,128)(2,1)S(1)}, u32[]{:S(2)}, u32[]{:S(2)}) collective-permute-start(bf16[128,128]{0,1:T(8,128)(2,1)S(1)} %pad_maximum_fusion.4), channel_id=1, source_target_pairs={{0,0},{8,16},{16,8},{24,24},{1,1},{9,17},{17,9},{25,25},{2,2},{10,... | collective-permute-start | bytes 98312 | tf_op jit(solution)/shard_map/ppermute | solution.py:176
  5.4 66.9 %collective-permute-start.1 = (bf16[3,1024,256]{2,1,0:T(8,128)(2,1)}, bf16[3,1024,256]{2,1,0:T(8,128)(2,1)S(1)}, u32[]{:S(2)}, u32[]{:S(2)}) collective-permute-start(bf16[3,1024,256]{2,1,0:T(8,128)(2,1)} %get-tuple-element.18), channel_id=1, source_target_pairs={{0,8},{8,0},{1,9},{9,1},{2,10},{10,2},{3,11},{11,3},{4,12},{12,4},... | collective-permute-start | bytes 4718600 | tf_op jit(solution)/shard_map/ppermute | solution.py:196
  13.8 58.6 %all-to-all-start = ((bf16[64,8,128]{2,1,0:T(8,128)(2,1)}), bf16[64,8,128]{2,1,0:T(8,128)(2,1)S(1)}, u32[]{:S(2)}, u32[]{:S(2)}) async-start(bf16[64,8,128]{2,1,0:T(8,128)(2,1)} %fusion.3), calls=%async_computation | async-start | bytes 262144 | tf_op jit(solution)/shard_map/all_to_all | solution.py:200
  72.4 20.4 %copy-start.1 = (bf16[3,1024,256]{2,1,0:T(8,128)(2,1)}, bf16[3,1024,256]{2,1,0:T(8,128)(2,1)S(1)}, u32[]{:S(2)}) copy-start(bf16[3,1024,256]{2,1,0:T(8,128)(2,1)S(1)} %collective-permute-done.1.far_ref) | copy-start | bytes 4718596
  73.8 18.9 %all-to-all-start.1 = ((bf16[16,64,256]{2,1,0:T(8,128)(2,1)}), bf16[16,64,256]{2,1,0:T(8,128)(2,1)S(1)}, u32[]{:S(2)}, u32[]{:S(2)}) async-start(bf16[16,64,256]{2,1,0:T(8,128)(2,1)} %bitcast.12), calls=%async_computation.1 | async-start | bytes 1048576 | tf_op jit(solution)/shard_map/all_to_all | solution.py:222
  97.3 14.9 %all-to-all-start.2 = ((bf16[32,48,128]{2,1,0:T(8,128)(2,1)}), bf16[32,48,128]{2,1,0:T(8,128)(2,1)S(1)}, u32[]{:S(2)}, u32[]{:S(2)}) async-start(bf16[32,48,128]{2,1,0:T(8,128)(2,1)} %get-tuple-element.21), calls=%async_computation.2 | async-start | bytes 786432 | tf_op jit(solution)/shard_map/all_to_all | solution.py:256
  113.6 28.4 %all-to-all-start.3 = ((bf16[32,8,128]{2,1,0:T(8,128)(2,1)}), bf16[32,8,128]{2,1,0:T(8,128)(2,1)S(1)}, u32[]{:S(2)}, u32[]{:S(2)}) async-start(bf16[32,8,128]{2,1,0:T(8,128)(2,1)} %bitcast.18), calls=%async_computation.3 | async-start | bytes 131072 | tf_op jit(solution)/shard_map/all_to_all | solution.py:276
  129.6 12.4 %copy-start.2 = (bf16[512,128]{1,0:T(8,128)(2,1)S(1)}, bf16[512,128]{1,0:T(8,128)(2,1)}, u32[]{:S(2)}) copy-start(bf16[512,128]{1,0:T(8,128)(2,1)} %get-tuple-element.15) | copy-start | bytes 393220
